TPU v7x, 512 devices: a whole 4x8x8 slice. The times are simulated.
512 devices in a mesh: patch: 64 (over z, x, y_lo), head: 8 (over y_hi, core).
Axes of the slice: x: 4, y: 8 (y_hi: 4, y_lo: 2; y = y_hi * 2 + y_lo), z: 8, core: 2. Of those that a mesh axis runs over, the one named last changes fastest.
Arguments:
- query_first: bfloat16 [2560, 5120], P(('patch', 'head')), may hold values from -200 to 200
- keys_first: bfloat16 [2560, 5120], P(('patch', 'head')), may hold values from -8 to 8
- values_first: bfloat16 [2560, 5120], P(('patch', 'head')), may hold values from -6 to 6
- query_second: bfloat16 [2560, 5120], P(('patch', 'head')), may hold values from -200 to 200
- keys_second: bfloat16 [2560, 5120], P(('patch', 'head')), may hold values from -6 to 6
- values_second: bfloat16 [2560, 5120], P(('patch', 'head')), may hold values from -6 to 6
- text_keys: bfloat16 [512, 5120], P(None, 'head'), may hold values from -6 to 6
- text_values: bfloat16 [512, 5120], P(None, 'head'), may hold values from -6 to 6
- gate_table: float32 [35, 5120], P(None, 'head'), may hold values from 0.1 to 1.9
- timesteps: int32 [2], replicated, may hold values from 0 to 34
- text_length: int32 [1], replicated, may hold values from 64 to 512
Outputs:
- first_output: bfloat16 [2560, 5120], P(('patch', 'head'))
- second_output: bfloat16 [2560, 5120], P(('patch', 'head'))
Inputs may be any that keep to these rules, and one draw needn't show every extreme that they name: Only the first text_length[0] of the 512 text token slots are real. `timesteps`: rows of gate_table are picked by these indices.
All inputs are finite; a program needn't handle non-finite values.
Results may differ from a plain program's by a relative error of at most 0.0075.
Values may be sent and summed in bfloat16 or wider, within the bound.
No kernel may reach another device: no remote copies, remote signals or barrier semaphores. Data moves between devices by JAX's collectives and lax.ppermute only.
A program may use at most 64 MiB of HBM per device.

v0:
```python
import jax
import jax.numpy as jnp
from jax import lax
from jax.sharding import PartitionSpec as P

HEAD_DIM = 128


block_cap = 1024


def block_stats(queries, key_rows, value_rows, usable, score_scale):
    key_count = key_rows.shape[0]
    head_count = queries.shape[1]
    key_heads = key_rows.reshape(key_count, head_count, -1)
    value_heads = value_rows.reshape(key_count, head_count, -1)
    scores = (
        jnp.einsum("qhd,khd->qhk", queries, key_heads, preferred_element_type=jnp.float32)
        * score_scale
    )
    live_mask = usable[None, None, :]
    scores = jnp.where(live_mask, scores, -1e30)
    row_top = jnp.max(scores, axis=2)
    raised = jnp.where(live_mask, jnp.exp(scores - row_top[:, :, None]), 0.0)
    weight_sum = jnp.sum(raised, axis=2)
    numerator = jnp.einsum(
        "qhk,khd->qhd", raised.astype(jnp.bfloat16), value_heads, preferred_element_type=jnp.float32
    )
    return (row_top, weight_sum, numerator)


def merge_stats(former, latter):
    joint_top = jnp.maximum(former[0], latter[0])
    former_scale = jnp.exp(former[0] - joint_top)
    latter_scale = jnp.exp(latter[0] - joint_top)
    weight_sum = former[1] * former_scale + latter[1] * latter_scale
    numerator = former[2] * former_scale[:, :, None] + latter[2] * latter_scale[:, :, None]
    return (joint_top, weight_sum, numerator)


def fold_keys(carried, queries, key_rows, value_rows, usable, score_scale):
    key_count = key_rows.shape[0]
    for lower_edge in range(0, key_count, block_cap):
        upper_edge = min(lower_edge + block_cap, key_count)
        fresh = block_stats(
            queries,
            key_rows[lower_edge:upper_edge],
            value_rows[lower_edge:upper_edge],
            usable[lower_edge:upper_edge],
            score_scale,
        )
        carried = merge_stats(carried, fresh)
    return carried


def normalize(carried, gate_row):
    attention = carried[2] / carried[1][:, :, None]
    flat = attention.reshape(attention.shape[0], -1)
    return (gate_row[None, :] * flat).astype(jnp.bfloat16)


def body(
    query_first,
    keys_first,
    values_first,
    query_second,
    keys_second,
    values_second,
    text_keys,
    text_values,
    gate_table,
    timesteps,
    text_length,
):
    regrouped = (
        lax.all_to_all(query_first, "head", split_axis=1, concat_axis=0, tiled=True),
        lax.all_to_all(keys_first, "head", split_axis=1, concat_axis=0, tiled=True),
        lax.all_to_all(values_first, "head", split_axis=1, concat_axis=0, tiled=True),
        lax.all_to_all(query_second, "head", split_axis=1, concat_axis=0, tiled=True),
        lax.all_to_all(keys_second, "head", split_axis=1, concat_axis=0, tiled=True),
        lax.all_to_all(values_second, "head", split_axis=1, concat_axis=0, tiled=True),
    )
    first_query_rows, first_keys, first_values, second_query_rows, second_keys, second_values = (
        regrouped
    )
    row_count = first_query_rows.shape[0]
    head_count = first_query_rows.shape[1] // HEAD_DIM
    first_queries = first_query_rows.reshape(row_count, head_count, HEAD_DIM)
    second_queries = second_query_rows.reshape(row_count, head_count, HEAD_DIM)
    score_scale = HEAD_DIM ** (-0.5)
    own_start = lax.axis_index("patch") * row_count
    text_live = jnp.arange(text_keys.shape[0]) < text_length[0]
    first_state = block_stats(first_queries, text_keys, text_values, text_live, score_scale)
    second_state = block_stats(second_queries, text_keys, text_values, text_live, score_scale)
    own_rows = jnp.ones((row_count,), jnp.bool_)
    second_state = fold_keys(
        second_state, second_queries, second_keys, second_values, own_rows, score_scale
    )
    fetched = (
        lax.all_gather(first_keys, "patch", axis=0, tiled=True),
        lax.all_gather(first_values, "patch", axis=0, tiled=True),
    )
    every_row = jnp.ones((fetched[0].shape[0],), jnp.bool_)
    first_state = fold_keys(
        first_state, first_queries, fetched[0], fetched[1], every_row, score_scale
    )
    fetched = (
        lax.all_gather(first_keys, "patch", axis=0, tiled=True),
        lax.all_gather(first_values, "patch", axis=0, tiled=True),
    )
    positions = jnp.arange(fetched[0].shape[0])
    usable = (positions < own_start) | (positions >= own_start + row_count)
    second_state = fold_keys(
        second_state, second_queries, fetched[0], fetched[1], usable, score_scale
    )
    step_onehot = (timesteps[:, None] == jnp.arange(gate_table.shape[0])[None, :]).astype(
        jnp.float32
    )
    gate_rows = jnp.dot(step_onehot, gate_table, precision=lax.Precision.HIGHEST)
    first_local = normalize(first_state, gate_rows[0])
    second_local = normalize(second_state, gate_rows[1])
    restored = (
        lax.all_to_all(first_local, "head", split_axis=0, concat_axis=1, tiled=True),
        lax.all_to_all(second_local, "head", split_axis=0, concat_axis=1, tiled=True),
    )
    return (restored[0], restored[1])


def solution(mesh):
    placed = (
        P(("patch", "head"), None),
        P(("patch", "head"), None),
        P(("patch", "head"), None),
        P(("patch", "head"), None),
        P(("patch", "head"), None),
        P(("patch", "head"), None),
        P(None, "head"),
        P(None, "head"),
        P(None, "head"),
        P(),
        P(),
    )
    return jax.shard_map(
        body,
        mesh=mesh,
        in_specs=placed,
        out_specs=(P(("patch", "head"), None), P(("patch", "head"), None)),
        check_vma=False,
    )
```

profile of v0, /device:TPU:1, one launch (start us, length us, event | category | flops | bytes accessed | tf_op | source)
XLA Modules:
  0.0 707.3 jit_solution(12423480519396046609)
XLA Ops:
  7.2 17.7 %all_to_all.134 = bf16[5,8,640]{2,0,1:T(8,128)(2,1)S(1)} all-to-all(bf16[5,8,640]{2,0,1:T(8,128)(2,1)} %bitcast.155), channel_id=1, replica_groups=mesh['patch'=64,'head'=8] {'head'}, dimensions={1} | all-to-all | bytes 102400 | tf_op jit(solution)/shard_map/all_to_all | solution.py:78
  25.0 0.6 all_to_all.110
  25.7 11.7 %all_to_all.135 = bf16[5,8,640]{2,0,1:T(8,128)(2,1)S(1)} all-to-all(bf16[5,8,640]{2,0,1:T(8,128)(2,1)} %bitcast.156), channel_id=1, replica_groups=mesh['patch'=64,'head'=8] {'head'}, dimensions={1} | all-to-all | bytes 102400 | tf_op jit(solution)/shard_map/all_to_all | solution.py:77
  38.1 4.3 all-to-all-start
  42.3 0.9 fusion.90
  43.2 6.6 all-to-all-done
  49.9 4.2 all-to-all-start.4
  56.0 1.1 copy.22
  57.2 4.7 all-to-all-done.4
  61.9 4.3 all-to-all-start.5
  66.8 7.1 %all-to-all-done.5 = bf16[5,8,640]{2,0,1:T(8,128)(2,1)S(1)} async-done(((bf16[5,8,640]{2,0,1:T(8,128)(2,1)}), bf16[5,8,640]{2,0,1:T(8,128)(2,1)S(1)}, u32[]{:S(2)}, u32[]{:S(2)}) %all-to-all-start.5) | async-done | bytes 51232 | tf_op jit(solution)/shard_map/all_to_all | solution.py:80
  73.9 4.4 all-to-all-start.6
  78.6 7.6 %all-to-all-done.6 = bf16[5,8,640]{2,0,1:T(8,128)(2,1)S(1)} async-done(((bf16[5,8,640]{2,0,1:T(8,128)(2,1)}), bf16[5,8,640]{2,0,1:T(8,128)(2,1)S(1)}, u32[]{:S(2)}, u32[]{:S(2)}) %all-to-all-start.6) | async-done | bytes 51232 | tf_op jit(solution)/shard_map/all_to_all | solution.py:81
  86.2 0.7 reshape.307
  89.1 0.9 fusion.61
  90.0 200.1 %all-gather.5.cloned.1.call-done = bf16[2560,640]{1,0:T(8,128)(2,1)} async-done(((bf16[40,640]{1,0:T(8,128)(2,1)}), bf16[2560,640]{1,0:T(8,128)(2,1)}) %all-gather.5.cloned.1.call-update) | async-done | bytes 3276816 | tf_op jit(solution)/shard_map/all_gather | solution.py:101
  290.1 3.0 fusion.107
  293.1 0.6 copy.34
  293.8 1.1 slice-done
  294.9 1.2 copy.39
  296.0 303.5 %all-gather.3.cloned.1.call-done = bf16[2560,640]{1,0:T(8,128)(2,1)} async-done(((bf16[40,640]{1,0:T(8,128)(2,1)}), bf16[2560,640]{1,0:T(8,128)(2,1)}) %all-gather.3.cloned.1.call-update) | async-done | bytes 3276816 | tf_op jit(solution)/shard_map/all_gather | solution.py:100
  599.6 3.4 fusion.108
  603.0 1.6 copy.25
  604.6 2.0 slice.55
  606.6 1.3 copy.36
  608.0 1.6 fusion.111
  609.6 1.6 fusion.115
  611.2 1.0 fusion.113
  612.2 1.2 fusion.117
  613.4 1.6 copy.31
  615.0 1.3 fusion.112
  616.8 0.8 copy-done.20
  619.6 0.7 multiply_add_fusion
  620.3 1.0 fusion.35
  621.4 1.0 fusion.25
  622.4 1.6 copy.29
  624.1 1.6 fusion.34
  627.2 0.7 copy.41
  628.0 1.6 reshape.304
  629.6 1.6 multiply_convert_fusion.1
  631.1 47.4 %all-to-all-start.3 = ((bf16[8,5,640]{2,1,0:T(8,128)(2,1)}), bf16[8,5,640]{2,1,0:T(8,128)(2,1)}, u32[]{:S(2)}, u32[]{:S(2)}) async-start(bf16[8,5,640]{2,1,0:T(8,128)(2,1)} %multiply_convert_fusion.1), calls=%async_computation.3 | async-start | bytes 163840 | tf_op jit(solution)/shard_map/all_to_all | solution.py:123
  678.5 1.3 fusion.36
  679.8 1.3 fusion.21
  682.9 0.6 multiply_convert_fusion
  683.5 2.6 all-to-all-done.3
  686.2 4.6 all-to-all-start.7
  690.7 7.5 %all-to-all-done.7 = bf16[8,5,640]{2,1,0:T(8,128)(2,1)S(1)} async-done(((bf16[8,5,640]{2,1,0:T(8,128)(2,1)}), bf16[8,5,640]{2,1,0:T(8,128)(2,1)S(1)}, u32[]{:S(2)}, u32[]{:S(2)}) %all-to-all-start.7) | async-done | bytes 51232 | tf_op jit(solution)/shard_map/all_to_all | solution.py:124
  698.3 1.5 copy.104
  (155 shorter events, 11.0 us)
Async XLA Ops:
  7.2 35.2 %copy-start = (f32[35,640]{1,0:T(8,128)S(1)}, f32[35,640]{1,0:T(8,128)}, u32[]{:S(2)}) copy-start(f32[35,640]{1,0:T(8,128)} %param.19) | copy-start | bytes 268804
  7.2 48.5 %copy-start.26 = (bf16[512,640]{1,0:T(8,128)(2,1)S(1)}, bf16[512,640]{1,0:T(8,128)(2,1)}, u32[]{:S(2)}) copy-start(bf16[512,640]{1,0:T(8,128)(2,1)} %param.17) | copy-start | bytes 1966084
  7.2 48.8 %copy-start.27 = (bf16[512,640]{1,0:T(8,128)(2,1)S(1)}, bf16[512,640]{1,0:T(8,128)(2,1)}, u32[]{:S(2)}) copy-start(bf16[512,640]{1,0:T(8,128)(2,1)} %param.18) | copy-start | bytes 1966084
  7.2 282.9 %all-gather.5.cloned.1.call-start = ((), (), s32[]{:S(2)}) async-start(), calls=%async_computation.9 | async-start | bytes 3328000 | tf_op jit(solution)/shard_map/all_gather | solution.py:101
  25.6 573.9 %all-gather.3.cloned.1.call-start = ((), (), s32[]{:S(2)}) async-start(), calls=%async_computation.8 | async-start | bytes 3328000 | tf_op jit(solution)/shard_map/all_gather | solution.py:100
  38.1 11.8 %all-to-all-start = ((bf16[5,8,640]{2,0,1:T(8,128)(2,1)}), bf16[5,8,640]{2,0,1:T(8,128)(2,1)S(1)}, u32[]{:S(2)}, u32[]{:S(2)}) async-start(bf16[5,8,640]{2,0,1:T(8,128)(2,1)} %bitcast.157), calls=%async_computation | async-start | bytes 163840 | tf_op jit(solution)/shard_map/all_to_all | solution.py:76
  49.9 12.0 %all-to-all-start.4 = ((bf16[5,8,640]{2,0,1:T(8,128)(2,1)}), bf16[5,8,640]{2,0,1:T(8,128)(2,1)S(1)}, u32[]{:S(2)}, u32[]{:S(2)}) async-start(bf16[5,8,640]{2,0,1:T(8,128)(2,1)} %bitcast.158), calls=%async_computation.4 | async-start | bytes 163840 | tf_op jit(solution)/shard_map/all_to_all | solution.py:79
  54.6 557.6 %copy-start.42 = (pred[1024]{0:T(1024)(128)(4,1)}, pred[1024]{0:T(1024)(128)(4,1)S(1)}, u32[]{:S(2)}) copy-start(pred[1024]{0:T(1024)(128)(4,1)S(1)} %get-tuple-element.26) | copy-start | bytes 3076
  61.9 12.0 %all-to-all-start.5 = ((bf16[5,8,640]{2,0,1:T(8,128)(2,1)}), bf16[5,8,640]{2,0,1:T(8,128)(2,1)S(1)}, u32[]{:S(2)}, u32[]{:S(2)}) async-start(bf16[5,8,640]{2,0,1:T(8,128)(2,1)} %bitcast.29), calls=%async_computation.5 | async-start | bytes 163840 | tf_op jit(solution)/shard_map/all_to_all | solution.py:80
  73.9 12.3 %all-to-all-start.6 = ((bf16[5,8,640]{2,0,1:T(8,128)(2,1)}), bf16[5,8,640]{2,0,1:T(8,128)(2,1)S(1)}, u32[]{:S(2)}, u32[]{:S(2)}) async-start(bf16[5,8,640]{2,0,1:T(8,128)(2,1)} %bitcast.32), calls=%async_computation.6 | async-start | bytes 163840 | tf_op jit(solution)/shard_map/all_to_all | solution.py:81
  78.3 10.1 %copy-start.54 = (pred[512]{0:T(512)(128)(4,1)}, pred[512]{0:T(512)(128)(4,1)S(1)}, u32[]{:S(2)}) copy-start(pred[512]{0:T(512)(128)(4,1)S(1)} %iota_compare_fusion.2) | copy-start | bytes 1540
  78.4 10.0 %copy-start.22 = (bf16[40,5,128]{2,1,0:T(8,128)(2,1)}, bf16[40,5,128]{2,1,0:T(8,128)(2,1)S(1)}, u32[]{:S(2)}) copy-start(bf16[40,5,128]{2,1,0:T(8,128)(2,1)S(1)} %reshape.296) | copy-start | bytes 153604
  78.5 9.9 %copy-start.16 = (bf16[40,5,128]{2,0,1:T(8,128)(2,1)}, bf16[40,5,128]{2,0,1:T(8,128)(2,1)S(1)}, u32[]{:S(2)}) copy-start(bf16[40,5,128]{2,0,1:T(8,128)(2,1)S(1)} %copy.44) | copy-start | bytes 153604
  88.4 204.8 %copy-start.28 = (f32[40,5]{0,1:T(8,128)}, f32[40,5]{0,1:T(8,128)S(1)}, u32[]{:S(2)}) copy-start(f32[40,5]{0,1:T(8,128)S(1)} %get-tuple-element.28) | copy-start | bytes 2404
  604.6 3.4 copy-start.23
  606.6 2.9 copy-start.17
  606.6 2.9 copy-start.58
  608.0 3.2 copy-start.24
  615.0 1.4 copy-start.19
  615.0 1.4 copy-start.40
  616.3 2.7 copy-start.1
  616.3 3.2 copy-start.34
  616.3 1.3 copy-start.20
  616.3 1.3 copy-start.38
  616.3 1.3 copy-start.59
  616.4 1.5 copy-start.8
  616.4 1.5 copy-start.30
  616.4 1.9 copy-start.3
  616.4 1.9 copy-start.43
  616.8 2.5 copy-start.5
  616.8 1.9 copy-start.32
  618.7 1.7 copy-start.7
  618.7 1.7 copy-start.13
  618.7 1.6 copy-start.55
  619.0 2.4 copy-start.11
  622.4 1.7 copy-start.33
  624.0 1.7 copy-start.2
  624.0 1.7 copy-start.35
  624.0 1.7 copy-start.50
  624.0 1.7 copy-start.51
  625.6 1.2 copy-start.14
  626.9 53.0 %copy-start.4 = (f32[40,5,1024]{2,0,1:T(8,128)S(1)}, f32[40,5,1024]{2,0,1:T(8,128)}, u32[]{:S(2)}) copy-start(f32[40,5,1024]{2,0,1:T(8,128)} %get-tuple-element.43) | copy-start | bytes 2457604
  631.1 55.0 %all-to-all-start.3 = ((bf16[8,5,640]{2,1,0:T(8,128)(2,1)}), bf16[8,5,640]{2,1,0:T(8,128)(2,1)}, u32[]{:S(2)}, u32[]{:S(2)}) async-start(bf16[8,5,640]{2,1,0:T(8,128)(2,1)} %multiply_convert_fusion.1), calls=%async_computation.3 | async-start | bytes 163840 | tf_op jit(solution)/shard_map/all_to_all | solution.py:123
  678.5 2.7 copy-start.6
  678.5 2.7 copy-start.41
  678.5 2.7 copy-start.46
  678.5 2.7 copy-start.47
  686.2 12.1 %all-to-all-start.7 = ((bf16[8,5,640]{2,1,0:T(8,128)(2,1)}), bf16[8,5,640]{2,1,0:T(8,128)(2,1)S(1)}, u32[]{:S(2)}, u32[]{:S(2)}) async-start(bf16[8,5,640]{2,1,0:T(8,128)(2,1)} %multiply_convert_fusion), calls=%async_computation.7 | async-start | bytes 163840 | tf_op jit(solution)/shard_map/all_to_all | solution.py:124
  (22 other events, 22.2 us)
Sparse Core Ops, SparseCore 0:
  25.7 264.3 all-gather.4
  292.2 307.3 all-gather.2
where the time goes:
time: 709 us; the launch traced here: 707 us
  waiting for transfers between devices  540 us (76%)
  starting transfers between devices  69.2 us (10%)
  local copies, waits for them, and re-layouts  30.3 us (4%)
  blocking collectives  29.4 us (4%)
  matrix products  16.9 us (2%)
  between operations  15.6 us (2%)
    all_gather x1, waiting for transfers between devices, body(): lax.all_gather(first_keys, 'patch', axis=0, tiled=True)  304 us
    all_gather x1, waiting for transfers between devices, body(): lax.all_gather(first_values, 'patch', axis=0, tiled=True)  200 us
    all_to_all x1, starting transfers between devices, body(): lax.all_to_all(first_local, 'head', split_axis=0, concat_axis=1, tiled=True)  47.4 us
    all_to_all x1, blocking collectives, body(): lax.all_to_all(values_first, 'head', split_axis=1, concat_axis=0, tiled=T...  17.7 us
  transfers between devices with their start and end apart: 8, of which 8 were waited for; matrix products, arithmetic and copies ran while one was open for 2% of the time, Pallas kernels for 0%

commit v1 on v0

v1 whole, which is shorter than its diff:
```python
import functools

import jax
import jax.numpy as jnp
import numpy as np
from jax import lax
from jax.experimental import pallas as pl
from jax.experimental.pallas import tpu as pltpu
from jax.sharding import Mesh
from jax.sharding import PartitionSpec as P

HEAD_DIM = 128
HEADS = 40
GROUP_HEADS = 5
GROUPS = 8
ROWS = 5
BLOCK = 40
CHUNK = 32
BACK = 16
EXP_SCALE = float(HEAD_DIM ** (-0.5) * np.log2(np.e))

AXES = ("z", "x", "yl", "yh", "c")
PLANE = ("yh", "c", "z")
REPLICAS = ("x", "yl")

VMEM_LIMIT = 48 * 1024 * 1024


def dot_f32(left, right):
    return lax.dot_general(
        left, right, (((1,), (0,)), ((), ())), preferred_element_type=jnp.float32
    )


def dot_t_f32(left, right):
    return lax.dot_general(
        left, right, (((1,), (1,)), ((), ())), preferred_element_type=jnp.float32
    )


def pack_kernel(k1, v1, q1, q2, k2, v2, out):
    total = None
    for index, array in enumerate((k1, v1, q1, q2, k2, v2)):
        row = lax.broadcasted_iota(jnp.int32, (CHUNK, ROWS), 0)
        column = lax.broadcasted_iota(jnp.int32, (CHUNK, ROWS), 1)
        place = jnp.where(row == column + index * ROWS, 1.0, 0.0).astype(jnp.bfloat16)
        part = dot_f32(place, array[...])
        total = part if total is None else total + part
    packed = total.astype(jnp.bfloat16)
    blank = jnp.zeros((CHUNK, HEAD_DIM), jnp.bfloat16)
    for group in range(GROUPS):
        for slot in range(8):
            if slot < GROUP_HEADS:
                head = group * GROUP_HEADS + slot
                out[group * 8 + slot] = packed[:, head * HEAD_DIM : (head + 1) * HEAD_DIM]
            else:
                out[group * 8 + slot] = blank


def pack(*arrays):
    return pl.pallas_call(
        pack_kernel,
        out_shape=jax.ShapeDtypeStruct((64, CHUNK, HEAD_DIM), jnp.bfloat16),
        compiler_params=pltpu.CompilerParams(vmem_limit_bytes=VMEM_LIMIT),
    )(*arrays)


def order_matrix():
    matrix = np.zeros((6, 2, BLOCK, 2, GROUPS, CHUNK), np.float32)
    for array in range(6):
        for pair in range(2):
            for t in range(BLOCK):
                matrix[array, pair, t, pair, t // ROWS, array * ROWS + t % ROWS] = 1.0
    return matrix.reshape(6 * 2 * BLOCK, 2 * GROUPS * CHUNK)


def unpack_kernel(order, messages, copies, own):
    for step in range(4):
        pieces = [messages[:, 2 * step + half] for half in range(2)]
        rows = jnp.concatenate([p.reshape(GROUPS * CHUNK, HEAD_DIM) for p in pieces], axis=0)
        sorted_rows = dot_f32(order[...], rows).astype(jnp.bfloat16)
        span = 2 * BLOCK
        for array in range(6):
            piece = sorted_rows[array * span : (array + 1) * span]
            if array < 2:
                for copy in range(8):
                    copies[copy, pl.ds(array * 320 + step * span, span)] = piece
            else:
                own[pl.ds((array - 2) * 320 + step * span, span)] = piece


def unpack(messages):
    order = jnp.asarray(order_matrix(), jnp.bfloat16)
    return pl.pallas_call(
        unpack_kernel,
        out_shape=(
            jax.ShapeDtypeStruct((8, 640, HEAD_DIM), jnp.bfloat16),
            jax.ShapeDtypeStruct((1280, HEAD_DIM), jnp.bfloat16),
        ),
        compiler_params=pltpu.CompilerParams(vmem_limit_bytes=VMEM_LIMIT),
    )(order, messages.reshape(GROUPS, 8, CHUNK, HEAD_DIM))


def block_of(index):
    return jnp.floor((index.astype(jnp.float32) + 0.5) * (1.0 / BLOCK))


def attention_kernel(
    steps, length, planes, own, text_k, text_v, gates, out, keys, values, tk, tv, gate, sems
):
    slot = jnp.minimum(lax.axis_index("z"), GROUP_HEADS - 1)
    columns = pl.ds(pl.multiple_of(slot * HEAD_DIM, HEAD_DIM), HEAD_DIM)
    fetches = [
        pltpu.make_async_copy(text_k.at[:, columns], tk, sems.at[0]),
        pltpu.make_async_copy(text_v.at[:, columns], tv, sems.at[1]),
        pltpu.make_async_copy(gates.at[:, columns], gate, sems.at[2]),
    ]
    for fetch in fetches:
        fetch.start()
    plane = lax.axis_index("x") * 2 + lax.axis_index("yl")
    for place in range(8):
        source = lax.rem(plane + place, 8)
        keys[pl.ds(place * 320, 320)] = planes[source, pl.ds(0, 320)]
        values[pl.ds(place * 320, 320)] = planes[source, pl.ds(320, 320)]
    for fetch in fetches:
        fetch.wait()

    live = lax.broadcasted_iota(jnp.int32, (1, 512), 1) < length[0]
    tile = 160
    finished = []
    for step in range(2):
        gate_row = gate[pl.ds(steps[step], 1), :]
        for first in range(0, 320, tile):
            queries = own[pl.ds(step * 320 + first, tile), :]
            scores = dot_t_f32(queries, keys[...])
            text_scores = jnp.where(live, dot_t_f32(queries, tk[...]), -1e30)
            if step == 1:
                row = block_of(lax.broadcasted_iota(jnp.int32, (tile, 1), 0) + first)
                column = block_of(lax.broadcasted_iota(jnp.int32, (1, 384), 1))
                same = row == column
                near_scores = dot_t_f32(queries, own[pl.ds(640, 384), :])
                near = jnp.where(same, near_scores, scores[:, :384])
                scores = jnp.concatenate([near, scores[:, 384:]], axis=1)
            top = jnp.maximum(
                jnp.max(scores, axis=1, keepdims=True), jnp.max(text_scores, axis=1, keepdims=True)
            )
            raised = jnp.exp2((scores - top) * EXP_SCALE)
            text_raised = jnp.exp2((text_scores - top) * EXP_SCALE)
            total = jnp.sum(raised, axis=1, keepdims=True) + jnp.sum(
                text_raised, axis=1, keepdims=True
            )
            weights = raised.astype(jnp.bfloat16)
            numerator = dot_f32(text_raised.astype(jnp.bfloat16), tv[...])
            if step == 1:
                local = raised[:, :384]
                near_weights = jnp.where(same, local, 0.0).astype(jnp.bfloat16)[:, :320]
                far_weights = jnp.where(same, 0.0, local).astype(jnp.bfloat16)
                numerator += dot_f32(near_weights, own[pl.ds(960, 320), :])
                weights = jnp.concatenate([far_weights, weights[:, 384:]], axis=1)
            numerator += dot_f32(weights, values[...])
            finished.append((gate_row * (numerator / total)).astype(jnp.bfloat16))
    row = lax.broadcasted_iota(jnp.int32, (GROUPS * BACK, BLOCK), 0)
    column = lax.broadcasted_iota(jnp.int32, (GROUPS * BACK, BLOCK), 1)
    place_first = jnp.zeros((GROUPS * BACK, BLOCK), jnp.bool_)
    place_second = jnp.zeros((GROUPS * BACK, BLOCK), jnp.bool_)
    for group in range(GROUPS):
        inside = (column >= group * ROWS) & (column < (group + 1) * ROWS)
        offset = row - group * BACK - column + group * ROWS
        place_first = place_first | (inside & (offset == 0))
        place_second = place_second | (inside & (offset == 8))
    place_first = jnp.where(place_first, 1.0, 0.0).astype(jnp.bfloat16)
    place_second = jnp.where(place_second, 1.0, 0.0).astype(jnp.bfloat16)
    per_tile = tile // BLOCK
    tiles = 320 // tile
    for block in range(8):
        begin = (block % per_tile) * BLOCK
        first_rows = finished[block // per_tile][begin : begin + BLOCK]
        second_rows = finished[tiles + block // per_tile][begin : begin + BLOCK]
        message = dot_f32(place_first, first_rows) + dot_f32(place_second, second_rows)
        out[:, block] = message.astype(jnp.bfloat16).reshape(GROUPS, BACK, HEAD_DIM)


def attention(timesteps, text_length, planes, own, text_keys, text_values, gate_table):
    smem = pl.BlockSpec(memory_space=pltpu.SMEM)
    vmem = pl.BlockSpec(memory_space=pltpu.VMEM)
    hbm = pl.BlockSpec(memory_space=pl.ANY)
    return pl.pallas_call(
        attention_kernel,
        out_shape=jax.ShapeDtypeStruct((GROUPS, 8, BACK, HEAD_DIM), jnp.bfloat16),
        in_specs=[smem, smem, vmem, vmem, hbm, hbm, hbm],
        out_specs=vmem,
        scratch_shapes=[
            pltpu.VMEM((2560, HEAD_DIM), jnp.bfloat16),
            pltpu.VMEM((2560, HEAD_DIM), jnp.bfloat16),
            pltpu.VMEM((512, HEAD_DIM), jnp.bfloat16),
            pltpu.VMEM((512, HEAD_DIM), jnp.bfloat16),
            pltpu.VMEM((35, HEAD_DIM), jnp.float32),
            pltpu.SemaphoreType.DMA((3,)),
        ],
        compiler_params=pltpu.CompilerParams(vmem_limit_bytes=VMEM_LIMIT),
    )(timesteps, text_length, planes, own, text_keys, text_values, gate_table)


def finish_kernel(messages, first, second):
    for group in range(GROUPS):
        for slot in range(GROUP_HEADS):
            head = group * GROUP_HEADS + slot
            columns = pl.ds(head * HEAD_DIM, HEAD_DIM)
            message = messages[group * 8 + slot]
            first[:, columns] = message[0:ROWS]
            second[:, columns] = message[8 : 8 + ROWS]


def finish(messages):
    shape = jax.ShapeDtypeStruct((ROWS, HEADS * HEAD_DIM), jnp.bfloat16)
    return pl.pallas_call(
        finish_kernel,
        out_shape=(shape, shape),
        compiler_params=pltpu.CompilerParams(vmem_limit_bytes=VMEM_LIMIT),
    )(messages)


def body(
    query_first,
    keys_first,
    values_first,
    query_second,
    keys_second,
    values_second,
    text_keys,
    text_values,
    gate_table,
    timesteps,
    text_length,
):
    sent = pack(keys_first, values_first, query_first, query_second, keys_second, values_second)
    arrived = lax.all_to_all(sent, PLANE, 0, 0, tiled=True)
    copies, own = unpack(arrived)
    planes = lax.all_to_all(copies, REPLICAS, 0, 0, tiled=True)
    back = attention(timesteps, text_length, planes, own, text_keys, text_values, gate_table)
    returned = lax.all_to_all(
        back.reshape(64, BACK, HEAD_DIM), PLANE, 0, 0, tiled=True
    )
    return finish(returned)


def solution(mesh):
    fine = Mesh(mesh.devices.reshape(8, 4, 2, 4, 2), AXES)
    rows = P(AXES, None)
    heads = P(None, ("yh", "c"))
    return jax.shard_map(
        body,
        mesh=fine,
        in_specs=(rows,) * 6 + (heads,) * 3 + (P(), P()),
        out_specs=(rows, rows),
        check_vma=False,
    )
```

time: 709 us -> 94.9 us (0.13)
  waiting for transfers between devices: 540 us -> 16.1 us
  starting transfers between devices: 69.2 us -> 4.23 us
  blocking collectives: 29.4 us -> 59.8 us
  local copies, waits for them, and re-layouts: 30.3 us -> 5.39 us
  matrix products: 16.9 us -> 0 us
  between operations: 15.6 us -> 1.34 us
  Pallas kernels: 0 us -> 7.56 us
    all_gather x2 -> x0, waiting for transfers between devices: 504 us -> none  [the longest x1 304 us: body(): lax.all_gather(first_keys, 'patch', axis=0, tiled=True)]
    all_to_all x6 -> x1, starting transfers between devices: 69.1 us -> 4.23 us  [body(): planes = lax.all_to_all(copies, REPLICAS, 0, 0, tiled=True)]
    all_to_all x2, blocking collectives: 29.4 us -> 59.8 us  [the longest x1 36.9 us: body(): arrived = lax.all_to_all(sent, PLANE, 0, 0, tiled=True)]
    all_to_all x6 -> x1, waiting for transfers between devices: 36.3 us -> 16.1 us  [body(): planes = lax.all_to_all(copies, REPLICAS, 0, 0, tiled=True)]
    slice x14 -> x0, local copies, waits for them, and re-layouts: 19.1 us -> none  [the longest x5 10 us: fold_keys(): key_rows[lower_edge:upper_edge]]
    dot_general x19 -> x0, matrix products: 16.9 us -> none  [the longest x9 8.24 us: block_stats(): jnp.einsum('qhk,khd->qhd', raised.astype(jnp.bfloat16), value_heads, pref...]
    pallas_call x0 -> x4, Pallas kernels: none -> 7.56 us  [the longest x1 4.5 us: attention(): pl.pallas_call(attention_kernel, out_shape=jax.ShapeDtypeStruct((GROUPS,...]
  transfers between devices with their start and end apart: 8 -> 1, of which waited for: 8 -> 1; matrix products, arithmetic and copies ran while one was open for 2% -> 0% of each run, Pallas kernels for 0% -> 0%
where the time goes in v1:
time: 94.9 us; the launch traced here: 94.4 us
  blocking collectives  59.8 us (63%)
  waiting for transfers between devices  16.1 us (17%)
  Pallas kernels  7.56 us (8%)
  local copies, waits for them, and re-layouts  5.39 us (6%)
  starting transfers between devices  4.23 us (4%)
  between operations  1.34 us (1%)
    all_to_all x1, blocking collectives, body(): arrived = lax.all_to_all(sent, PLANE, 0, 0, tiled=True)  36.9 us
    all_to_all x1, blocking collectives, body(): lax.all_to_all(back.reshape(64, BACK, HEAD_DIM), PLANE, 0, 0, tiled=True)  22.9 us
    all_to_all x1, waiting for transfers between devices, body(): planes = lax.all_to_all(copies, REPLICAS, 0, 0, tiled=True)  16.1 us
    unnamed x22, local copies, waits for them, and re-layouts  5.39 us
    pallas_call x1, Pallas kernels, attention(): pl.pallas_call(attention_kernel, out_shape=jax.ShapeDtypeStruct((GROUPS,...  4.5 us
    all_to_all x1, starting transfers between devices, body(): planes = lax.all_to_all(copies, REPLICAS, 0, 0, tiled=True)  4.23 us
  transfers between devices with their start and end apart: 1, of which 1 were waited for; matrix products, arithmetic and copies ran while one was open for 0% of the time, Pallas kernels for 0%

profile of v1, /device:TPU:1, one launch (start us, length us, event | category | flops | bytes accessed | tf_op | source)
XLA Modules:
  0.0 94.4 jit_solution(13515613886977434050)
XLA Ops:
  0.6 0.0 copy-start.2
  0.6 0.0 copy-start.4
  0.7 0.9 copy-done.4
  1.6 0.0 copy-start.5
  1.6 0.9 copy-done.5
  2.5 0.0 copy-start.6
  2.5 0.9 copy-done.6
  3.4 0.0 copy-start.7
  3.4 0.9 copy-done.7
  4.2 0.0 copy-start.8
  4.3 0.9 copy-done.8
  5.1 0.0 copy-start.9
  5.1 0.9 copy-done.9
  6.0 0.6 shard_map.131
  6.7 36.9 %all_to_all.15 = bf16[64,32,128]{2,1,0:T(8,128)(2,1)S(1)} all-to-all(bf16[64,32,128]{2,1,0:T(8,128)(2,1)S(1)} %shard_map.131), channel_id=1, replica_groups=mesh['z'=8,'x'=4,'yl'=2,'yh'=4,'c'=2] {'yh','c','z'}, dimensions={0} | all-to-all | bytes 1048576 | tf_op jit(solution)/shard_map/all_to_all | solution.py:237
  43.5 0.0 copy-done.2
  43.5 1.7 %shard_map.132 = (bf16[8,640,128]{2,1,0:T(8,128)(2,1)}, bf16[1280,128]{1,0:T(8,128)(2,1)S(1)}) custom-call(bf16[480,512]{1,0:T(8,128)(2,1)S(1)} %copy-done.2, bf16[8,8,32,128]{3,2,1,0:T(8,128)(2,1)S(1)} %bitcast.2), custom_call_target="tpu_custom_call" | custom-call | tf_op jit(solution)/shard_map/pallas_call | solution.py:94
  45.2 0.0 copy-start
  45.2 0.0 copy-start.1
  45.2 0.0 copy-start.3
  45.2 0.0 copy-start.10
  45.3 4.2 %all-to-all-start.1 = ((bf16[8,640,128]{2,1,0:T(8,128)(2,1)}), bf16[8,640,128]{2,1,0:T(8,128)(2,1)S(1)}, u32[]{:S(2)}, u32[]{:S(2)}) async-start(bf16[8,640,128]{2,1,0:T(8,128)(2,1)} %get-tuple-element.4), calls=%async_computation.1 | async-start | bytes 2621440 | tf_op jit(solution)/shard_map/all_to_all | solution.py:239
  50.1 16.1 %all-to-all-done.1.planes = bf16[8,640,128]{2,1,0:T(8,128)(2,1)S(1)} async-done(((bf16[8,640,128]{2,1,0:T(8,128)(2,1)}), bf16[8,640,128]{2,1,0:T(8,128)(2,1)S(1)}, u32[]{:S(2)}, u32[]{:S(2)}) %all-to-all-start.1) | async-done | bytes 1310752 | tf_op jit(solution)/shard_map/all_to_all | solution.py:239
  66.2 0.0 copy-done
  66.3 0.0 copy-done.1
  66.3 0.0 copy-done.3
  66.3 0.0 copy-done.10
  66.3 4.5 %shard_map.133 = bf16[8,8,16,128]{3,2,1,0:T(8,128)(2,1)S(1)} custom-call(s32[2]{0:T(128)S(1)} %copy-done.10, s32[1]{0:T(128)S(6)} %copy.14.length, bf16[8,640,128]{2,1,0:T(8,128)(2,1)S(1)} %all-to-all-done.1.planes, bf16[1280,128]{1,0:T(8,128)(2,1)S(1)} %get-tuple-element.5.own, bf16[512,640]{1,0:T(8,128)(2,1)S(1)} %copy-done, ...), custom_call_target="tpu_custom_call" | custom-call | tf_op jit(solution)/shard_map/pallas_call | solution.py:187
  70.8 22.9 %all_to_all.16.messages = bf16[64,16,128]{2,1,0:T(8,128)(2,1)S(1)} all-to-all(bf16[64,16,128]{2,1,0:T(8,128)(2,1)S(1)} %bitcast.3), channel_id=1, replica_groups=mesh['z'=8,'x'=4,'yl'=2,'yh'=4,'c'=2] {'yh','c','z'}, dimensions={0} | all-to-all | bytes 524288 | tf_op jit(solution)/shard_map/all_to_all | solution.py:241
  93.7 0.7 shard_map.134
Async XLA Ops:
  0.6 42.9 %copy-start.2 = (bf16[480,512]{1,0:T(8,128)(2,1)S(1)}, bf16[480,512]{1,0:T(8,128)(2,1)}, u32[]{:S(2)}) copy-start(bf16[480,512]{1,0:T(8,128)(2,1)} %constant.2.clone.order) | copy-start | bytes 1474564
  0.6 0.9 copy-start.4
  1.6 0.9 copy-start.5
  2.5 0.9 copy-start.6
  3.4 0.9 copy-start.7
  4.2 0.9 copy-start.8
  5.1 0.9 copy-start.9
  45.2 21.0 %copy-start = (bf16[512,640]{1,0:T(8,128)(2,1)S(1)}, bf16[512,640]{1,0:T(8,128)(2,1)}, u32[]{:S(2)}) copy-start(bf16[512,640]{1,0:T(8,128)(2,1)} %text_k.1) | copy-start | bytes 1966084
  45.2 21.0 %copy-start.1 = (bf16[512,640]{1,0:T(8,128)(2,1)S(1)}, bf16[512,640]{1,0:T(8,128)(2,1)}, u32[]{:S(2)}) copy-start(bf16[512,640]{1,0:T(8,128)(2,1)} %text_v.1) | copy-start | bytes 1966084
  45.2 21.0 %copy-start.3 = (f32[35,640]{1,0:T(8,128)S(1)}, f32[35,640]{1,0:T(8,128)}, u32[]{:S(2)}) copy-start(f32[35,640]{1,0:T(8,128)} %gates.1) | copy-start | bytes 268804
  45.2 21.0 %copy-start.10 = (s32[2]{0:T(128)S(1)}, s32[2]{0:T(128)}, u32[]{:S(2)}) copy-start(s32[2]{0:T(128)} %steps.1) | copy-start | bytes 28
  45.3 21.0 %all-to-all-start.1 = ((bf16[8,640,128]{2,1,0:T(8,128)(2,1)}), bf16[8,640,128]{2,1,0:T(8,128)(2,1)S(1)}, u32[]{:S(2)}, u32[]{:S(2)}) async-start(bf16[8,640,128]{2,1,0:T(8,128)(2,1)} %get-tuple-element.4), calls=%async_computation.1 | async-start | bytes 2621440 | tf_op jit(solution)/shard_map/all_to_all | solution.py:239

commit v2 on v1

v2 whole, which is shorter than its diff:
```python
import jax
import jax.numpy as jnp
import numpy as np
from jax import lax
from jax.experimental import pallas as pl
from jax.experimental.pallas import tpu as pltpu
from jax.sharding import Mesh
from jax.sharding import PartitionSpec as P

HEAD_DIM = 128
HEADS = 40
GROUP_HEADS = 5
PAIR_HEADS = 10
ROWS = 5
PLANE_ROWS = 320
BLOCK_ROWS = 20
PEERS = 64
CHUNK = 32
BACK = 16
TEXT = 512
EXP_SCALE = float(HEAD_DIM ** (-0.5) * np.log2(np.e))

AXES = ("z", "x", "yl", "yh", "c")
PLANE = ("z", "yl", "yh")
ACTIVE = 4 * PAIR_HEADS

NEAR_AT = 4 * 2 * PLANE_ROWS
TEXT_AT = NEAR_AT + 2 * PLANE_ROWS
GATE_AT = TEXT_AT + 2 * TEXT
SHARED = GATE_AT + 16
REST = SHARED - NEAR_AT

VMEM_LIMIT = 48 * 1024 * 1024


def dot_f32(left, right):
    return lax.dot_general(
        left, right, (((1,), (0,)), ((), ())), preferred_element_type=jnp.float32
    )


def dot_t_f32(left, right):
    return lax.dot_general(
        left, right, (((1,), (1,)), ((), ())), preferred_element_type=jnp.float32
    )


def one_hot(condition):
    return jnp.where(condition, 1.0, 0.0).astype(jnp.bfloat16)


def pack_kernel(k1, v1, q1, q2, k2, v2, out, held, sems):
    fetches = [
        pltpu.make_async_copy(array, held.at[index], sems.at[index])
        for index, array in enumerate((k1, v1, q1, q2, k2, v2))
    ]
    for fetch in fetches:
        fetch.start()
    total = None
    for index, fetch in enumerate(fetches):
        row = lax.broadcasted_iota(jnp.int32, (CHUNK, ROWS), 0)
        column = lax.broadcasted_iota(jnp.int32, (CHUNK, ROWS), 1)
        fetch.wait()
        part = dot_f32(one_hot(row == column + index * ROWS), held[index])
        total = part if total is None else total + part
    packed = total.astype(jnp.bfloat16)
    for rank in range(PEERS):
        if rank < ACTIVE:
            head = (rank % 4) * PAIR_HEADS + rank // 4
            out[rank] = packed[:, head * HEAD_DIM : (head + 1) * HEAD_DIM]
        else:
            out[rank] = jnp.zeros((CHUNK, HEAD_DIM), jnp.bfloat16)


def pack(*arrays):
    return pl.pallas_call(
        pack_kernel,
        out_shape=jax.ShapeDtypeStruct((PEERS, CHUNK, HEAD_DIM), jnp.bfloat16),
        in_specs=[pl.BlockSpec(memory_space=pltpu.HBM)] * 6,
        out_specs=pl.BlockSpec(memory_space=pltpu.VMEM),
        scratch_shapes=[
            pltpu.VMEM((6, ROWS, HEADS * HEAD_DIM), jnp.bfloat16),
            pltpu.SemaphoreType.DMA((6,)),
        ],
        compiler_params=pltpu.CompilerParams(vmem_limit_bytes=60 * 1024 * 1024),
    )(*arrays)


def head_slot():
    return lax.axis_index("z") * 2 + lax.axis_index("yl")


def unpack_kernel(steps, messages, text_k, text_v, gates, copies, queries, rest, gate, sems):
    slot = lax.rem(head_slot(), GROUP_HEADS)
    columns = pl.ds(pl.multiple_of(slot * HEAD_DIM, HEAD_DIM), HEAD_DIM)
    text_at = TEXT_AT - NEAR_AT
    fetches = [
        pltpu.make_async_copy(text_k.at[:, columns], rest.at[pl.ds(text_at, TEXT)], sems.at[0]),
        pltpu.make_async_copy(
            text_v.at[:, columns], rest.at[pl.ds(text_at + TEXT, TEXT)], sems.at[1]
        ),
        pltpu.make_async_copy(gates.at[:, columns], gate, sems.at[2]),
    ]
    for fetch in fetches:
        fetch.start()
    source = lax.broadcasted_iota(jnp.int32, (1, 512), 1)
    message, entry = source // CHUNK, source % CHUNK
    target = entry + ((entry * 13) // 64) * 75 + message * ROWS
    order = one_hot(lax.broadcasted_iota(jnp.int32, (480, 512), 0) == target)
    for step in range(4):
        rows = messages[pl.ds(step * 16, 16)].reshape(512, HEAD_DIM)
        ordered = dot_f32(order, rows).astype(jnp.bfloat16)
        for array in range(6):
            piece = ordered[array * 80 : (array + 1) * 80]
            place = pl.ds((array % 2) * PLANE_ROWS + step * 80, 80)
            if array < 2:
                for copy in range(4):
                    copies[copy, place] = piece
            elif array < 4:
                queries[place] = piece
            else:
                rest[place] = piece
    for fetch in fetches:
        fetch.wait()
    row = lax.broadcasted_iota(jnp.int32, (16, HEAD_DIM), 0)
    parts = jnp.zeros((16, HEAD_DIM), jnp.float32)
    for step in range(2):
        left = gate[pl.ds(steps[step], 1), :]
        for index in range(3):
            part = left.astype(jnp.bfloat16).astype(jnp.float32)
            parts = jnp.where(row == step * 3 + index, part, parts)
            left = left - part
    rest[pl.ds(GATE_AT - NEAR_AT, 16)] = parts.astype(jnp.bfloat16)


def unpack(timesteps, messages, text_keys, text_values, gate_table):
    vmem = pl.BlockSpec(memory_space=pltpu.VMEM)
    hbm = pl.BlockSpec(memory_space=pl.ANY)
    return pl.pallas_call(
        unpack_kernel,
        out_shape=(
            jax.ShapeDtypeStruct((4, 2 * PLANE_ROWS, HEAD_DIM), jnp.bfloat16),
            jax.ShapeDtypeStruct((2 * PLANE_ROWS, HEAD_DIM), jnp.bfloat16),
            jax.ShapeDtypeStruct((REST, HEAD_DIM), jnp.bfloat16),
        ),
        in_specs=[pl.BlockSpec(memory_space=pltpu.SMEM), vmem, hbm, hbm, hbm],
        out_specs=(vmem, vmem, vmem),
        scratch_shapes=[
            pltpu.VMEM((35, HEAD_DIM), jnp.float32),
            pltpu.SemaphoreType.DMA((3,)),
        ],
        compiler_params=pltpu.CompilerParams(vmem_limit_bytes=VMEM_LIMIT),
    )(timesteps, messages, text_keys, text_values, gate_table)


def join_kernel(planes, rest, out):
    out[pl.ds(0, NEAR_AT)] = planes[...].reshape(NEAR_AT, HEAD_DIM)
    out[pl.ds(NEAR_AT, REST)] = rest[...]


def join(planes, rest):
    return pl.pallas_call(
        join_kernel,
        out_shape=jax.ShapeDtypeStruct((SHARED, HEAD_DIM), jnp.bfloat16),
        compiler_params=pltpu.CompilerParams(vmem_limit_bytes=VMEM_LIMIT),
    )(planes, rest)


def block_of(index):
    return jnp.floor((index.astype(jnp.float32) + 0.5) * (1.0 / BLOCK_ROWS))


def attention_kernel(length, queries, mine, theirs, out, keys, values, text):
    own = lax.axis_index("x")
    for place in range(4):
        begin = pl.multiple_of(lax.rem(own + place, 4) * (2 * PLANE_ROWS), 2 * PLANE_ROWS)
        for side, shared in enumerate((mine, theirs)):
            target = pl.ds((place * 2 + side) * PLANE_ROWS, PLANE_ROWS)
            keys[target] = shared[pl.ds(begin, PLANE_ROWS)]
            values[target] = shared[pl.ds(begin + PLANE_ROWS, PLANE_ROWS)]
    here = head_slot() // GROUP_HEADS == lax.axis_index("c")

    @pl.when(here)
    def _():
        text[...] = mine[pl.ds(TEXT_AT, SHARED - TEXT_AT)]

    @pl.when(jnp.logical_not(here))
    def _():
        text[...] = theirs[pl.ds(TEXT_AT, SHARED - TEXT_AT)]

    near_keys, near_values = [
        jnp.concatenate([shared[pl.ds(begin, PLANE_ROWS)] for shared in (mine, theirs)], axis=0)
        for begin in (NEAR_AT, NEAR_AT + PLANE_ROWS)
    ]
    near = 2 * PLANE_ROWS
    parts = text[pl.ds(2 * TEXT, 16)].astype(jnp.float32)
    live = lax.broadcasted_iota(jnp.int32, (1, TEXT), 1) < length[0]
    column = lax.broadcasted_iota(jnp.int32, (1, near), 1)
    column_block = block_of(jnp.where(column < PLANE_ROWS, column, column - PLANE_ROWS))
    tile = 160
    finished = []
    for step in range(2):
        gate_row = parts[3 * step : 3 * step + 1] + parts[3 * step + 1 : 3 * step + 2]
        gate_row = gate_row + parts[3 * step + 2 : 3 * step + 3]
        for first in range(0, PLANE_ROWS, tile):
            rows = queries[pl.ds(step * PLANE_ROWS + first, tile), :]
            scores = dot_t_f32(rows, keys[...])
            text_scores = jnp.where(live, dot_t_f32(rows, text[pl.ds(0, TEXT)]), -1e30)
            if step == 1:
                row = block_of(lax.broadcasted_iota(jnp.int32, (tile, 1), 0) + first)
                same = row == column_block
                near_scores = jnp.where(same, dot_t_f32(rows, near_keys), scores[:, :near])
                scores = jnp.concatenate([near_scores, scores[:, near:]], axis=1)
            top = jnp.maximum(
                jnp.max(scores, axis=1, keepdims=True), jnp.max(text_scores, axis=1, keepdims=True)
            )
            raised = jnp.exp2((scores - top) * EXP_SCALE)
            text_raised = jnp.exp2((text_scores - top) * EXP_SCALE)
            total = jnp.sum(raised, axis=1, keepdims=True) + jnp.sum(
                text_raised, axis=1, keepdims=True
            )
            weights = raised.astype(jnp.bfloat16)
            numerator = dot_f32(text_raised.astype(jnp.bfloat16), text[pl.ds(TEXT, TEXT)])
            if step == 1:
                local = raised[:, :near]
                numerator += dot_f32(jnp.where(same, local, 0.0).astype(jnp.bfloat16), near_values)
                far = jnp.where(same, 0.0, local).astype(jnp.bfloat16)
                weights = jnp.concatenate([far, weights[:, near:]], axis=1)
            numerator += dot_f32(weights, values[...])
            finished.append((gate_row * (numerator / total)).astype(jnp.bfloat16))
    row = lax.broadcasted_iota(jnp.int32, (16 * BACK, 80), 0)
    column = lax.broadcasted_iota(jnp.int32, (16 * BACK, 80), 1)
    entry = row % BACK
    begin = (row // BACK) * ROWS
    place_first = one_hot((column == begin + entry) & (entry < ROWS))
    place_second = one_hot((column == begin + entry - 8) & (entry >= 8) & (entry < 8 + ROWS))
    for part in range(4):
        index, begin = part // 2, (part % 2) * 80
        message = dot_f32(place_first, finished[index][begin : begin + 80])
        message += dot_f32(place_second, finished[2 + index][begin : begin + 80])
        out[pl.ds(part * 16, 16)] = message.astype(jnp.bfloat16).reshape(16, BACK, HEAD_DIM)


def attention(text_length, queries, mine, theirs):
    vmem = pl.BlockSpec(memory_space=pltpu.VMEM)
    return pl.pallas_call(
        attention_kernel,
        out_shape=jax.ShapeDtypeStruct((PEERS, BACK, HEAD_DIM), jnp.bfloat16),
        in_specs=[pl.BlockSpec(memory_space=pltpu.SMEM), vmem, vmem, vmem],
        out_specs=vmem,
        scratch_shapes=[
            pltpu.VMEM((8 * PLANE_ROWS, HEAD_DIM), jnp.bfloat16),
            pltpu.VMEM((8 * PLANE_ROWS, HEAD_DIM), jnp.bfloat16),
            pltpu.VMEM((SHARED - TEXT_AT, HEAD_DIM), jnp.bfloat16),
        ],
        compiler_params=pltpu.CompilerParams(vmem_limit_bytes=VMEM_LIMIT),
    )(text_length, queries, mine, theirs)


def finish_kernel(messages, first, second):
    for rank in range(ACTIVE):
        head = (rank % 4) * PAIR_HEADS + rank // 4
        columns = pl.ds(head * HEAD_DIM, HEAD_DIM)
        message = messages[rank]
        first[:, columns] = message[0:ROWS]
        second[:, columns] = message[8 : 8 + ROWS]


def finish(messages):
    shape = jax.ShapeDtypeStruct((ROWS, HEADS * HEAD_DIM), jnp.bfloat16)
    return pl.pallas_call(
        finish_kernel,
        out_shape=(shape, shape),
        compiler_params=pltpu.CompilerParams(vmem_limit_bytes=VMEM_LIMIT),
    )(messages)


def body(
    query_first,
    keys_first,
    values_first,
    query_second,
    keys_second,
    values_second,
    text_keys,
    text_values,
    gate_table,
    timesteps,
    text_length,
):
    sent = pack(keys_first, values_first, query_first, query_second, keys_second, values_second)
    arrived = lax.all_to_all(sent, PLANE, 0, 0, tiled=True)
    copies, queries, rest = unpack(timesteps, arrived, text_keys, text_values, gate_table)
    planes = lax.all_to_all(copies, "x", 0, 0, tiled=True)
    mine = join(planes, rest)
    theirs = lax.ppermute(mine, "c", [(0, 1), (1, 0)])
    back = attention(text_length, queries, mine, theirs)
    returned = lax.all_to_all(back, PLANE, 0, 0, tiled=True)
    return finish(returned)


def solution(mesh):
    fine = Mesh(mesh.devices.reshape(8, 4, 2, 4, 2), AXES)
    rows = P(AXES, None)
    heads = P(None, ("yh", "c"))
    return jax.shard_map(
        body,
        mesh=fine,
        in_specs=(rows,) * 6 + (heads,) * 3 + (P(), P()),
        out_specs=(rows, rows),
        check_vma=False,
    )
```

time: 94.9 us -> 84.5 us (0.89)
  waiting for transfers between devices: 16.1 us -> 1.67 us
  blocking collectives: 59.8 us -> 66.2 us
  local copies, waits for them, and re-layouts: 5.39 us -> 0.02 us
  starting transfers between devices: 4.23 us -> 6.29 us
  Pallas kernels: 7.56 us -> 8.53 us
    all_to_all x1 -> x0, waiting for transfers between devices: 16.1 us -> none  [body(): planes = lax.all_to_all(copies, REPLICAS, 0, 0, tiled=True)]
    all_to_all x1 -> x2, blocking collectives: 22.9 us -> 30.3 us  [the longest x1 18.8 us: body(): returned = lax.all_to_all(back, PLANE, 0, 0, tiled=True)]
    ppermute x0 -> x1, starting transfers between devices: none -> 6.29 us  [body(): theirs = lax.ppermute(mine, 'c', [(0, 1), (1, 0)])]
    unnamed x22 -> x8, local copies, waits for them, and re-layouts: 5.39 us -> 0.02 us
    all_to_all x1 -> x0, starting transfers between devices: 4.23 us -> none  [body(): planes = lax.all_to_all(copies, REPLICAS, 0, 0, tiled=True)]
    ppermute x0 -> x1, waiting for transfers between devices: none -> 1.67 us  [body(): theirs = lax.ppermute(mine, 'c', [(0, 1), (1, 0)])]
    pallas_call x3 -> x4, Pallas kernels: 6.86 us -> 7.83 us  [the longest x1 3.86 us: attention(): pl.pallas_call(attention_kernel, out_shape=jax.ShapeDtypeStruct((PEERS, B...]
where the time goes in v2:
time: 84.5 us; the launch traced here: 84.1 us
  blocking collectives  66.2 us (78%)
  Pallas kernels  8.53 us (10%)
  starting transfers between devices  6.29 us (7%)
  waiting for transfers between devices  1.67 us (2%)
  between operations  1.36 us (2%)
    all_to_all x1, blocking collectives, body(): arrived = lax.all_to_all(sent, PLANE, 0, 0, tiled=True)  35.9 us
    all_to_all x1, blocking collectives, body(): returned = lax.all_to_all(back, PLANE, 0, 0, tiled=True)  18.8 us
    all_to_all x1, blocking collectives, body(): planes = lax.all_to_all(copies, 'x', 0, 0, tiled=True)  11.5 us
    ppermute x1, starting transfers between devices, body(): theirs = lax.ppermute(mine, 'c', [(0, 1), (1, 0)])  6.29 us
    pallas_call x1, Pallas kernels, attention(): pl.pallas_call(attention_kernel, out_shape=jax.ShapeDtypeStruct((PEERS, B...  3.86 us
    pallas_call x1, Pallas kernels, pack(): pl.pallas_call(pack_kernel, out_shape=jax.ShapeDtypeStruct((PEERS, CHUNK,...  2.55 us
  transfers between devices with their start and end apart: 1, of which 1 were waited for; matrix products, arithmetic and copies ran while one was open for 0% of the time, Pallas kernels for 0%

profile of v2, /device:TPU:1, one launch (start us, length us, event | category | flops | bytes accessed | tf_op | source)
XLA Modules:
  0.0 84.1 jit_solution(14674588508357459307)
XLA Ops:
  0.6 0.0 copy-start.3
  0.6 0.0 copy-start.2
  0.7 0.0 copy-start.1
  0.7 0.0 copy-start
  0.7 2.5 %shard_map.122 = bf16[64,32,128]{2,1,0:T(8,128)(2,1)} custom-call(bf16[5,5120]{1,0:T(8,128)(2,1)} %k1.1, bf16[5,5120]{1,0:T(8,128)(2,1)} %v1.1, bf16[5,5120]{1,0:T(8,128)(2,1)} %q1.1, bf16[5,5120]{1,0:T(8,128)(2,1)} %q2.1, bf16[5,5120]{1,0:T(8,128)(2,1)} %k2.1, bf16[5,5120]{1,0:T(8,128)(2,1)} %v2.1), custom_call_target="tpu_custom_call" | custom-call | tf_op jit(solution)/shard_map/pallas_call | solution.py:76
  3.2 35.9 %all_to_all.15.messages = bf16[64,32,128]{2,1,0:T(8,128)(2,1)S(1)} all-to-all(bf16[64,32,128]{2,1,0:T(8,128)(2,1)} %shard_map.122), channel_id=1, replica_groups=mesh['z'=8,'x'=4,'yl'=2,'yh'=4,'c'=2] {'z','yl','yh'}, dimensions={0} | all-to-all | bytes 1048576 | tf_op jit(solution)/shard_map/all_to_all | solution.py:292
  39.2 0.0 copy-done.3
  39.2 0.0 copy-done.2
  39.2 0.0 copy-done.1
  39.2 0.0 copy-done
  39.2 1.3 %shard_map.123 = (bf16[4,640,128]{2,1,0:T(8,128)(2,1)S(1)}, bf16[640,128]{1,0:T(8,128)(2,1)S(1)}, bf16[1680,128]{1,0:T(8,128)(2,1)S(1)}) custom-call(s32[2]{0:T(128)S(1)} %copy-done.3, bf16[64,32,128]{2,1,0:T(8,128)(2,1)S(1)} %all_to_all.15.messages, bf16[512,640]{1,0:T(8,128)(2,1)S(1)} %copy-done, bf16[512,640]{1,0:T(8,128)(2,1)S(1)} %copy-done.1, ...), custom_call_target="tpu_custom_call" | custom-call | tf_op jit(solution)/shard_map/pallas_call | solution.py:139
  40.5 11.5 %all_to_all.16.planes = bf16[4,640,128]{2,1,0:T(8,128)(2,1)S(1)} all-to-all(bf16[4,640,128]{2,1,0:T(8,128)(2,1)S(1)} %get-tuple-element.6), channel_id=1, replica_groups=mesh['z'=8,'x'=4,'yl'=2,'yh'=4,'c'=2] {'x'}, dimensions={0} | all-to-all | bytes 1310720 | tf_op jit(solution)/shard_map/all_to_all | solution.py:294
  52.0 0.1 shard_map.124.mine
  52.1 6.3 %collective-permute-start = (bf16[4240,128]{1,0:T(8,128)(2,1)S(1)}, bf16[4240,128]{1,0:T(8,128)(2,1)S(1)}, u32[]{:S(2)}, u32[]{:S(2)}) collective-permute-start(bf16[4240,128]{1,0:T(8,128)(2,1)S(1)} %shard_map.124.mine), channel_id=1, source_target_pairs={{0,1},{1,0},{2,3},{3,2},{4,5},{5,4},{6,7},{7,6},{8,9},{9,8},{10,11... | collective-permute-start | bytes 3256328 | tf_op jit(solution)/shard_map/ppermute | solution.py:296
  59.0 1.7 %collective-permute-done.theirs = bf16[4240,128]{1,0:T(8,128)(2,1)S(1)} collective-permute-done((bf16[4240,128]{1,0:T(8,128)(2,1)S(1)}, bf16[4240,128]{1,0:T(8,128)(2,1)S(1)}, u32[]{:S(2)}, u32[]{:S(2)}) %collective-permute-start) | collective-permute-done | bytes 1085472 | tf_op jit(solution)/shard_map/ppermute | solution.py:296
  60.7 3.9 %shard_map.125 = bf16[64,16,128]{2,1,0:T(8,128)(2,1)S(1)} custom-call(s32[1]{0:T(128)S(6)} %copy.13.length, bf16[640,128]{1,0:T(8,128)(2,1)S(1)} %get-tuple-element.5.queries, bf16[4240,128]{1,0:T(8,128)(2,1)S(1)} %shard_map.124.mine, bf16[4240,128]{1,0:T(8,128)(2,1)S(1)} %collective-permute-done.theirs), custom_call_target="tpu_custom_call" | custom-call | tf_op jit(solution)/shard_map/pallas_call | solution.py:246
  64.6 18.8 %all_to_all.17.messages = bf16[64,16,128]{2,1,0:T(8,128)(2,1)S(1)} all-to-all(bf16[64,16,128]{2,1,0:T(8,128)(2,1)S(1)} %shard_map.125), channel_id=1, replica_groups=mesh['z'=8,'x'=4,'yl'=2,'yh'=4,'c'=2] {'z','yl','yh'}, dimensions={0} | all-to-all | bytes 524288 | tf_op jit(solution)/shard_map/all_to_all | solution.py:298
  83.4 0.7 shard_map.126
Async XLA Ops:
  0.6 38.5 %copy-start.3 = (s32[2]{0:T(128)S(1)}, s32[2]{0:T(128)}, u32[]{:S(2)}) copy-start(s32[2]{0:T(128)} %steps.1) | copy-start | bytes 28
  0.6 38.5 %copy-start.2 = (f32[35,640]{1,0:T(8,128)S(1)}, f32[35,640]{1,0:T(8,128)}, u32[]{:S(2)}) copy-start(f32[35,640]{1,0:T(8,128)} %gates.1) | copy-start | bytes 268804
  0.7 38.5 %copy-start.1 = (bf16[512,640]{1,0:T(8,128)(2,1)S(1)}, bf16[512,640]{1,0:T(8,128)(2,1)}, u32[]{:S(2)}) copy-start(bf16[512,640]{1,0:T(8,128)(2,1)} %text_v.1) | copy-start | bytes 1966084
  0.7 38.5 %copy-start = (bf16[512,640]{1,0:T(8,128)(2,1)S(1)}, bf16[512,640]{1,0:T(8,128)(2,1)}, u32[]{:S(2)}) copy-start(bf16[512,640]{1,0:T(8,128)(2,1)} %text_k.1) | copy-start | bytes 1966084
  52.1 8.6 %collective-permute-start = (bf16[4240,128]{1,0:T(8,128)(2,1)S(1)}, bf16[4240,128]{1,0:T(8,128)(2,1)S(1)}, u32[]{:S(2)}, u32[]{:S(2)}) collective-permute-start(bf16[4240,128]{1,0:T(8,128)(2,1)S(1)} %shard_map.124.mine), channel_id=1, source_target_pairs={{0,1},{1,0},{2,3},{3,2},{4,5},{5,4},{6,7},{7,6},{8,9},{9,8},{10,11... | collective-permute-start | bytes 3256328 | tf_op jit(solution)/shard_map/ppermute | solution.py:296

commit v3 on v2

--- a/solution.py
+++ b/solution.py
@@ -24,7 +24,8 @@
 PLANE = ("z", "yl", "yh")
 ACTIVE = 4 * PAIR_HEADS
 
-NEAR_AT = 4 * 2 * PLANE_ROWS
+HALF = 4 * PLANE_ROWS
+NEAR_AT = 2 * HALF
 TEXT_AT = NEAR_AT + 2 * PLANE_ROWS
 GATE_AT = TEXT_AT + 2 * TEXT
 SHARED = GATE_AT + 16
@@ -43,6 +44,10 @@
     return lax.dot_general(
         left, right, (((1,), (1,)), ((), ())), preferred_element_type=jnp.float32
     )
+
+
+def in_hbm(array):
+    return pltpu.with_memory_space_constraint(array, pltpu.HBM)
 
 
 def one_hot(condition):
@@ -82,8 +87,8 @@
             pltpu.VMEM((6, ROWS, HEADS * HEAD_DIM), jnp.bfloat16),
             pltpu.SemaphoreType.DMA((6,)),
         ],
-        compiler_params=pltpu.CompilerParams(vmem_limit_bytes=60 * 1024 * 1024),
-    )(*arrays)
+        compiler_params=pltpu.CompilerParams(vmem_limit_bytes=VMEM_LIMIT),
+    )(*[in_hbm(array) for array in arrays])
 
 
 def head_slot():
@@ -103,16 +108,16 @@
     ]
     for fetch in fetches:
         fetch.start()
-    source = lax.broadcasted_iota(jnp.int32, (1, 512), 1)
+    source = lax.broadcasted_iota(jnp.int32, (1, 256), 1)
     message, entry = source // CHUNK, source % CHUNK
-    target = entry + ((entry * 13) // 64) * 75 + message * ROWS
-    order = one_hot(lax.broadcasted_iota(jnp.int32, (480, 512), 0) == target)
-    for step in range(4):
-        rows = messages[pl.ds(step * 16, 16)].reshape(512, HEAD_DIM)
+    target = entry + ((entry * 13) // 64) * 35 + message * ROWS
+    order = one_hot(lax.broadcasted_iota(jnp.int32, (240, 256), 0) == target)
+    for step in range(8):
+        rows = messages[pl.ds(step * 8, 8)].reshape(256, HEAD_DIM)
         ordered = dot_f32(order, rows).astype(jnp.bfloat16)
         for array in range(6):
-            piece = ordered[array * 80 : (array + 1) * 80]
-            place = pl.ds((array % 2) * PLANE_ROWS + step * 80, 80)
+            piece = ordered[array * 40 : (array + 1) * 40]
+            place = pl.ds((array % 2) * PLANE_ROWS + step * 40, 40)
             if array < 2:
                 for copy in range(4):
                     copies[copy, place] = piece
@@ -135,7 +140,7 @@
 
 def unpack(timesteps, messages, text_keys, text_values, gate_table):
     vmem = pl.BlockSpec(memory_space=pltpu.VMEM)
-    hbm = pl.BlockSpec(memory_space=pl.ANY)
+    hbm = pl.BlockSpec(memory_space=pltpu.HBM)
     return pl.pallas_call(
         unpack_kernel,
         out_shape=(
@@ -150,11 +155,17 @@
             pltpu.SemaphoreType.DMA((3,)),
         ],
         compiler_params=pltpu.CompilerParams(vmem_limit_bytes=VMEM_LIMIT),
-    )(timesteps, messages, text_keys, text_values, gate_table)
+    )(timesteps, messages, in_hbm(text_keys), in_hbm(text_values), in_hbm(gate_table))
 
 
 def join_kernel(planes, rest, out):
-    out[pl.ds(0, NEAR_AT)] = planes[...].reshape(NEAR_AT, HEAD_DIM)
+    own = lax.axis_index("x")
+    for place in range(4):
+        source = lax.rem(own + place, 4)
+        for part in range(2):
+            out[pl.ds(part * HALF + place * PLANE_ROWS, PLANE_ROWS)] = planes[
+                source, pl.ds(part * PLANE_ROWS, PLANE_ROWS)
+            ]
     out[pl.ds(NEAR_AT, REST)] = rest[...]
 
 
@@ -166,18 +177,104 @@
     )(planes, rest)
 
 
+TILE = 160
+TILES = 2 * PLANE_ROWS // TILE
+NEAR = 384
+CUTS = ((0, 512), (512, 1024), (1024, HALF))
+
+
 def block_of(index):
     return jnp.floor((index.astype(jnp.float32) + 0.5) * (1.0 / BLOCK_ROWS))
 
 
-def attention_kernel(length, queries, mine, theirs, out, keys, values, text):
-    own = lax.axis_index("x")
-    for place in range(4):
-        begin = pl.multiple_of(lax.rem(own + place, 4) * (2 * PLANE_ROWS), 2 * PLANE_ROWS)
-        for side, shared in enumerate((mine, theirs)):
-            target = pl.ds((place * 2 + side) * PLANE_ROWS, PLANE_ROWS)
-            keys[target] = shared[pl.ds(begin, PLANE_ROWS)]
-            values[target] = shared[pl.ds(begin + PLANE_ROWS, PLANE_ROWS)]
+def beside_ones(target, rows):
+    target[:, :HEAD_DIM] = rows
+    target[:, HEAD_DIM:] = jnp.ones_like(rows)
+
+
+def same_block(tile):
+    row = lax.broadcasted_iota(jnp.int32, (TILE, 1), 0) + (tile * TILE) % PLANE_ROWS
+    column = lax.broadcasted_iota(jnp.int32, (1, NEAR), 1)
+    return block_of(row) == block_of(column)
+
+
+def tile_rows(tile):
+    return pl.ds(tile * TILE, TILE)
+
+
+def half_scores(queries, keys, tile, cut):
+    rows = queries[tile_rows(tile)]
+    scores = dot_t_f32(rows, keys[pl.ds(cut[0], cut[1] - cut[0])])
+    if tile * TILE >= PLANE_ROWS and cut[0] == 0:
+        near = dot_t_f32(rows, keys[pl.ds(NEAR_AT, NEAR)])
+        near = jnp.where(same_block(tile), near, scores[:, :NEAR])
+        scores = jnp.concatenate([near, scores[:, NEAR:]], axis=1)
+    return scores
+
+
+def half_sums(weights, values, near_values, tile, cut):
+    part = values[pl.ds(cut[0], cut[1] - cut[0])]
+    if tile * TILE >= PLANE_ROWS and cut[0] == 0:
+        same = same_block(tile)
+        local = weights[:, :NEAR]
+        blank = jnp.zeros_like(local)
+        far = jnp.concatenate([jnp.where(same, blank, local), weights[:, NEAR:]], axis=1)
+        return dot_f32(far, part) + dot_f32(jnp.where(same, local, blank), near_values[...])
+    return dot_f32(weights, part)
+
+
+def lane_max(scores, former):
+    for begin in range(0, scores.shape[1], HEAD_DIM):
+        piece = scores[:, begin : begin + HEAD_DIM]
+        former = piece if former is None else jnp.maximum(former, piece)
+    return former
+
+
+def weigh(scores, top):
+    return jnp.exp2((scores - top) * EXP_SCALE).astype(jnp.bfloat16)
+
+
+def run_tiles(score_parts, sum_parts, start_top, finish_tile):
+    former = None
+    for tile in range(TILES + 1):
+        scores, lanes, sums = [], None, None
+        for index in range(len(score_parts)):
+            if tile < TILES:
+                part = score_parts[index](tile)
+                lanes = lane_max(part, lanes)
+                scores.append(part)
+            if former is not None:
+                part = sum_parts[index](weigh(former[0][index], former[1]), tile - 1)
+                sums = part if sums is None else sums + part
+        if former is not None:
+            finish_tile(tile - 1, former[1], sums)
+        if tile < TILES:
+            top = jnp.max(lanes, axis=1, keepdims=True)
+            former = (scores, start_top(tile, top))
+
+
+def first_kernel(queries, mine, sums, tops, values, near_values):
+    beside_ones(values, mine[pl.ds(HALF, HALF)])
+    beside_ones(near_values, mine[pl.ds(NEAR_AT + PLANE_ROWS, NEAR)])
+
+    def finish_tile(tile, top, total):
+        sums[tile_rows(tile)] = total
+        tops[tile_rows(tile)] = jnp.broadcast_to(top, (TILE, HEAD_DIM))
+
+    run_tiles(
+        [lambda tile, cut=cut: half_scores(queries, mine, tile, cut) for cut in CUTS],
+        [
+            lambda weights, tile, cut=cut: half_sums(weights, values, near_values, tile, cut)
+            for cut in CUTS
+        ],
+        lambda tile, top: top,
+        finish_tile,
+    )
+
+
+def second_kernel(
+    length, queries, mine, theirs, sums, tops, out, values, near_values, text, text_values, done
+):
     here = head_slot() // GROUP_HEADS == lax.axis_index("c")
 
     @pl.when(here)
@@ -188,46 +285,39 @@
     def _():
         text[...] = theirs[pl.ds(TEXT_AT, SHARED - TEXT_AT)]
 
-    near_keys, near_values = [
-        jnp.concatenate([shared[pl.ds(begin, PLANE_ROWS)] for shared in (mine, theirs)], axis=0)
-        for begin in (NEAR_AT, NEAR_AT + PLANE_ROWS)
-    ]
-    near = 2 * PLANE_ROWS
+    beside_ones(values, theirs[pl.ds(HALF, HALF)])
+    beside_ones(near_values, theirs[pl.ds(NEAR_AT + PLANE_ROWS, NEAR)])
+    beside_ones(text_values, text[pl.ds(TEXT, TEXT)])
     parts = text[pl.ds(2 * TEXT, 16)].astype(jnp.float32)
     live = lax.broadcasted_iota(jnp.int32, (1, TEXT), 1) < length[0]
-    column = lax.broadcasted_iota(jnp.int32, (1, near), 1)
-    column_block = block_of(jnp.where(column < PLANE_ROWS, column, column - PLANE_ROWS))
-    tile = 160
-    finished = []
-    for step in range(2):
-        gate_row = parts[3 * step : 3 * step + 1] + parts[3 * step + 1 : 3 * step + 2]
-        gate_row = gate_row + parts[3 * step + 2 : 3 * step + 3]
-        for first in range(0, PLANE_ROWS, tile):
-            rows = queries[pl.ds(step * PLANE_ROWS + first, tile), :]
-            scores = dot_t_f32(rows, keys[...])
-            text_scores = jnp.where(live, dot_t_f32(rows, text[pl.ds(0, TEXT)]), -1e30)
-            if step == 1:
-                row = block_of(lax.broadcasted_iota(jnp.int32, (tile, 1), 0) + first)
-                same = row == column_block
-                near_scores = jnp.where(same, dot_t_f32(rows, near_keys), scores[:, :near])
-                scores = jnp.concatenate([near_scores, scores[:, near:]], axis=1)
-            top = jnp.maximum(
-                jnp.max(scores, axis=1, keepdims=True), jnp.max(text_scores, axis=1, keepdims=True)
-            )
-            raised = jnp.exp2((scores - top) * EXP_SCALE)
-            text_raised = jnp.exp2((text_scores - top) * EXP_SCALE)
-            total = jnp.sum(raised, axis=1, keepdims=True) + jnp.sum(
-                text_raised, axis=1, keepdims=True
-            )
-            weights = raised.astype(jnp.bfloat16)
-            numerator = dot_f32(text_raised.astype(jnp.bfloat16), text[pl.ds(TEXT, TEXT)])
-            if step == 1:
-                local = raised[:, :near]
-                numerator += dot_f32(jnp.where(same, local, 0.0).astype(jnp.bfloat16), near_values)
-                far = jnp.where(same, 0.0, local).astype(jnp.bfloat16)
-                weights = jnp.concatenate([far, weights[:, near:]], axis=1)
-            numerator += dot_f32(weights, values[...])
-            finished.append((gate_row * (numerator / total)).astype(jnp.bfloat16))
+
+    def text_scores(tile):
+        scores = dot_t_f32(queries[tile_rows(tile)], text[pl.ds(0, TEXT)])
+        return jnp.where(live, scores, -1e30)
+
+    def start_top(tile, top):
+        return jnp.maximum(tops[tile_rows(tile), 0:1], top)
+
+    def finish_tile(tile, top, total):
+        former = jnp.exp2((tops[tile_rows(tile), 0:1] - top) * EXP_SCALE)
+        total = total + sums[tile_rows(tile)] * former
+        step = tile * TILE // PLANE_ROWS
+        gate = parts[3 * step : 3 * step + 1] + parts[3 * step + 1 : 3 * step + 2]
+        gate = gate + parts[3 * step + 2 : 3 * step + 3]
+        attended = total[:, :HEAD_DIM] / total[:, HEAD_DIM:]
+        done[tile_rows(tile)] = (gate * attended).astype(jnp.bfloat16)
+
+    run_tiles(
+        [lambda tile, cut=cut: half_scores(queries, theirs, tile, cut) for cut in CUTS]
+        + [text_scores],
+        [
+            lambda weights, tile, cut=cut: half_sums(weights, values, near_values, tile, cut)
+            for cut in CUTS
+        ]
+        + [lambda weights, tile: dot_f32(weights, text_values[...])],
+        start_top,
+        finish_tile,
+    )
     row = lax.broadcasted_iota(jnp.int32, (16 * BACK, 80), 0)
     column = lax.broadcasted_iota(jnp.int32, (16 * BACK, 80), 1)
     entry = row % BACK
@@ -235,26 +325,48 @@
     place_first = one_hot((column == begin + entry) & (entry < ROWS))
     place_second = one_hot((column == begin + entry - 8) & (entry >= 8) & (entry < 8 + ROWS))
     for part in range(4):
-        index, begin = part // 2, (part % 2) * 80
-        message = dot_f32(place_first, finished[index][begin : begin + 80])
-        message += dot_f32(place_second, finished[2 + index][begin : begin + 80])
+        message = dot_f32(place_first, done[pl.ds(part * 80, 80)])
+        message += dot_f32(place_second, done[pl.ds(PLANE_ROWS + part * 80, 80)])
         out[pl.ds(part * 16, 16)] = message.astype(jnp.bfloat16).reshape(16, BACK, HEAD_DIM)
 
 
-def attention(text_length, queries, mine, theirs):
+def first_pass(queries, mine):
     vmem = pl.BlockSpec(memory_space=pltpu.VMEM)
     return pl.pallas_call(
-        attention_kernel,
+        first_kernel,
+        out_shape=(
+            jax.ShapeDtypeStruct((2 * PLANE_ROWS, 2 * HEAD_DIM), jnp.float32),
+            jax.ShapeDtypeStruct((2 * PLANE_ROWS, HEAD_DIM), jnp.float32),
+        ),
+        in_specs=[vmem, vmem],
+        out_specs=(vmem, vmem),
+        scratch_shapes=[
+            pltpu.VMEM((HALF, 2 * HEAD_DIM), jnp.bfloat16),
+            pltpu.VMEM((NEAR, 2 * HEAD_DIM), jnp.bfloat16),
+        ],
+        cost_estimate=pl.CostEstimate(
+            flops=4 * 640 * 1600 * HEAD_DIM, bytes_accessed=2 * SHARED * HEAD_DIM, transcendentals=640 * HALF
+        ),
+        compiler_params=pltpu.CompilerParams(vmem_limit_bytes=VMEM_LIMIT),
+    )(queries, mine)
+
+
+def second_pass(text_length, queries, mine, theirs, sums, tops):
+    vmem = pl.BlockSpec(memory_space=pltpu.VMEM)
+    return pl.pallas_call(
+        second_kernel,
         out_shape=jax.ShapeDtypeStruct((PEERS, BACK, HEAD_DIM), jnp.bfloat16),
-        in_specs=[pl.BlockSpec(memory_space=pltpu.SMEM), vmem, vmem, vmem],
+        in_specs=[pl.BlockSpec(memory_space=pltpu.SMEM)] + [vmem] * 5,
         out_specs=vmem,
         scratch_shapes=[
-            pltpu.VMEM((8 * PLANE_ROWS, HEAD_DIM), jnp.bfloat16),
-            pltpu.VMEM((8 * PLANE_ROWS, HEAD_DIM), jnp.bfloat16),
+            pltpu.VMEM((HALF, 2 * HEAD_DIM), jnp.bfloat16),
+            pltpu.VMEM((NEAR, 2 * HEAD_DIM), jnp.bfloat16),
             pltpu.VMEM((SHARED - TEXT_AT, HEAD_DIM), jnp.bfloat16),
+            pltpu.VMEM((TEXT, 2 * HEAD_DIM), jnp.bfloat16),
+            pltpu.VMEM((2 * PLANE_ROWS, HEAD_DIM), jnp.bfloat16),
         ],
         compiler_params=pltpu.CompilerParams(vmem_limit_bytes=VMEM_LIMIT),
-    )(text_length, queries, mine, theirs)
+    )(text_length, queries, mine, theirs, sums, tops)
 
 
 def finish_kernel(messages, first, second):
@@ -294,7 +406,8 @@
     planes = lax.all_to_all(copies, "x", 0, 0, tiled=True)
     mine = join(planes, rest)
     theirs = lax.ppermute(mine, "c", [(0, 1), (1, 0)])
-    back = attention(text_length, queries, mine, theirs)
+    sums, tops = first_pass(queries, mine)
+    back = second_pass(text_length, queries, mine, theirs, sums, tops)
     returned = lax.all_to_all(back, PLANE, 0, 0, tiled=True)
     return finish(returned)
 

time: 84.5 us -> 82.2 us (0.973)
  waiting for transfers between devices: 1.67 us -> 0.06 us
    ppermute x1, waiting for transfers between devices: 1.67 us -> 0.06 us  [body(): theirs = lax.ppermute(mine, 'c', [(0, 1), (1, 0)])]
    pallas_call x1, Pallas kernels: 2.55 us -> 1.64 us  [pack(): pl.pallas_call(pack_kernel, out_shape=jax.ShapeDtypeStruct((PEERS, CHUNK,...]
    pallas_call x1 -> x2, Pallas kernels: 3.86 us -> 4.07 us  [the longest x1 2.47 us: second_pass(): pl.pallas_call(second_kernel, out_shape=jax.ShapeDtypeStruct((PEERS, BACK...]
  transfers between devices with their start and end apart: 1 -> 1, of which waited for: 1 -> 1; matrix products, arithmetic and copies ran while one was open for 0% -> 0% of each run, Pallas kernels for 0% -> 2%
where the time goes in v3:
time: 82.2 us; the launch traced here: 81.8 us
  blocking collectives  66 us (80%)
  Pallas kernels  8.07 us (10%)
  starting transfers between devices  6.28 us (8%)
  between operations  1.33 us (2%)
    all_to_all x1, blocking collectives, body(): arrived = lax.all_to_all(sent, PLANE, 0, 0, tiled=True)  35.7 us
    all_to_all x1, blocking collectives, body(): returned = lax.all_to_all(back, PLANE, 0, 0, tiled=True)  18.8 us
    all_to_all x1, blocking collectives, body(): planes = lax.all_to_all(copies, 'x', 0, 0, tiled=True)  11.5 us
    ppermute x1, starting transfers between devices, body(): theirs = lax.ppermute(mine, 'c', [(0, 1), (1, 0)])  6.28 us
    pallas_call x1, Pallas kernels, second_pass(): pl.pallas_call(second_kernel, out_shape=jax.ShapeDtypeStruct((PEERS, BACK...  2.47 us
  transfers between devices with their start and end apart: 1, of which 1 were waited for; matrix products, arithmetic and copies ran while one was open for 0% of the time, Pallas kernels for 2%

profile of v3, /device:TPU:1, one launch (start us, length us, event | category | flops | bytes accessed | tf_op | source)
XLA Modules:
  0.0 81.8 jit_solution(16049243577113515261)
XLA Ops:
  0.6 0.0 copy-start
  0.6 1.6 %shard_map.122 = bf16[64,32,128]{2,1,0:T(8,128)(2,1)S(1)} custom-call(bf16[5,5120]{1,0:T(8,128)(2,1)} %k1.1, bf16[5,5120]{1,0:T(8,128)(2,1)} %v1.1, bf16[5,5120]{1,0:T(8,128)(2,1)} %q1.1, bf16[5,5120]{1,0:T(8,128)(2,1)} %q2.1, bf16[5,5120]{1,0:T(8,128)(2,1)} %k2.1, bf16[5,5120]{1,0:T(8,128)(2,1)} %v2.1), custom_call_target="tpu_custom_call" | custom-call | tf_op jit(solution)/shard_map/pallas_call | solution.py:81
  2.3 35.7 %all_to_all.15.messages = bf16[64,32,128]{2,1,0:T(8,128)(2,1)S(1)} all-to-all(bf16[64,32,128]{2,1,0:T(8,128)(2,1)S(1)} %shard_map.122), channel_id=1, replica_groups=mesh['z'=8,'x'=4,'yl'=2,'yh'=4,'c'=2] {'z','yl','yh'}, dimensions={0} | all-to-all | bytes 1048576 | tf_op jit(solution)/shard_map/all_to_all | solution.py:404
  38.0 0.0 copy-done
  38.0 1.6 %shard_map.123 = (bf16[4,640,128]{2,1,0:T(8,128)(2,1)S(1)}, bf16[640,128]{1,0:T(8,128)(2,1)S(1)}, bf16[1680,128]{1,0:T(8,128)(2,1)S(1)}) custom-call(s32[2]{0:T(128)S(1)} %copy-done, bf16[64,32,128]{2,1,0:T(8,128)(2,1)S(1)} %all_to_all.15.messages, bf16[512,640]{1,0:T(8,128)(2,1)} %text_k.1, bf16[512,640]{1,0:T(8,128)(2,1)} %text_v.1, f32[35,640]{1,0:T(8,128)} %gates.1), custom_call_target="tpu_custom_call" | custom-call | tf_op jit(solution)/shard_map/pallas_call | solution.py:144
  39.6 11.5 %all_to_all.16.planes = bf16[4,640,128]{2,1,0:T(8,128)(2,1)S(1)} all-to-all(bf16[4,640,128]{2,1,0:T(8,128)(2,1)S(1)} %get-tuple-element.8), channel_id=1, replica_groups=mesh['z'=8,'x'=4,'yl'=2,'yh'=4,'c'=2] {'x'}, dimensions={0} | all-to-all | bytes 1310720 | tf_op jit(solution)/shard_map/all_to_all | solution.py:406
  51.1 0.1 shard_map.124.mine
  51.1 6.3 %collective-permute-start = (bf16[4240,128]{1,0:T(8,128)(2,1)S(1)}, bf16[4240,128]{1,0:T(8,128)(2,1)S(1)}, u32[]{:S(2)}, u32[]{:S(2)}) collective-permute-start(bf16[4240,128]{1,0:T(8,128)(2,1)S(1)} %shard_map.124.mine), channel_id=1, source_target_pairs={{0,1},{1,0},{2,3},{3,2},{4,5},{5,4},{6,7},{7,6},{8,9},{9,8},{10,11... | collective-permute-start | bytes 3256328 | tf_op jit(solution)/shard_map/ppermute | solution.py:408
  58.1 1.6 %shard_map.125 = (f32[640,256]{1,0:T(8,128)S(1)}, f32[640,128]{1,0:T(8,128)S(1)}) custom-call(bf16[640,128]{1,0:T(8,128)(2,1)S(1)} %get-tuple-element.7.queries, bf16[4240,128]{1,0:T(8,128)(2,1)S(1)} %shard_map.124.mine), custom_call_target="tpu_custom_call" | custom-call | flops 524288000 | bytes 1085440 | tf_op jit(solution)/shard_map/pallas_call | solution.py:335
  59.7 0.1 collective-permute-done.theirs
  59.8 2.5 %shard_map.126 = bf16[64,16,128]{2,1,0:T(8,128)(2,1)S(1)} custom-call(s32[1]{0:T(128)S(6)} %copy.13.length, bf16[640,128]{1,0:T(8,128)(2,1)S(1)} %get-tuple-element.7.queries, bf16[4240,128]{1,0:T(8,128)(2,1)S(1)} %shard_map.124.mine, bf16[4240,128]{1,0:T(8,128)(2,1)S(1)} %collective-permute-done.theirs, f32[640,256]{1,0:T(8,128)S(1)} %get-tuple-element.10.sums, ...), custom_call_target="tpu_custom_call" | custom-call | tf_op jit(solution)/shard_map/pallas_call | solution.py:356
  62.2 18.8 %all_to_all.17.messages = bf16[64,16,128]{2,1,0:T(8,128)(2,1)S(1)} all-to-all(bf16[64,16,128]{2,1,0:T(8,128)(2,1)S(1)} %shard_map.126), channel_id=1, replica_groups=mesh['z'=8,'x'=4,'yl'=2,'yh'=4,'c'=2] {'z','yl','yh'}, dimensions={0} | all-to-all | bytes 524288 | tf_op jit(solution)/shard_map/all_to_all | solution.py:411
  81.1 0.7 shard_map.127
Async XLA Ops:
  0.6 37.4 %copy-start = (s32[2]{0:T(128)S(1)}, s32[2]{0:T(128)}, u32[]{:S(2)}) copy-start(s32[2]{0:T(128)} %steps.1) | copy-start | bytes 28
  51.1 8.6 %collective-permute-start = (bf16[4240,128]{1,0:T(8,128)(2,1)S(1)}, bf16[4240,128]{1,0:T(8,128)(2,1)S(1)}, u32[]{:S(2)}, u32[]{:S(2)}) collective-permute-start(bf16[4240,128]{1,0:T(8,128)(2,1)S(1)} %shard_map.124.mine), channel_id=1, source_target_pairs={{0,1},{1,0},{2,3},{3,2},{4,5},{5,4},{6,7},{7,6},{8,9},{9,8},{10,11... | collective-permute-start | bytes 3256328 | tf_op jit(solution)/shard_map/ppermute | solution.py:408

commit v4 on v3

--- a/solution.py
+++ b/solution.py
@@ -29,7 +29,7 @@
 TEXT_AT = NEAR_AT + 2 * PLANE_ROWS
 GATE_AT = TEXT_AT + 2 * TEXT
 SHARED = GATE_AT + 16
-REST = SHARED - NEAR_AT
+EXTRA = SHARED - TEXT_AT
 
 VMEM_LIMIT = 48 * 1024 * 1024
 
@@ -46,6 +46,10 @@
     )
 
 
+def head_slot():
+    return lax.axis_index("z") * 2 + lax.axis_index("yl")
+
+
 def in_hbm(array):
     return pltpu.with_memory_space_constraint(array, pltpu.HBM)
 
@@ -54,18 +58,29 @@
     return jnp.where(condition, 1.0, 0.0).astype(jnp.bfloat16)
 
 
-def pack_kernel(k1, v1, q1, q2, k2, v2, out, held, sems):
+def pack_kernel(
+    k1, v1, q1, q2, k2, v2, text_k, text_v, gates, steps, out, extra, held, gate, step_ids, sems
+):
+    slot = lax.rem(head_slot(), GROUP_HEADS)
+    columns = pl.ds(pl.multiple_of(slot * HEAD_DIM, HEAD_DIM), HEAD_DIM)
+    targets = [(array, held.at[index]) for index, array in enumerate((k1, v1, q1, q2, k2, v2))]
+    targets += [
+        (steps, step_ids),
+        (gates.at[:, columns], gate),
+        (text_k.at[:, columns], extra.at[pl.ds(0, TEXT)]),
+        (text_v.at[:, columns], extra.at[pl.ds(TEXT, TEXT)]),
+    ]
     fetches = [
-        pltpu.make_async_copy(array, held.at[index], sems.at[index])
-        for index, array in enumerate((k1, v1, q1, q2, k2, v2))
+        pltpu.make_async_copy(source, target, sems.at[index])
+        for index, (source, target) in enumerate(targets)
     ]
     for fetch in fetches:
         fetch.start()
     total = None
-    for index, fetch in enumerate(fetches):
+    for index in range(6):
         row = lax.broadcasted_iota(jnp.int32, (CHUNK, ROWS), 0)
         column = lax.broadcasted_iota(jnp.int32, (CHUNK, ROWS), 1)
-        fetch.wait()
+        fetches[index].wait()
         part = dot_f32(one_hot(row == column + index * ROWS), held[index])
         total = part if total is None else total + part
     packed = total.astype(jnp.bfloat16)
@@ -75,39 +90,40 @@
             out[rank] = packed[:, head * HEAD_DIM : (head + 1) * HEAD_DIM]
         else:
             out[rank] = jnp.zeros((CHUNK, HEAD_DIM), jnp.bfloat16)
+    for fetch in fetches[6:]:
+        fetch.wait()
+    row = lax.broadcasted_iota(jnp.int32, (16, HEAD_DIM), 0)
+    parts = jnp.zeros((16, HEAD_DIM), jnp.float32)
+    for step in range(2):
+        left = gate[pl.ds(step_ids[step], 1), :]
+        for index in range(3):
+            part = left.astype(jnp.bfloat16).astype(jnp.float32)
+            parts = jnp.where(row == step * 3 + index, part, parts)
+            left = left - part
+    extra[pl.ds(2 * TEXT, 16)] = parts.astype(jnp.bfloat16)
 
 
 def pack(*arrays):
+    vmem = pl.BlockSpec(memory_space=pltpu.VMEM)
     return pl.pallas_call(
         pack_kernel,
-        out_shape=jax.ShapeDtypeStruct((PEERS, CHUNK, HEAD_DIM), jnp.bfloat16),
-        in_specs=[pl.BlockSpec(memory_space=pltpu.HBM)] * 6,
-        out_specs=pl.BlockSpec(memory_space=pltpu.VMEM),
+        out_shape=(
+            jax.ShapeDtypeStruct((PEERS, CHUNK, HEAD_DIM), jnp.bfloat16),
+            jax.ShapeDtypeStruct((EXTRA, HEAD_DIM), jnp.bfloat16),
+        ),
+        in_specs=[pl.BlockSpec(memory_space=pltpu.HBM)] * 10,
+        out_specs=(vmem, vmem),
         scratch_shapes=[
             pltpu.VMEM((6, ROWS, HEADS * HEAD_DIM), jnp.bfloat16),
-            pltpu.SemaphoreType.DMA((6,)),
+            pltpu.VMEM((35, HEAD_DIM), jnp.float32),
+            pltpu.SMEM((2,), jnp.int32),
+            pltpu.SemaphoreType.DMA((10,)),
         ],
         compiler_params=pltpu.CompilerParams(vmem_limit_bytes=VMEM_LIMIT),
     )(*[in_hbm(array) for array in arrays])
 
 
-def head_slot():
-    return lax.axis_index("z") * 2 + lax.axis_index("yl")
-
-
-def unpack_kernel(steps, messages, text_k, text_v, gates, copies, queries, rest, gate, sems):
-    slot = lax.rem(head_slot(), GROUP_HEADS)
-    columns = pl.ds(pl.multiple_of(slot * HEAD_DIM, HEAD_DIM), HEAD_DIM)
-    text_at = TEXT_AT - NEAR_AT
-    fetches = [
-        pltpu.make_async_copy(text_k.at[:, columns], rest.at[pl.ds(text_at, TEXT)], sems.at[0]),
-        pltpu.make_async_copy(
-            text_v.at[:, columns], rest.at[pl.ds(text_at + TEXT, TEXT)], sems.at[1]
-        ),
-        pltpu.make_async_copy(gates.at[:, columns], gate, sems.at[2]),
-    ]
-    for fetch in fetches:
-        fetch.start()
+def unpack_kernel(messages, copies, queries, near):
     source = lax.broadcasted_iota(jnp.int32, (1, 256), 1)
     message, entry = source // CHUNK, source % CHUNK
     target = entry + ((entry * 13) // 64) * 35 + message * ROWS
@@ -124,41 +140,23 @@
             elif array < 4:
                 queries[place] = piece
             else:
-                rest[place] = piece
-    for fetch in fetches:
-        fetch.wait()
-    row = lax.broadcasted_iota(jnp.int32, (16, HEAD_DIM), 0)
-    parts = jnp.zeros((16, HEAD_DIM), jnp.float32)
-    for step in range(2):
-        left = gate[pl.ds(steps[step], 1), :]
-        for index in range(3):
-            part = left.astype(jnp.bfloat16).astype(jnp.float32)
-            parts = jnp.where(row == step * 3 + index, part, parts)
-            left = left - part
-    rest[pl.ds(GATE_AT - NEAR_AT, 16)] = parts.astype(jnp.bfloat16)
-
-
-def unpack(timesteps, messages, text_keys, text_values, gate_table):
-    vmem = pl.BlockSpec(memory_space=pltpu.VMEM)
-    hbm = pl.BlockSpec(memory_space=pltpu.HBM)
+                near[place] = piece
+
+
+def unpack(messages):
+    rows = jax.ShapeDtypeStruct((2 * PLANE_ROWS, HEAD_DIM), jnp.bfloat16)
     return pl.pallas_call(
         unpack_kernel,
         out_shape=(
             jax.ShapeDtypeStruct((4, 2 * PLANE_ROWS, HEAD_DIM), jnp.bfloat16),
-            jax.ShapeDtypeStruct((2 * PLANE_ROWS, HEAD_DIM), jnp.bfloat16),
-            jax.ShapeDtypeStruct((REST, HEAD_DIM), jnp.bfloat16),
+            rows,
+            rows,
         ),
-        in_specs=[pl.BlockSpec(memory_space=pltpu.SMEM), vmem, hbm, hbm, hbm],
-        out_specs=(vmem, vmem, vmem),
-        scratch_shapes=[
-            pltpu.VMEM((35, HEAD_DIM), jnp.float32),
-            pltpu.SemaphoreType.DMA((3,)),
-        ],
-        compiler_params=pltpu.CompilerParams(vmem_limit_bytes=VMEM_LIMIT),
-    )(timesteps, messages, in_hbm(text_keys), in_hbm(text_values), in_hbm(gate_table))
-
-
-def join_kernel(planes, rest, out):
+        compiler_params=pltpu.CompilerParams(vmem_limit_bytes=VMEM_LIMIT),
+    )(messages)
+
+
+def join_kernel(planes, near, extra, out):
     own = lax.axis_index("x")
     for place in range(4):
         source = lax.rem(own + place, 4)
@@ -166,15 +164,16 @@
             out[pl.ds(part * HALF + place * PLANE_ROWS, PLANE_ROWS)] = planes[
                 source, pl.ds(part * PLANE_ROWS, PLANE_ROWS)
             ]
-    out[pl.ds(NEAR_AT, REST)] = rest[...]
-
-
-def join(planes, rest):
+    out[pl.ds(NEAR_AT, 2 * PLANE_ROWS)] = near[...]
+    out[pl.ds(TEXT_AT, EXTRA)] = extra[...]
+
+
+def join(planes, near, extra):
     return pl.pallas_call(
         join_kernel,
         out_shape=jax.ShapeDtypeStruct((SHARED, HEAD_DIM), jnp.bfloat16),
         compiler_params=pltpu.CompilerParams(vmem_limit_bytes=VMEM_LIMIT),
-    )(planes, rest)
+    )(planes, near, extra)
 
 
 TILE = 160
@@ -279,11 +278,11 @@
 
     @pl.when(here)
     def _():
-        text[...] = mine[pl.ds(TEXT_AT, SHARED - TEXT_AT)]
+        text[...] = mine[pl.ds(TEXT_AT, EXTRA)]
 
     @pl.when(jnp.logical_not(here))
     def _():
-        text[...] = theirs[pl.ds(TEXT_AT, SHARED - TEXT_AT)]
+        text[...] = theirs[pl.ds(TEXT_AT, EXTRA)]
 
     beside_ones(values, theirs[pl.ds(HALF, HALF)])
     beside_ones(near_values, theirs[pl.ds(NEAR_AT + PLANE_ROWS, NEAR)])
@@ -361,7 +360,7 @@
         scratch_shapes=[
             pltpu.VMEM((HALF, 2 * HEAD_DIM), jnp.bfloat16),
             pltpu.VMEM((NEAR, 2 * HEAD_DIM), jnp.bfloat16),
-            pltpu.VMEM((SHARED - TEXT_AT, HEAD_DIM), jnp.bfloat16),
+            pltpu.VMEM((EXTRA, HEAD_DIM), jnp.bfloat16),
             pltpu.VMEM((TEXT, 2 * HEAD_DIM), jnp.bfloat16),
             pltpu.VMEM((2 * PLANE_ROWS, HEAD_DIM), jnp.bfloat16),
         ],
@@ -400,11 +399,22 @@
     timesteps,
     text_length,
 ):
-    sent = pack(keys_first, values_first, query_first, query_second, keys_second, values_second)
+    sent, extra = pack(
+        keys_first,
+        values_first,
+        query_first,
+        query_second,
+        keys_second,
+        values_second,
+        text_keys,
+        text_values,
+        gate_table,
+        timesteps,
+    )
     arrived = lax.all_to_all(sent, PLANE, 0, 0, tiled=True)
-    copies, queries, rest = unpack(timesteps, arrived, text_keys, text_values, gate_table)
+    copies, queries, near = unpack(arrived)
     planes = lax.all_to_all(copies, "x", 0, 0, tiled=True)
-    mine = join(planes, rest)
+    mine = join(planes, near, extra)
     theirs = lax.ppermute(mine, "c", [(0, 1), (1, 0)])
     sums, tops = first_pass(queries, mine)
     back = second_pass(text_length, queries, mine, theirs, sums, tops)

time: 82.2 us -> 81 us (0.985)
  Pallas kernels: 8.07 us -> 6.95 us
    pallas_call x1, Pallas kernels: 1.58 us -> 0.4 us  [unpack(): pl.pallas_call(unpack_kernel, out_shape=(jax.ShapeDtypeStruct((4, 2 * PLA...]
  transfers between devices with their start and end apart: 1 -> 1, of which waited for: 1 -> 0; matrix products, arithmetic and copies ran while one was open for 0% -> 0% of each run, Pallas kernels for 2% -> 2%
where the time goes in v4:
time: 81 us; the launch traced here: 80.7 us
  blocking collectives  66.1 us (82%)
  Pallas kernels  6.95 us (9%)
  starting transfers between devices  6.28 us (8%)
  between operations  1.32 us (2%)
    all_to_all x1, blocking collectives, body(): arrived = lax.all_to_all(sent, PLANE, 0, 0, tiled=True)  35.8 us
    all_to_all x1, blocking collectives, body(): returned = lax.all_to_all(back, PLANE, 0, 0, tiled=True)  18.8 us
    all_to_all x1, blocking collectives, body(): planes = lax.all_to_all(copies, 'x', 0, 0, tiled=True)  11.5 us
    ppermute x1, starting transfers between devices, body(): theirs = lax.ppermute(mine, 'c', [(0, 1), (1, 0)])  6.28 us
    pallas_call x1, Pallas kernels, second_pass(): pl.pallas_call(second_kernel, out_shape=jax.ShapeDtypeStruct((PEERS, BACK...  2.47 us
    pallas_call x1, Pallas kernels, pack(): pl.pallas_call(pack_kernel, out_shape=(jax.ShapeDtypeStruct((PEERS, CHUNK...  1.69 us
  transfers between devices with their start and end apart: 1, of which 0 were waited for; matrix products, arithmetic and copies ran while one was open for 0% of the time, Pallas kernels for 2%

profile of v4, /device:TPU:1, one launch (start us, length us, event | category | flops | bytes accessed | tf_op | source)
XLA Modules:
  0.0 80.7 jit_solution(926567766735124472)
XLA Ops:
  0.6 1.7 %shard_map.122 = (bf16[64,32,128]{2,1,0:T(8,128)(2,1)S(1)}, bf16[1040,128]{1,0:T(8,128)(2,1)S(1)}) custom-call(bf16[5,5120]{1,0:T(8,128)(2,1)} %k1.1, bf16[5,5120]{1,0:T(8,128)(2,1)} %v1.1, bf16[5,5120]{1,0:T(8,128)(2,1)} %q1.1, bf16[5,5120]{1,0:T(8,128)(2,1)} %q2.1, bf16[5,5120]{1,0:T(8,128)(2,1)} %k2.1, bf16[5,5120]{1,0:T(8,128)(2,1)} %v2.1, ...), custom_call_target="tpu_custom_call" | custom-call | tf_op jit(solution)/shard_map/pallas_call | solution.py:108
  2.3 35.8 %all_to_all.15.messages = bf16[64,32,128]{2,1,0:T(8,128)(2,1)S(1)} all-to-all(bf16[64,32,128]{2,1,0:T(8,128)(2,1)S(1)} %get-tuple-element.9), channel_id=1, replica_groups=mesh['z'=8,'x'=4,'yl'=2,'yh'=4,'c'=2] {'z','yl','yh'}, dimensions={0} | all-to-all | bytes 1048576 | tf_op jit(solution)/shard_map/all_to_all | solution.py:414
  38.1 0.4 shard_map.123
  38.5 11.5 %all_to_all.16.planes = bf16[4,640,128]{2,1,0:T(8,128)(2,1)S(1)} all-to-all(bf16[4,640,128]{2,1,0:T(8,128)(2,1)S(1)} %get-tuple-element.11), channel_id=1, replica_groups=mesh['z'=8,'x'=4,'yl'=2,'yh'=4,'c'=2] {'x'}, dimensions={0} | all-to-all | bytes 1310720 | tf_op jit(solution)/shard_map/all_to_all | solution.py:416
  49.9 0.1 shard_map.124.mine
  50.0 6.3 %collective-permute-start = (bf16[4240,128]{1,0:T(8,128)(2,1)S(1)}, bf16[4240,128]{1,0:T(8,128)(2,1)S(1)}, u32[]{:S(2)}, u32[]{:S(2)}) collective-permute-start(bf16[4240,128]{1,0:T(8,128)(2,1)S(1)} %shard_map.124.mine), channel_id=1, source_target_pairs={{0,1},{1,0},{2,3},{3,2},{4,5},{5,4},{6,7},{7,6},{8,9},{9,8},{10,11... | collective-permute-start | bytes 3256328 | tf_op jit(solution)/shard_map/ppermute | solution.py:418
  57.0 1.6 %shard_map.125 = (f32[640,256]{1,0:T(8,128)S(1)}, f32[640,128]{1,0:T(8,128)S(1)}) custom-call(bf16[640,128]{1,0:T(8,128)(2,1)S(1)} %get-tuple-element.10.queries, bf16[4240,128]{1,0:T(8,128)(2,1)S(1)} %shard_map.124.mine), custom_call_target="tpu_custom_call" | custom-call | flops 524288000 | bytes 1085440 | tf_op jit(solution)/shard_map/pallas_call | solution.py:334
  58.6 0.0 collective-permute-done.theirs
  58.6 2.5 %shard_map.126 = bf16[64,16,128]{2,1,0:T(8,128)(2,1)S(1)} custom-call(s32[1]{0:T(128)S(6)} %copy.13.length, bf16[640,128]{1,0:T(8,128)(2,1)S(1)} %get-tuple-element.10.queries, bf16[4240,128]{1,0:T(8,128)(2,1)S(1)} %shard_map.124.mine, bf16[4240,128]{1,0:T(8,128)(2,1)S(1)} %collective-permute-done.theirs, f32[640,256]{1,0:T(8,128)S(1)} %get-tuple-element.14.sums, ...), custom_call_target="tpu_custom_call" | custom-call | tf_op jit(solution)/shard_map/pallas_call | solution.py:355
  61.1 18.8 %all_to_all.17.messages = bf16[64,16,128]{2,1,0:T(8,128)(2,1)S(1)} all-to-all(bf16[64,16,128]{2,1,0:T(8,128)(2,1)S(1)} %shard_map.126), channel_id=1, replica_groups=mesh['z'=8,'x'=4,'yl'=2,'yh'=4,'c'=2] {'z','yl','yh'}, dimensions={0} | all-to-all | bytes 524288 | tf_op jit(solution)/shard_map/all_to_all | solution.py:421
  79.9 0.7 shard_map.127
Async XLA Ops:
  50.0 8.6 %collective-permute-start = (bf16[4240,128]{1,0:T(8,128)(2,1)S(1)}, bf16[4240,128]{1,0:T(8,128)(2,1)S(1)}, u32[]{:S(2)}, u32[]{:S(2)}) collective-permute-start(bf16[4240,128]{1,0:T(8,128)(2,1)S(1)} %shard_map.124.mine), channel_id=1, source_target_pairs={{0,1},{1,0},{2,3},{3,2},{4,5},{5,4},{6,7},{7,6},{8,9},{9,8},{10,11... | collective-permute-start | bytes 3256328 | tf_op jit(solution)/shard_map/ppermute | solution.py:418

commit v5 on v4

--- a/solution.py
+++ b/solution.py
@@ -16,7 +16,7 @@
 BLOCK_ROWS = 20
 PEERS = 64
 CHUNK = 32
-BACK = 16
+BACK = 2 * ROWS
 TEXT = 512
 EXP_SCALE = float(HEAD_DIM ** (-0.5) * np.log2(np.e))
 
@@ -317,16 +317,14 @@
         start_top,
         finish_tile,
     )
-    row = lax.broadcasted_iota(jnp.int32, (16 * BACK, 80), 0)
-    column = lax.broadcasted_iota(jnp.int32, (16 * BACK, 80), 1)
-    entry = row % BACK
-    begin = (row // BACK) * ROWS
-    place_first = one_hot((column == begin + entry) & (entry < ROWS))
-    place_second = one_hot((column == begin + entry - 8) & (entry >= 8) & (entry < 8 + ROWS))
+    row = lax.broadcasted_iota(jnp.int32, (160, 80), 0)
+    column = lax.broadcasted_iota(jnp.int32, (160, 80), 1)
+    place_first = one_hot(row == 2 * column)
+    place_second = one_hot(row == 2 * column + 1)
     for part in range(4):
-        message = dot_f32(place_first, done[pl.ds(part * 80, 80)])
-        message += dot_f32(place_second, done[pl.ds(PLANE_ROWS + part * 80, 80)])
-        out[pl.ds(part * 16, 16)] = message.astype(jnp.bfloat16).reshape(16, BACK, HEAD_DIM)
+        rows = dot_f32(place_first, done[pl.ds(part * 80, 80)])
+        rows += dot_f32(place_second, done[pl.ds(PLANE_ROWS + part * 80, 80)])
+        out[pl.ds(part * 160, 160)] = rows.astype(jnp.bfloat16)
 
 
 def first_pass(queries, mine):
@@ -354,7 +352,7 @@
     vmem = pl.BlockSpec(memory_space=pltpu.VMEM)
     return pl.pallas_call(
         second_kernel,
-        out_shape=jax.ShapeDtypeStruct((PEERS, BACK, HEAD_DIM), jnp.bfloat16),
+        out_shape=jax.ShapeDtypeStruct((PEERS * BACK, HEAD_DIM), jnp.bfloat16),
         in_specs=[pl.BlockSpec(memory_space=pltpu.SMEM)] + [vmem] * 5,
         out_specs=vmem,
         scratch_shapes=[
@@ -369,12 +367,19 @@
 
 
 def finish_kernel(messages, first, second):
-    for rank in range(ACTIVE):
-        head = (rank % 4) * PAIR_HEADS + rank // 4
-        columns = pl.ds(head * HEAD_DIM, HEAD_DIM)
-        message = messages[rank]
-        first[:, columns] = message[0:ROWS]
-        second[:, columns] = message[8 : 8 + ROWS]
+    source = lax.broadcasted_iota(jnp.int32, (1, 8 * BACK), 1)
+    message = (source * 205) // 2048
+    entry = source - message * BACK
+    target = message * 16 + (entry % 2) * 8 + entry // 2
+    order = one_hot(lax.broadcasted_iota(jnp.int32, (128, 8 * BACK), 0) == target)
+    for part in range(ACTIVE // 8):
+        rows = dot_f32(order, messages[pl.ds(part * 8 * BACK, 8 * BACK)]).astype(jnp.bfloat16)
+        for index in range(8):
+            rank = part * 8 + index
+            head = (rank % 4) * PAIR_HEADS + rank // 4
+            columns = pl.ds(head * HEAD_DIM, HEAD_DIM)
+            first[:, columns] = rows[index * 16 : index * 16 + ROWS]
+            second[:, columns] = rows[index * 16 + 8 : index * 16 + 8 + ROWS]
 
 
 def finish(messages):
@@ -418,8 +423,9 @@
     theirs = lax.ppermute(mine, "c", [(0, 1), (1, 0)])
     sums, tops = first_pass(queries, mine)
     back = second_pass(text_length, queries, mine, theirs, sums, tops)
-    returned = lax.all_to_all(back, PLANE, 0, 0, tiled=True)
-    return finish(returned)
+    pairs = back.reshape(PEERS, ROWS, 2, HEAD_DIM)
+    returned = lax.all_to_all(pairs, PLANE, 0, 0, tiled=True)
+    return finish(returned.reshape(PEERS * BACK, HEAD_DIM))
 
 
 def solution(mesh):

time: 81 us -> 79.3 us (0.979)
  blocking collectives: 66.1 us -> 64.3 us
    all_to_all x1, blocking collectives: 18.8 us -> 17.1 us  [body(): returned = lax.all_to_all(pairs, PLANE, 0, 0, tiled=True)]
where the time goes in v5:
time: 79.3 us; the launch traced here: 79 us
  blocking collectives  64.3 us (81%)
  Pallas kernels  7.02 us (9%)
  starting transfers between devices  6.28 us (8%)
  between operations  1.32 us (2%)
    all_to_all x1, blocking collectives, body(): arrived = lax.all_to_all(sent, PLANE, 0, 0, tiled=True)  35.8 us
    all_to_all x1, blocking collectives, body(): returned = lax.all_to_all(pairs, PLANE, 0, 0, tiled=True)  17.1 us
    all_to_all x1, blocking collectives, body(): planes = lax.all_to_all(copies, 'x', 0, 0, tiled=True)  11.5 us
    ppermute x1, starting transfers between devices, body(): theirs = lax.ppermute(mine, 'c', [(0, 1), (1, 0)])  6.28 us
    pallas_call x1, Pallas kernels, second_pass(): pl.pallas_call(second_kernel, out_shape=jax.ShapeDtypeStruct((PEERS * BAC...  2.39 us
    pallas_call x1, Pallas kernels, pack(): pl.pallas_call(pack_kernel, out_shape=(jax.ShapeDtypeStruct((PEERS, CHUNK...  1.69 us
    pallas_call x1, Pallas kernels, first_pass(): pl.pallas_call(first_kernel, out_shape=(jax.ShapeDtypeStruct((2 * PLANE_R...  1.62 us
  transfers between devices with their start and end apart: 1, of which 0 were waited for; matrix products, arithmetic and copies ran while one was open for 0% of the time, Pallas kernels for 2%

profile of v5, /device:TPU:1, one launch (start us, length us, event | category | flops | bytes accessed | tf_op | source)
XLA Modules:
  0.0 79.0 jit_solution(2933404379031818203)
XLA Ops:
  0.6 1.7 %shard_map.122 = (bf16[64,32,128]{2,1,0:T(8,128)(2,1)S(1)}, bf16[1040,128]{1,0:T(8,128)(2,1)S(1)}) custom-call(bf16[5,5120]{1,0:T(8,128)(2,1)} %k1.1, bf16[5,5120]{1,0:T(8,128)(2,1)} %v1.1, bf16[5,5120]{1,0:T(8,128)(2,1)} %q1.1, bf16[5,5120]{1,0:T(8,128)(2,1)} %q2.1, bf16[5,5120]{1,0:T(8,128)(2,1)} %k2.1, bf16[5,5120]{1,0:T(8,128)(2,1)} %v2.1, ...), custom_call_target="tpu_custom_call" | custom-call | tf_op jit(solution)/shard_map/pallas_call | solution.py:108
  2.3 35.8 %all_to_all.15.messages = bf16[64,32,128]{2,1,0:T(8,128)(2,1)S(1)} all-to-all(bf16[64,32,128]{2,1,0:T(8,128)(2,1)S(1)} %get-tuple-element.9), channel_id=1, replica_groups=mesh['z'=8,'x'=4,'yl'=2,'yh'=4,'c'=2] {'z','yl','yh'}, dimensions={0} | all-to-all | bytes 1048576 | tf_op jit(solution)/shard_map/all_to_all | solution.py:419
  38.1 0.4 shard_map.123
  38.5 11.5 %all_to_all.16.planes = bf16[4,640,128]{2,1,0:T(8,128)(2,1)S(1)} all-to-all(bf16[4,640,128]{2,1,0:T(8,128)(2,1)S(1)} %get-tuple-element.11), channel_id=1, replica_groups=mesh['z'=8,'x'=4,'yl'=2,'yh'=4,'c'=2] {'x'}, dimensions={0} | all-to-all | bytes 1310720 | tf_op jit(solution)/shard_map/all_to_all | solution.py:421
  49.9 0.1 shard_map.124.mine
  50.0 6.3 %collective-permute-start = (bf16[4240,128]{1,0:T(8,128)(2,1)S(1)}, bf16[4240,128]{1,0:T(8,128)(2,1)S(1)}, u32[]{:S(2)}, u32[]{:S(2)}) collective-permute-start(bf16[4240,128]{1,0:T(8,128)(2,1)S(1)} %shard_map.124.mine), channel_id=1, source_target_pairs={{0,1},{1,0},{2,3},{3,2},{4,5},{5,4},{6,7},{7,6},{8,9},{9,8},{10,11... | collective-permute-start | bytes 3256328 | tf_op jit(solution)/shard_map/ppermute | solution.py:423
  57.0 1.6 %shard_map.125 = (f32[640,256]{1,0:T(8,128)S(1)}, f32[640,128]{1,0:T(8,128)S(1)}) custom-call(bf16[640,128]{1,0:T(8,128)(2,1)S(1)} %get-tuple-element.10.queries, bf16[4240,128]{1,0:T(8,128)(2,1)S(1)} %shard_map.124.mine), custom_call_target="tpu_custom_call" | custom-call | flops 524288000 | bytes 1085440 | tf_op jit(solution)/shard_map/pallas_call | solution.py:332
  58.6 0.0 collective-permute-done.theirs
  58.6 2.4 %shard_map.126 = bf16[640,128]{1,0:T(8,128)(2,1)S(1)} custom-call(s32[1]{0:T(128)S(6)} %copy.13.length, bf16[640,128]{1,0:T(8,128)(2,1)S(1)} %get-tuple-element.10.queries, bf16[4240,128]{1,0:T(8,128)(2,1)S(1)} %shard_map.124.mine, bf16[4240,128]{1,0:T(8,128)(2,1)S(1)} %collective-permute-done.theirs, f32[640,256]{1,0:T(8,128)S(1)} %get-tuple-element.14.sums, ...), custom_call_target="tpu_custom_call" | custom-call | tf_op jit(solution)/shard_map/pallas_call | solution.py:353
  61.0 17.1 %all_to_all.17 = bf16[64,5,2,128]{3,2,1,0:T(2,128)(2,1)S(1)} all-to-all(bf16[64,5,2,128]{3,2,1,0:T(2,128)(2,1)S(1)} %bitcast.2), channel_id=1, replica_groups=mesh['z'=8,'x'=4,'yl'=2,'yh'=4,'c'=2] {'z','yl','yh'}, dimensions={0} | all-to-all | bytes 327680 | tf_op jit(solution)/shard_map/all_to_all | solution.py:427
  78.1 0.9 %shard_map.127 = (bf16[5,5120]{1,0:T(8,128)(2,1)}, bf16[5,5120]{1,0:T(8,128)(2,1)}) custom-call(bf16[640,128]{1,0:T(8,128)(2,1)S(1)} %bitcast.3), custom_call_target="tpu_custom_call" | custom-call | tf_op jit(solution)/shard_map/pallas_call | solution.py:387
Async XLA Ops:
  50.0 8.6 %collective-permute-start = (bf16[4240,128]{1,0:T(8,128)(2,1)S(1)}, bf16[4240,128]{1,0:T(8,128)(2,1)S(1)}, u32[]{:S(2)}, u32[]{:S(2)}) collective-permute-start(bf16[4240,128]{1,0:T(8,128)(2,1)S(1)} %shard_map.124.mine), channel_id=1, source_target_pairs={{0,1},{1,0},{2,3},{3,2},{4,5},{5,4},{6,7},{7,6},{8,9},{9,8},{10,11... | collective-permute-start | bytes 3256328 | tf_op jit(solution)/shard_map/ppermute | solution.py:423

commit v6 on v5

--- a/solution.py
+++ b/solution.py
@@ -15,7 +15,7 @@
 PLANE_ROWS = 320
 BLOCK_ROWS = 20
 PEERS = 64
-CHUNK = 32
+CHUNK = 6 * ROWS
 BACK = 2 * ROWS
 TEXT = 512
 EXP_SCALE = float(HEAD_DIM ** (-0.5) * np.log2(np.e))
@@ -58,8 +58,13 @@
     return jnp.where(condition, 1.0, 0.0).astype(jnp.bfloat16)
 
 
+def message_of(source, rows):
+    return (source * (65536 // rows + 1)) // 65536
+
+
 def pack_kernel(
-    k1, v1, q1, q2, k2, v2, text_k, text_v, gates, steps, out, extra, held, gate, step_ids, sems
+    k1, v1, q1, q2, k2, v2, text_k, text_v, gates, steps, out, extra,
+    held, stacked, gate, step_ids, sems,
 ):
     slot = lax.rem(head_slot(), GROUP_HEADS)
     columns = pl.ds(pl.multiple_of(slot * HEAD_DIM, HEAD_DIM), HEAD_DIM)
@@ -76,20 +81,26 @@
     ]
     for fetch in fetches:
         fetch.start()
-    total = None
+    stacked[...] = jnp.zeros_like(stacked)
     for index in range(6):
-        row = lax.broadcasted_iota(jnp.int32, (CHUNK, ROWS), 0)
-        column = lax.broadcasted_iota(jnp.int32, (CHUNK, ROWS), 1)
         fetches[index].wait()
-        part = dot_f32(one_hot(row == column + index * ROWS), held[index])
-        total = part if total is None else total + part
-    packed = total.astype(jnp.bfloat16)
-    for rank in range(PEERS):
-        if rank < ACTIVE:
+        stacked[pl.ds(index * 8, ROWS)] = held[index]
+    source = lax.broadcasted_iota(jnp.int32, (1, 8 * 48), 1)
+    message = message_of(source, 48)
+    array = (source - message * 48) // 8
+    entry = source - message * 48 - array * 8
+    target = jnp.where(entry < ROWS, message * CHUNK + array * ROWS + entry, -1)
+    order = one_hot(lax.broadcasted_iota(jnp.int32, (8 * CHUNK, 8 * 48), 0) == target)
+    for part in range(PEERS // 8):
+        place = pl.ds(part * 8 * CHUNK, 8 * CHUNK)
+        if part * 8 >= ACTIVE:
+            out[place] = jnp.zeros((8 * CHUNK, HEAD_DIM), jnp.bfloat16)
+            continue
+        pieces = []
+        for rank in range(part * 8, part * 8 + 8):
             head = (rank % 4) * PAIR_HEADS + rank // 4
-            out[rank] = packed[:, head * HEAD_DIM : (head + 1) * HEAD_DIM]
-        else:
-            out[rank] = jnp.zeros((CHUNK, HEAD_DIM), jnp.bfloat16)
+            pieces.append(stacked[:, head * HEAD_DIM : (head + 1) * HEAD_DIM])
+        out[place] = dot_f32(order, jnp.concatenate(pieces, axis=0)).astype(jnp.bfloat16)
     for fetch in fetches[6:]:
         fetch.wait()
     row = lax.broadcasted_iota(jnp.int32, (16, HEAD_DIM), 0)
@@ -108,13 +119,14 @@
     return pl.pallas_call(
         pack_kernel,
         out_shape=(
-            jax.ShapeDtypeStruct((PEERS, CHUNK, HEAD_DIM), jnp.bfloat16),
+            jax.ShapeDtypeStruct((PEERS * CHUNK, HEAD_DIM), jnp.bfloat16),
             jax.ShapeDtypeStruct((EXTRA, HEAD_DIM), jnp.bfloat16),
         ),
         in_specs=[pl.BlockSpec(memory_space=pltpu.HBM)] * 10,
         out_specs=(vmem, vmem),
         scratch_shapes=[
             pltpu.VMEM((6, ROWS, HEADS * HEAD_DIM), jnp.bfloat16),
+            pltpu.VMEM((48, HEADS * HEAD_DIM), jnp.bfloat16),
             pltpu.VMEM((35, HEAD_DIM), jnp.float32),
             pltpu.SMEM((2,), jnp.int32),
             pltpu.SemaphoreType.DMA((10,)),
@@ -124,12 +136,13 @@
 
 
 def unpack_kernel(messages, copies, queries, near):
-    source = lax.broadcasted_iota(jnp.int32, (1, 256), 1)
-    message, entry = source // CHUNK, source % CHUNK
+    source = lax.broadcasted_iota(jnp.int32, (1, 8 * CHUNK), 1)
+    message = message_of(source, CHUNK)
+    entry = source - message * CHUNK
     target = entry + ((entry * 13) // 64) * 35 + message * ROWS
-    order = one_hot(lax.broadcasted_iota(jnp.int32, (240, 256), 0) == target)
+    order = one_hot(lax.broadcasted_iota(jnp.int32, (240, 8 * CHUNK), 0) == target)
     for step in range(8):
-        rows = messages[pl.ds(step * 8, 8)].reshape(256, HEAD_DIM)
+        rows = messages[pl.ds(step * 8 * CHUNK, 8 * CHUNK)]
         ordered = dot_f32(order, rows).astype(jnp.bfloat16)
         for array in range(6):
             piece = ordered[array * 40 : (array + 1) * 40]
@@ -368,7 +381,7 @@
 
 def finish_kernel(messages, first, second):
     source = lax.broadcasted_iota(jnp.int32, (1, 8 * BACK), 1)
-    message = (source * 205) // 2048
+    message = message_of(source, BACK)
     entry = source - message * BACK
     target = message * 16 + (entry % 2) * 8 + entry // 2
     order = one_hot(lax.broadcasted_iota(jnp.int32, (128, 8 * BACK), 0) == target)
@@ -416,8 +429,9 @@
         gate_table,
         timesteps,
     )
-    arrived = lax.all_to_all(sent, PLANE, 0, 0, tiled=True)
-    copies, queries, near = unpack(arrived)
+    pairs = sent.reshape(PEERS, CHUNK // 2, 2, HEAD_DIM)
+    arrived = lax.all_to_all(pairs, PLANE, 0, 0, tiled=True)
+    copies, queries, near = unpack(arrived.reshape(PEERS * CHUNK, HEAD_DIM))
     planes = lax.all_to_all(copies, "x", 0, 0, tiled=True)
     mine = join(planes, near, extra)
     theirs = lax.ppermute(mine, "c", [(0, 1), (1, 0)])

time: 79.3 us -> 78.7 us (level)
  no operation moved by 1% of the time
where the time goes in v6:
time: 78.7 us; the launch traced here: 78.4 us
  blocking collectives  63.7 us (81%)
  Pallas kernels  7.04 us (9%)
  starting transfers between devices  6.36 us (8%)
  between operations  1.32 us (2%)
    all_to_all x1, blocking collectives, body(): arrived = lax.all_to_all(pairs, PLANE, 0, 0, tiled=True)  35 us
    all_to_all x1, blocking collectives, body(): returned = lax.all_to_all(pairs, PLANE, 0, 0, tiled=True)  17.2 us
    all_to_all x1, blocking collectives, body(): planes = lax.all_to_all(copies, 'x', 0, 0, tiled=True)  11.5 us
    ppermute x1, starting transfers between devices, body(): theirs = lax.ppermute(mine, 'c', [(0, 1), (1, 0)])  6.36 us
    pallas_call x1, Pallas kernels, second_pass(): pl.pallas_call(second_kernel, out_shape=jax.ShapeDtypeStruct((PEERS * BAC...  2.38 us
    pallas_call x1, Pallas kernels, pack(): pl.pallas_call(pack_kernel, out_shape=(jax.ShapeDtypeStruct((PEERS * CHUN...  1.71 us
    pallas_call x1, Pallas kernels, first_pass(): pl.pallas_call(first_kernel, out_shape=(jax.ShapeDtypeStruct((2 * PLANE_R...  1.62 us
  transfers between devices with their start and end apart: 1, of which 0 were waited for; matrix products, arithmetic and copies ran while one was open for 0% of the time, Pallas kernels for 2%

profile of v6, /device:TPU:1, one launch (start us, length us, event | category | flops | bytes accessed | tf_op | source)
XLA Modules:
  0.0 78.4 jit_solution(12077386373725983356)
XLA Ops:
  0.6 1.7 %shard_map.122 = (bf16[1920,128]{1,0:T(8,128)(2,1)S(1)}, bf16[1040,128]{1,0:T(8,128)(2,1)S(1)}) custom-call(bf16[5,5120]{1,0:T(8,128)(2,1)} %k1.1, bf16[5,5120]{1,0:T(8,128)(2,1)} %v1.1, bf16[5,5120]{1,0:T(8,128)(2,1)} %q1.1, bf16[5,5120]{1,0:T(8,128)(2,1)} %q2.1, bf16[5,5120]{1,0:T(8,128)(2,1)} %k2.1, bf16[5,5120]{1,0:T(8,128)(2,1)} %v2.1, ...), custom_call_target="tpu_custom_call" | custom-call | tf_op jit(solution)/shard_map/pallas_call | solution.py:119
  2.4 35.0 %all_to_all.15 = bf16[64,15,2,128]{3,2,1,0:T(2,128)(2,1)S(1)} all-to-all(bf16[64,15,2,128]{3,2,1,0:T(2,128)(2,1)S(1)} %bitcast.7), channel_id=1, replica_groups=mesh['z'=8,'x'=4,'yl'=2,'yh'=4,'c'=2] {'z','yl','yh'}, dimensions={0} | all-to-all | bytes 983040 | tf_op jit(solution)/shard_map/all_to_all | solution.py:433
  37.3 0.4 shard_map.123
  37.7 11.5 %all_to_all.16.planes = bf16[4,640,128]{2,1,0:T(8,128)(2,1)S(1)} all-to-all(bf16[4,640,128]{2,1,0:T(8,128)(2,1)S(1)} %get-tuple-element.11), channel_id=1, replica_groups=mesh['z'=8,'x'=4,'yl'=2,'yh'=4,'c'=2] {'x'}, dimensions={0} | all-to-all | bytes 1310720 | tf_op jit(solution)/shard_map/all_to_all | solution.py:435
  49.2 0.1 shard_map.124.mine
  49.3 6.4 %collective-permute-start = (bf16[4240,128]{1,0:T(8,128)(2,1)S(1)}, bf16[4240,128]{1,0:T(8,128)(2,1)S(1)}, u32[]{:S(2)}, u32[]{:S(2)}) collective-permute-start(bf16[4240,128]{1,0:T(8,128)(2,1)S(1)} %shard_map.124.mine), channel_id=1, source_target_pairs={{0,1},{1,0},{2,3},{3,2},{4,5},{5,4},{6,7},{7,6},{8,9},{9,8},{10,11... | collective-permute-start | bytes 3256328 | tf_op jit(solution)/shard_map/ppermute | solution.py:437
  56.3 1.6 %shard_map.125 = (f32[640,256]{1,0:T(8,128)S(1)}, f32[640,128]{1,0:T(8,128)S(1)}) custom-call(bf16[640,128]{1,0:T(8,128)(2,1)S(1)} %get-tuple-element.10.queries, bf16[4240,128]{1,0:T(8,128)(2,1)S(1)} %shard_map.124.mine), custom_call_target="tpu_custom_call" | custom-call | flops 524288000 | bytes 1085440 | tf_op jit(solution)/shard_map/pallas_call | solution.py:345
  57.9 0.0 collective-permute-done.theirs
  58.0 2.4 %shard_map.126 = bf16[640,128]{1,0:T(8,128)(2,1)S(1)} custom-call(s32[1]{0:T(128)S(6)} %copy.13.length, bf16[640,128]{1,0:T(8,128)(2,1)S(1)} %get-tuple-element.10.queries, bf16[4240,128]{1,0:T(8,128)(2,1)S(1)} %shard_map.124.mine, bf16[4240,128]{1,0:T(8,128)(2,1)S(1)} %collective-permute-done.theirs, f32[640,256]{1,0:T(8,128)S(1)} %get-tuple-element.14.sums, ...), custom_call_target="tpu_custom_call" | custom-call | tf_op jit(solution)/shard_map/pallas_call | solution.py:366
  60.4 17.2 %all_to_all.17 = bf16[64,5,2,128]{3,2,1,0:T(2,128)(2,1)S(1)} all-to-all(bf16[64,5,2,128]{3,2,1,0:T(2,128)(2,1)S(1)} %bitcast.5), channel_id=1, replica_groups=mesh['z'=8,'x'=4,'yl'=2,'yh'=4,'c'=2] {'z','yl','yh'}, dimensions={0} | all-to-all | bytes 327680 | tf_op jit(solution)/shard_map/all_to_all | solution.py:441
  77.6 0.9 %shard_map.127 = (bf16[5,5120]{1,0:T(8,128)(2,1)}, bf16[5,5120]{1,0:T(8,128)(2,1)}) custom-call(bf16[640,128]{1,0:T(8,128)(2,1)S(1)} %bitcast.6), custom_call_target="tpu_custom_call" | custom-call | tf_op jit(solution)/shard_map/pallas_call | solution.py:400
Async XLA Ops:
  49.3 8.7 %collective-permute-start = (bf16[4240,128]{1,0:T(8,128)(2,1)S(1)}, bf16[4240,128]{1,0:T(8,128)(2,1)S(1)}, u32[]{:S(2)}, u32[]{:S(2)}) collective-permute-start(bf16[4240,128]{1,0:T(8,128)(2,1)S(1)} %shard_map.124.mine), channel_id=1, source_target_pairs={{0,1},{1,0},{2,3},{3,2},{4,5},{5,4},{6,7},{7,6},{8,9},{9,8},{10,11... | collective-permute-start | bytes 3256328 | tf_op jit(solution)/shard_map/ppermute | solution.py:437

commit v7 on v6

v7 whole, which is shorter than its diff:
```python
import jax
import jax.numpy as jnp
import numpy as np
from jax import lax
from jax.experimental import pallas as pl
from jax.experimental.pallas import tpu as pltpu
from jax.sharding import Mesh
from jax.sharding import PartitionSpec as P

HEAD_DIM = 128
HEADS = 40
GROUP_HEADS = 5
PAIR_HEADS = 10
ROWS = 5
PLANE_ROWS = 320
BLOCK_ROWS = 20
PEERS = 64
CHUNK = 6 * ROWS
BACK = 2 * ROWS
TEXT = 512
EXP_SCALE = float(HEAD_DIM ** (-0.5) * np.log2(np.e))

AXES = ("z", "x", "yl", "yh", "c")
PLANE = ("z", "yl", "yh")
ACTIVE = 4 * PAIR_HEADS

EARLY_VALUES_AT = 2 * PLANE_ROWS
TEXT_AT = 2 * EARLY_VALUES_AT
EXTRA = 2 * TEXT + 16
EARLY = TEXT_AT + EXTRA
FAR = 3 * PLANE_ROWS
FAR_KEYS = 1024
LATE = FAR_KEYS + FAR

VMEM_LIMIT = 24 * 1024 * 1024


def dot_f32(left, right):
    return lax.dot_general(
        left, right, (((1,), (0,)), ((), ())), preferred_element_type=jnp.float32
    )


def dot_t_f32(left, right):
    return lax.dot_general(
        left, right, (((1,), (1,)), ((), ())), preferred_element_type=jnp.float32
    )


def head_slot():
    return lax.axis_index("z") * 2 + lax.axis_index("yl")


def in_hbm(array):
    return pltpu.with_memory_space_constraint(array, pltpu.HBM)


def one_hot(condition):
    return jnp.where(condition, 1.0, 0.0).astype(jnp.bfloat16)


def message_of(source, rows):
    return (source * (65536 // rows + 1)) // 65536


def pack_kernel(k1, v1, q1, q2, k2, v2, out, held, stacked, ready, fetch_sems, send_sems):
    fetches = [
        pltpu.make_async_copy(array, held.at[index], fetch_sems.at[index])
        for index, array in enumerate((k1, v1, q1, q2, k2, v2))
    ]
    for fetch in fetches:
        fetch.start()
    blank = pl.ds(ACTIVE * CHUNK, (PEERS - ACTIVE) * CHUNK)
    places = [pl.ds(part * 8 * CHUNK, 8 * CHUNK) for part in range(ACTIVE // 8)] + [blank]
    sends = [
        pltpu.make_async_copy(ready.at[place], out.at[place], send_sems.at[index])
        for index, place in enumerate(places)
    ]
    ready[blank] = jnp.zeros(((PEERS - ACTIVE) * CHUNK, HEAD_DIM), jnp.bfloat16)
    sends[-1].start()
    stacked[...] = jnp.zeros_like(stacked)
    for index in range(6):
        fetches[index].wait()
        stacked[pl.ds(index * 8, ROWS)] = held[index]
    source = lax.broadcasted_iota(jnp.int32, (1, 8 * 48), 1)
    message = message_of(source, 48)
    array = (source - message * 48) // 8
    entry = source - message * 48 - array * 8
    target = jnp.where(entry < ROWS, message * CHUNK + array * ROWS + entry, -1)
    order = one_hot(lax.broadcasted_iota(jnp.int32, (8 * CHUNK, 8 * 48), 0) == target)
    for part in range(ACTIVE // 8):
        pieces = []
        for rank in range(part * 8, part * 8 + 8):
            head = (rank % 4) * PAIR_HEADS + rank // 4
            pieces.append(stacked[:, head * HEAD_DIM : (head + 1) * HEAD_DIM])
        rows = dot_f32(order, jnp.concatenate(pieces, axis=0))
        ready[places[part]] = rows.astype(jnp.bfloat16)
        sends[part].start()
    for send in sends:
        send.wait()


def pack(*arrays):
    hbm = pl.BlockSpec(memory_space=pltpu.HBM)
    return pl.pallas_call(
        pack_kernel,
        out_shape=jax.ShapeDtypeStruct((PEERS * CHUNK, HEAD_DIM), jnp.bfloat16),
        in_specs=[hbm] * 6,
        out_specs=hbm,
        scratch_shapes=[
            pltpu.VMEM((6, ROWS, HEADS * HEAD_DIM), jnp.bfloat16),
            pltpu.VMEM((48, HEADS * HEAD_DIM), jnp.bfloat16),
            pltpu.VMEM((PEERS * CHUNK, HEAD_DIM), jnp.bfloat16),
            pltpu.SemaphoreType.DMA((6,)),
            pltpu.SemaphoreType.DMA((ACTIVE // 8 + 1,)),
        ],
        compiler_params=pltpu.CompilerParams(vmem_limit_bytes=VMEM_LIMIT),
    )(*[in_hbm(array) for array in arrays])


def prepare_kernel(length, steps, text_k, text_v, gates, extra, dead, order, gate, sems):
    slot = lax.rem(head_slot(), GROUP_HEADS)
    columns = pl.ds(pl.multiple_of(slot * HEAD_DIM, HEAD_DIM), HEAD_DIM)
    fetches = [
        pltpu.make_async_copy(text_k.at[:, columns], extra.at[pl.ds(0, TEXT)], sems.at[0]),
        pltpu.make_async_copy(text_v.at[:, columns], extra.at[pl.ds(TEXT, TEXT)], sems.at[1]),
        pltpu.make_async_copy(gates.at[:, columns], gate, sems.at[2]),
    ]
    for fetch in fetches:
        fetch.start()
    source = lax.broadcasted_iota(jnp.int32, (1, 8 * CHUNK), 1)
    message = message_of(source, CHUNK)
    entry = source - message * CHUNK
    target = entry + ((entry * 13) // 64) * 35 + message * ROWS
    order[...] = one_hot(lax.broadcasted_iota(jnp.int32, (240, 8 * CHUNK), 0) == target)
    slots = lax.broadcasted_iota(jnp.int32, (8, TEXT), 1)
    dead[...] = jnp.where(slots < length[0], 0.0, 1.0)
    for fetch in fetches:
        fetch.wait()
    row = lax.broadcasted_iota(jnp.int32, (16, HEAD_DIM), 0)
    parts = jnp.zeros((16, HEAD_DIM), jnp.float32)
    for step in range(2):
        left = gate[pl.ds(steps[step], 1), :]
        for index in range(3):
            part = left.astype(jnp.bfloat16).astype(jnp.float32)
            parts = jnp.where(row == step * 3 + index, part, parts)
            left = left - part
    extra[pl.ds(2 * TEXT, 16)] = parts.astype(jnp.bfloat16)


def prepare(text_length, timesteps, text_keys, text_values, gate_table):
    smem = pl.BlockSpec(memory_space=pltpu.SMEM)
    hbm = pl.BlockSpec(memory_space=pltpu.HBM)
    vmem = pl.BlockSpec(memory_space=pltpu.VMEM)
    return pl.pallas_call(
        prepare_kernel,
        out_shape=(
            jax.ShapeDtypeStruct((EXTRA, HEAD_DIM), jnp.bfloat16),
            jax.ShapeDtypeStruct((8, TEXT), jnp.float32),
            jax.ShapeDtypeStruct((240, 8 * CHUNK), jnp.bfloat16),
        ),
        in_specs=[smem, smem, hbm, hbm, hbm],
        out_specs=(vmem, vmem, vmem),
        scratch_shapes=[
            pltpu.VMEM((35, HEAD_DIM), jnp.float32),
            pltpu.SemaphoreType.DMA((3,)),
        ],
        compiler_params=pltpu.CompilerParams(vmem_limit_bytes=VMEM_LIMIT),
    )(text_length, timesteps, in_hbm(text_keys), in_hbm(text_values), in_hbm(gate_table))


def unpack_kernel(messages, extra, order, copies, queries, early, plane, sems):
    def ordered(step, first, last):
        rows = messages[pl.ds(step * 8 * CHUNK, 8 * CHUNK)]
        result = dot_f32(order[pl.ds(first * 40, (last - first) * 40)], rows)
        return result.astype(jnp.bfloat16)

    for step in range(8):
        result = ordered(step, 0, 2)
        for array in range(2):
            piece = result[array * 40 : (array + 1) * 40]
            plane[pl.ds(array * PLANE_ROWS + step * 40, 40)] = piece
            early[pl.ds(array * EARLY_VALUES_AT + step * 40, 40)] = piece
    sends = [pltpu.make_async_copy(plane, copies.at[copy], sems.at[copy]) for copy in range(4)]
    for send in sends:
        send.start()
    for step in range(8):
        result = ordered(step, 2, 6)
        for array in range(4):
            piece = result[array * 40 : (array + 1) * 40]
            if array < 2:
                queries[pl.ds(array * PLANE_ROWS + step * 40, 40)] = piece
            else:
                begin = (array - 2) * EARLY_VALUES_AT + PLANE_ROWS
                early[pl.ds(begin + step * 40, 40)] = piece
    early[pl.ds(TEXT_AT, EXTRA)] = extra[...]
    for send in sends:
        send.wait()


def unpack(messages, extra, order):
    vmem = pl.BlockSpec(memory_space=pltpu.VMEM)
    return pl.pallas_call(
        unpack_kernel,
        out_shape=(
            jax.ShapeDtypeStruct((4, 2 * PLANE_ROWS, HEAD_DIM), jnp.bfloat16),
            jax.ShapeDtypeStruct((2 * PLANE_ROWS, HEAD_DIM), jnp.bfloat16),
            jax.ShapeDtypeStruct((EARLY, HEAD_DIM), jnp.bfloat16),
        ),
        in_specs=[vmem] * 3,
        out_specs=(pl.BlockSpec(memory_space=pltpu.HBM), vmem, vmem),
        scratch_shapes=[
            pltpu.VMEM((2 * PLANE_ROWS, HEAD_DIM), jnp.bfloat16),
            pltpu.SemaphoreType.DMA((4,)),
        ],
        compiler_params=pltpu.CompilerParams(vmem_limit_bytes=VMEM_LIMIT),
    )(messages, extra, order)


def join_kernel(planes, behind, out):
    del behind
    own = lax.axis_index("x")
    for place in range(3):
        source = lax.rem(own + place + 1, 4)
        for part in range(2):
            out[pl.ds(part * FAR_KEYS + place * PLANE_ROWS, PLANE_ROWS)] = planes[
                source, pl.ds(part * PLANE_ROWS, PLANE_ROWS)
            ]
    out[pl.ds(FAR, FAR_KEYS - FAR)] = planes[lax.rem(own + 1, 4), pl.ds(0, FAR_KEYS - FAR)]


def join(planes, behind):
    return pl.pallas_call(
        join_kernel,
        out_shape=jax.ShapeDtypeStruct((LATE, HEAD_DIM), jnp.bfloat16),
        compiler_params=pltpu.CompilerParams(vmem_limit_bytes=VMEM_LIMIT),
    )(planes, behind)


TILE = 160
TILES = 2 * PLANE_ROWS // TILE


def block_of(index):
    return jnp.floor((index.astype(jnp.float32) + 0.5) * (1.0 / BLOCK_ROWS))


def beside_ones(target, rows):
    target[:, :HEAD_DIM] = rows
    target[:, HEAD_DIM:] = jnp.ones_like(rows)


def tile_rows(tile):
    return pl.ds(tile * TILE, TILE)


class OwnPart:
    def __init__(self, queries, early, values):
        self.queries, self.early, self.values = queries, early, values
        beside_ones(values, early[pl.ds(EARLY_VALUES_AT, 2 * PLANE_ROWS)])

    def width(self, tile):
        return 384 if tile * TILE < PLANE_ROWS else 2 * PLANE_ROWS

    def scores(self, tile):
        width = self.width(tile)
        scores = dot_t_f32(self.queries[tile_rows(tile)], self.early[pl.ds(0, width)])
        column = lax.broadcasted_iota(jnp.int32, (1, width), 1)
        first = column < PLANE_ROWS
        if tile * TILE < PLANE_ROWS:
            return jnp.where(first, scores, -1e30)
        row = lax.broadcasted_iota(jnp.int32, (TILE, 1), 0) + (tile * TILE) % PLANE_ROWS
        same = block_of(row) == block_of(jnp.where(first, column, column - PLANE_ROWS))
        return jnp.where(jnp.logical_xor(same, first), scores, -1e30)

    def sums(self, weights, tile):
        return dot_f32(weights, self.values[pl.ds(0, self.width(tile))])


class TextPart:
    def __init__(self, queries, dead, text, values):
        self.queries, self.dead, self.text, self.values = queries, dead, text, values
        beside_ones(values, text[pl.ds(TEXT, TEXT)])

    def scores(self, tile):
        scores = dot_t_f32(self.queries[tile_rows(tile)], self.text[pl.ds(0, TEXT)])
        return jnp.where(self.dead[0:1] == 0.0, scores, -1e30)

    def sums(self, weights, tile):
        return dot_f32(weights, self.values[...])


class FarPart:
    def __init__(self, queries, late, values, half):
        self.queries, self.late, self.values = queries, late, values
        self.place = pl.ds(half * (FAR_KEYS // 2), FAR_KEYS // 2)
        if half == 0:
            beside_ones(values.at[pl.ds(0, FAR)], late[pl.ds(FAR_KEYS, FAR)])
            rest = FAR_KEYS - FAR
            values[pl.ds(FAR, rest)] = jnp.zeros((rest, 2 * HEAD_DIM), jnp.bfloat16)

    def scores(self, tile):
        return dot_t_f32(self.queries[tile_rows(tile)], self.late[self.place])

    def sums(self, weights, tile):
        return dot_f32(weights, self.values[self.place])


def lane_max(scores, former):
    for begin in range(0, scores.shape[1], HEAD_DIM):
        piece = scores[:, begin : begin + HEAD_DIM]
        former = piece if former is None else jnp.maximum(former, piece)
    return former


def weigh(scores, top):
    return jnp.exp2((scores - top) * EXP_SCALE).astype(jnp.bfloat16)


def run_tiles(parts, before, finish_tile):
    former = None
    for tile in range(TILES + 1):
        scores, lanes, sums = [], None, None
        for index, part in enumerate(parts):
            if tile < TILES:
                scores.append(part.scores(tile))
                lanes = lane_max(scores[-1], lanes)
            if former is not None:
                fresh = part.sums(weigh(former[0][index], former[1]), tile - 1)
                sums = fresh if sums is None else sums + fresh
        if former is not None:
            top = former[1]
            if before is not None:
                scale = jnp.exp2((before[1][tile_rows(tile - 1), 0:1] - top) * EXP_SCALE)
                sums = sums + before[0][tile_rows(tile - 1)] * scale
            finish_tile(tile - 1, top, sums)
        if tile < TILES:
            top = jnp.max(lanes, axis=1, keepdims=True)
            if before is not None:
                top = jnp.maximum(before[1][tile_rows(tile), 0:1], top)
            former = (scores, top)


def keep(sums, tops):
    def finish_tile(tile, top, total):
        sums[tile_rows(tile)] = total
        tops[tile_rows(tile)] = jnp.broadcast_to(top, (TILE, HEAD_DIM))

    return finish_tile


STATE = (
    jax.ShapeDtypeStruct((2 * PLANE_ROWS, 2 * HEAD_DIM), jnp.float32),
    jax.ShapeDtypeStruct((2 * PLANE_ROWS, HEAD_DIM), jnp.float32),
)


def values_scratch(rows):
    return pltpu.VMEM((rows, 2 * HEAD_DIM), jnp.bfloat16)


def mine_kernel(queries, early, sums, tops, values):
    run_tiles([OwnPart(queries, early, values)], None, keep(sums, tops))


def mine_pass(queries, early):
    return pl.pallas_call(
        mine_kernel,
        out_shape=STATE,
        scratch_shapes=[values_scratch(2 * PLANE_ROWS)],
        cost_estimate=pl.CostEstimate(flops=8 * 10**9, bytes_accessed=0, transcendentals=0),
        compiler_params=pltpu.CompilerParams(vmem_limit_bytes=VMEM_LIMIT),
    )(queries, early)


def theirs_kernel(
    dead, queries, mine, theirs, sums, tops, new_sums, new_tops, gate, values, text, text_values
):
    here = head_slot() // GROUP_HEADS == lax.axis_index("c")

    @pl.when(here)
    def _():
        text[...] = mine[pl.ds(TEXT_AT, EXTRA)]

    @pl.when(jnp.logical_not(here))
    def _():
        text[...] = theirs[pl.ds(TEXT_AT, EXTRA)]

    parts = text[pl.ds(2 * TEXT, 16)].astype(jnp.float32)
    for step in range(2):
        row = parts[3 * step : 3 * step + 1] + parts[3 * step + 1 : 3 * step + 2]
        gate[pl.ds(step, 1)] = row + parts[3 * step + 2 : 3 * step + 3]
    run_tiles(
        [OwnPart(queries, theirs, values), TextPart(queries, dead, text, text_values)],
        (sums, tops),
        keep(new_sums, new_tops),
    )


def theirs_pass(dead, queries, mine, theirs, sums, tops):
    vmem = pl.BlockSpec(memory_space=pltpu.VMEM)
    return pl.pallas_call(
        theirs_kernel,
        out_shape=STATE + (jax.ShapeDtypeStruct((2, HEAD_DIM), jnp.float32),),
        in_specs=[vmem] * 6,
        out_specs=(vmem, vmem, vmem),
        scratch_shapes=[
            values_scratch(2 * PLANE_ROWS),
            pltpu.VMEM((EXTRA, HEAD_DIM), jnp.bfloat16),
            values_scratch(TEXT),
        ],
        compiler_params=pltpu.CompilerParams(vmem_limit_bytes=VMEM_LIMIT),
    )(dead, queries, mine, theirs, sums, tops)


def far_parts(queries, late, values):
    return [FarPart(queries, late, values, half) for half in range(2)]


def far_kernel(queries, late, sums, tops, new_sums, new_tops, values):
    run_tiles(far_parts(queries, late, values), (sums, tops), keep(new_sums, new_tops))


def far_pass(queries, late, sums, tops):
    return pl.pallas_call(
        far_kernel,
        out_shape=STATE,
        scratch_shapes=[values_scratch(FAR_KEYS)],
        compiler_params=pltpu.CompilerParams(vmem_limit_bytes=VMEM_LIMIT),
    )(queries, late, sums, tops)


def last_kernel(queries, late, sums, tops, gate, out, values, done):
    def finish_tile(tile, top, total):
        step = tile * TILE // PLANE_ROWS
        attended = total[:, :HEAD_DIM] / total[:, HEAD_DIM:]
        done[tile_rows(tile)] = (gate[pl.ds(step, 1)] * attended).astype(jnp.bfloat16)

    run_tiles(far_parts(queries, late, values), (sums, tops), finish_tile)
    row = lax.broadcasted_iota(jnp.int32, (160, 80), 0)
    column = lax.broadcasted_iota(jnp.int32, (160, 80), 1)
    place_first = one_hot(row == 2 * column)
    place_second = one_hot(row == 2 * column + 1)
    for part in range(4):
        rows = dot_f32(place_first, done[pl.ds(part * 80, 80)])
        rows += dot_f32(place_second, done[pl.ds(PLANE_ROWS + part * 80, 80)])
        out[pl.ds(part * 160, 160)] = rows.astype(jnp.bfloat16)


def last_pass(queries, late, sums, tops, gate):
    return pl.pallas_call(
        last_kernel,
        out_shape=jax.ShapeDtypeStruct((PEERS * BACK, HEAD_DIM), jnp.bfloat16),
        scratch_shapes=[
            values_scratch(FAR_KEYS),
            pltpu.VMEM((2 * PLANE_ROWS, HEAD_DIM), jnp.bfloat16),
        ],
        compiler_params=pltpu.CompilerParams(vmem_limit_bytes=VMEM_LIMIT),
    )(queries, late, sums, tops, gate)


def finish_kernel(messages, first, second):
    source = lax.broadcasted_iota(jnp.int32, (1, 8 * BACK), 1)
    message = message_of(source, BACK)
    entry = source - message * BACK
    target = message * 16 + (entry % 2) * 8 + entry // 2
    order = one_hot(lax.broadcasted_iota(jnp.int32, (128, 8 * BACK), 0) == target)
    for part in range(ACTIVE // 8):
        rows = dot_f32(order, messages[pl.ds(part * 8 * BACK, 8 * BACK)]).astype(jnp.bfloat16)
        for index in range(8):
            rank = part * 8 + index
            head = (rank % 4) * PAIR_HEADS + rank // 4
            columns = pl.ds(head * HEAD_DIM, HEAD_DIM)
            first[:, columns] = rows[index * 16 : index * 16 + ROWS]
            second[:, columns] = rows[index * 16 + 8 : index * 16 + 8 + ROWS]


def finish(messages):
    shape = jax.ShapeDtypeStruct((ROWS, HEADS * HEAD_DIM), jnp.bfloat16)
    return pl.pallas_call(
        finish_kernel,
        out_shape=(shape, shape),
        compiler_params=pltpu.CompilerParams(vmem_limit_bytes=VMEM_LIMIT),
    )(messages)


def body(
    query_first,
    keys_first,
    values_first,
    query_second,
    keys_second,
    values_second,
    text_keys,
    text_values,
    gate_table,
    timesteps,
    text_length,
):
    sent = pack(keys_first, values_first, query_first, query_second, keys_second, values_second)
    pairs = sent.reshape(PEERS, CHUNK // 2, 2, HEAD_DIM)
    arrived = lax.all_to_all(pairs, PLANE, 0, 0, tiled=True)
    extra, dead, order = prepare(text_length, timesteps, text_keys, text_values, gate_table)
    copies, queries, mine = unpack(arrived.reshape(PEERS * CHUNK, HEAD_DIM), extra, order)
    planes = lax.all_to_all(copies, "x", 0, 0, tiled=True)
    theirs = lax.ppermute(mine, "c", [(0, 1), (1, 0)])
    sums, tops = mine_pass(queries, mine)
    sums, tops, gate = theirs_pass(dead, queries, mine, theirs, sums, tops)
    late_mine = join(planes, gate)
    late_theirs = lax.ppermute(late_mine, "c", [(0, 1), (1, 0)])
    sums, tops = far_pass(queries, late_mine, sums, tops)
    back = last_pass(queries, late_theirs, sums, tops, gate)
    pairs = back.reshape(PEERS, ROWS, 2, HEAD_DIM)
    returned = lax.all_to_all(pairs, PLANE, 0, 0, tiled=True)
    return finish(returned.reshape(PEERS * BACK, HEAD_DIM))


def solution(mesh):
    fine = Mesh(mesh.devices.reshape(8, 4, 2, 4, 2), AXES)
    rows = P(AXES, None)
    heads = P(None, ("yh", "c"))
    return jax.shard_map(
        body,
        mesh=fine,
        in_specs=(rows,) * 6 + (heads,) * 3 + (P(), P()),
        out_specs=(rows, rows),
        check_vma=False,
    )
```

time: 78.7 us -> 78.9 us (level)
  blocking collectives: 63.7 us -> 17.2 us
  starting transfers between devices: 6.36 us -> 31.9 us
  waiting for transfers between devices: 0.05 us -> 16.6 us
  Pallas kernels: 7.04 us -> 11.4 us
    all_to_all x2 -> x0, blocking collectives: 46.4 us -> none  [the longest x1 35 us: body(): arrived = lax.all_to_all(pairs, PLANE, 0, 0, tiled=True)]
    all_to_all x0 -> x2, starting transfers between devices: none -> 21.2 us  [the longest x1 17.1 us: body(): arrived = lax.all_to_all(pairs, PLANE, 0, 0, tiled=True)]
    all_to_all x0 -> x2, waiting for transfers between devices: none -> 15.8 us  [the longest x1 15.8 us: body(): arrived = lax.all_to_all(pairs, PLANE, 0, 0, tiled=True)]
    ppermute x0 -> x1, starting transfers between devices: none -> 5.53 us  [body(): late_theirs = lax.ppermute(late_mine, 'c', [(0, 1), (1, 0)])]
    pallas_call x4 -> x7, Pallas kernels: 5.78 us -> 9.33 us  [the longest x1 2.37 us: pack(): pl.pallas_call(pack_kernel, out_shape=jax.ShapeDtypeStruct((PEERS * CHUNK...]
    ppermute x1, starting transfers between devices: 6.36 us -> 5.2 us  [body(): theirs = lax.ppermute(mine, 'c', [(0, 1), (1, 0)])]
    pallas_call x1, Pallas kernels: 0.41 us -> 1.2 us  [unpack(): pl.pallas_call(unpack_kernel, out_shape=(jax.ShapeDtypeStruct((4, 2 * PLA...]
  transfers between devices with their start and end apart: 1 -> 4, of which waited for: 0 -> 3; matrix products, arithmetic and copies ran while one was open for 0% -> 0% of each run, Pallas kernels for 2% -> 7%
where the time goes in v7:
time: 78.9 us; the launch traced here: 78.5 us
  starting transfers between devices  31.9 us (40%)
  blocking collectives  17.2 us (22%)
  waiting for transfers between devices  16.6 us (21%)
  Pallas kernels  11.4 us (14%)
  between operations  1.4 us (2%)
    all_to_all x1, blocking collectives, body(): returned = lax.all_to_all(pairs, PLANE, 0, 0, tiled=True)  17.2 us
    all_to_all x1, starting transfers between devices, body(): arrived = lax.all_to_all(pairs, PLANE, 0, 0, tiled=True)  17.1 us
    all_to_all x1, waiting for transfers between devices, body(): arrived = lax.all_to_all(pairs, PLANE, 0, 0, tiled=True)  15.8 us
    ppermute x1, starting transfers between devices, body(): late_theirs = lax.ppermute(late_mine, 'c', [(0, 1), (1, 0)])  5.53 us
    ppermute x1, starting transfers between devices, body(): theirs = lax.ppermute(mine, 'c', [(0, 1), (1, 0)])  5.2 us
    all_to_all x1, starting transfers between devices, body(): planes = lax.all_to_all(copies, 'x', 0, 0, tiled=True)  4.02 us
    pallas_call x1, Pallas kernels, pack(): pl.pallas_call(pack_kernel, out_shape=jax.ShapeDtypeStruct((PEERS * CHUNK...  2.37 us
    pallas_call x1, Pallas kernels, theirs_pass(): pl.pallas_call(theirs_kernel, out_shape=STATE + (jax.ShapeDtypeStruct((2,...  1.61 us
  transfers between devices with their start and end apart: 4, of which 3 were waited for; matrix products, arithmetic and copies ran while one was open for 0% of the time, Pallas kernels for 7%

profile of v7, /device:TPU:1, one launch (start us, length us, event | category | flops | bytes accessed | tf_op | source)
XLA Modules:
  0.0 78.5 jit_solution(5251290997280685001)
XLA Ops:
  0.6 2.4 %shard_map.122 = bf16[1920,128]{1,0:T(8,128)(2,1)} custom-call(bf16[5,5120]{1,0:T(8,128)(2,1)} %k1.1, bf16[5,5120]{1,0:T(8,128)(2,1)} %v1.1, bf16[5,5120]{1,0:T(8,128)(2,1)} %q1.1, bf16[5,5120]{1,0:T(8,128)(2,1)} %q2.1, bf16[5,5120]{1,0:T(8,128)(2,1)} %k2.1, bf16[5,5120]{1,0:T(8,128)(2,1)} %v2.1), custom_call_target="tpu_custom_call" | custom-call | tf_op jit(solution)/shard_map/pallas_call | solution.py:105
  3.0 17.1 %all-to-all-start = ((bf16[64,15,2,128]{3,2,1,0:T(2,128)(2,1)}), bf16[64,15,2,128]{3,2,1,0:T(2,128)(2,1)S(1)}, u32[]{:S(2)}, u32[]{:S(2)}) async-start(bf16[64,15,2,128]{3,2,1,0:T(2,128)(2,1)} %bitcast), calls=%async_computation | async-start | bytes 983040 | tf_op jit(solution)/shard_map/all_to_all | solution.py:502
  20.2 0.0 copy-start
  20.8 0.0 copy-done
  20.8 1.6 %shard_map.123 = (bf16[1040,128]{1,0:T(8,128)(2,1)S(1)}, f32[8,512]{1,0:T(8,128)S(1)}, bf16[240,240]{1,0:T(8,128)(2,1)S(1)}) custom-call(s32[1]{0:T(128)S(6)} %copy.13.length, s32[2]{0:T(128)S(1)} %copy-done, bf16[512,640]{1,0:T(8,128)(2,1)} %text_k.1, bf16[512,640]{1,0:T(8,128)(2,1)} %text_v.1, f32[35,640]{1,0:T(8,128)} %gates.1), custom_call_target="tpu_custom_call" | custom-call | tf_op jit(solution)/shard_map/pallas_call | solution.py:155
  22.4 15.8 %all-to-all-done = bf16[64,15,2,128]{3,2,1,0:T(2,128)(2,1)S(1)} async-done(((bf16[64,15,2,128]{3,2,1,0:T(2,128)(2,1)}), bf16[64,15,2,128]{3,2,1,0:T(2,128)(2,1)S(1)}, u32[]{:S(2)}, u32[]{:S(2)}) %all-to-all-start) | async-done | bytes 491552 | tf_op jit(solution)/shard_map/all_to_all | solution.py:502
  38.2 1.2 %shard_map.124 = (bf16[4,640,128]{2,1,0:T(8,128)(2,1)}, bf16[640,128]{1,0:T(8,128)(2,1)S(1)}, bf16[2320,128]{1,0:T(8,128)(2,1)S(1)}) custom-call(bf16[1920,128]{1,0:T(8,128)(2,1)S(1)} %bitcast.4, bf16[1040,128]{1,0:T(8,128)(2,1)S(1)} %get-tuple-element.15.extra, bf16[240,240]{1,0:T(8,128)(2,1)S(1)} %get-tuple-element.16.order), custom_call_target="tpu_custom_call" | custom-call | tf_op jit(solution)/shard_map/pallas_call | solution.py:203
  39.4 4.0 %all-to-all-start.1 = ((bf16[4,640,128]{2,1,0:T(8,128)(2,1)}), bf16[4,640,128]{2,1,0:T(8,128)(2,1)S(1)}, u32[]{:S(2)}, u32[]{:S(2)}) async-start(bf16[4,640,128]{2,1,0:T(8,128)(2,1)} %get-tuple-element.18), calls=%async_computation.1 | async-start | bytes 1310720 | tf_op jit(solution)/shard_map/all_to_all | solution.py:505
  43.4 5.2 %collective-permute-start = (bf16[2320,128]{1,0:T(8,128)(2,1)S(1)}, bf16[2320,128]{1,0:T(8,128)(2,1)S(1)}, u32[]{:S(2)}, u32[]{:S(2)}) collective-permute-start(bf16[2320,128]{1,0:T(8,128)(2,1)S(1)} %get-tuple-element.20.early.mine), channel_id=1, source_target_pairs={{0,1},{1,0},{2,3},{3,2},{4,5},{5,4},{6,7},{7,6},{8,9},{9,8},{10,11... | collective-permute-start | bytes 1781768 | tf_op jit(solution)/shard_map/ppermute | solution.py:506
  48.7 1.0 %shard_map.125 = (f32[640,256]{1,0:T(8,128)S(1)}, f32[640,128]{1,0:T(8,128)S(1)}) custom-call(bf16[640,128]{1,0:T(8,128)(2,1)S(1)} %get-tuple-element.17.queries, bf16[2320,128]{1,0:T(8,128)(2,1)S(1)} %get-tuple-element.20.early.mine), custom_call_target="tpu_custom_call" | custom-call | flops 8000000000 | tf_op jit(solution)/shard_map/pallas_call | solution.py:367
  49.6 0.6 collective-permute-done.theirs
  50.3 1.6 %shard_map.126 = (f32[640,256]{1,0:T(8,128)S(1)}, f32[640,128]{1,0:T(8,128)S(1)}, f32[2,128]{1,0:T(2,128)S(1)}) custom-call(f32[8,512]{1,0:T(8,128)S(1)} %get-tuple-element.19.dead, bf16[640,128]{1,0:T(8,128)(2,1)S(1)} %get-tuple-element.17.queries, bf16[2320,128]{1,0:T(8,128)(2,1)S(1)} %get-tuple-element.20.early.mine, ...), custom_call_target="tpu_custom_call" | custom-call | tf_op jit(solution)/shard_map/pallas_call | solution.py:402
  51.9 0.0 all-to-all-done.1.planes
  51.9 0.1 shard_map.127.late
  52.0 5.5 %collective-permute-start.1 = (bf16[1984,128]{1,0:T(8,128)(2,1)S(1)}, bf16[1984,128]{1,0:T(8,128)(2,1)S(1)}, u32[]{:S(2)}, u32[]{:S(2)}) collective-permute-start(bf16[1984,128]{1,0:T(8,128)(2,1)S(1)} %shard_map.127.late), channel_id=1, source_target_pairs={{0,1},{1,0},{2,3},{3,2},{4,5},{5,4},{6,7},{7,6},{8,9},{9,8},{10,11... | collective-permute-start | bytes 1523720 | tf_op jit(solution)/shard_map/ppermute | solution.py:510
  57.5 1.3 %shard_map.128 = (f32[640,256]{1,0:T(8,128)S(1)}, f32[640,128]{1,0:T(8,128)S(1)}) custom-call(bf16[640,128]{1,0:T(8,128)(2,1)S(1)} %get-tuple-element.17.queries, bf16[1984,128]{1,0:T(8,128)(2,1)S(1)} %shard_map.127.late, f32[640,256]{1,0:T(8,128)S(1)} %get-tuple-element.24.sums, f32[640,128]{1,0:T(8,128)S(1)} %get-tuple-element.25.tops), custom_call_target="tpu_custom_call" | custom-call | tf_op jit(solution)/shard_map/pallas_call | solution.py:425
  58.8 0.2 collective-permute-done.1.late
  59.0 1.5 %shard_map.129 = bf16[640,128]{1,0:T(8,128)(2,1)S(1)} custom-call(bf16[640,128]{1,0:T(8,128)(2,1)S(1)} %get-tuple-element.17.queries, bf16[1984,128]{1,0:T(8,128)(2,1)S(1)} %collective-permute-done.1.late, f32[640,256]{1,0:T(8,128)S(1)} %get-tuple-element.26.sums, f32[640,128]{1,0:T(8,128)S(1)} %get-tuple-element.27.tops, ...), custom_call_target="tpu_custom_call" | custom-call | tf_op jit(solution)/shard_map/pallas_call | solution.py:451
  60.5 17.2 %all_to_all.15 = bf16[64,5,2,128]{3,2,1,0:T(2,128)(2,1)S(1)} all-to-all(bf16[64,5,2,128]{3,2,1,0:T(2,128)(2,1)S(1)} %bitcast.5), channel_id=1, replica_groups=mesh['z'=8,'x'=4,'yl'=2,'yh'=4,'c'=2] {'z','yl','yh'}, dimensions={0} | all-to-all | bytes 327680 | tf_op jit(solution)/shard_map/all_to_all | solution.py:514
  77.7 0.9 %shard_map.130 = (bf16[5,5120]{1,0:T(8,128)(2,1)}, bf16[5,5120]{1,0:T(8,128)(2,1)}) custom-call(bf16[640,128]{1,0:T(8,128)(2,1)S(1)} %bitcast.6), custom_call_target="tpu_custom_call" | custom-call | tf_op jit(solution)/shard_map/pallas_call | solution.py:480
Async XLA Ops:
  3.0 35.2 %all-to-all-start = ((bf16[64,15,2,128]{3,2,1,0:T(2,128)(2,1)}), bf16[64,15,2,128]{3,2,1,0:T(2,128)(2,1)S(1)}, u32[]{:S(2)}, u32[]{:S(2)}) async-start(bf16[64,15,2,128]{3,2,1,0:T(2,128)(2,1)} %bitcast), calls=%async_computation | async-start | bytes 983040 | tf_op jit(solution)/shard_map/all_to_all | solution.py:502
  20.2 0.7 copy-start
  39.4 12.5 %all-to-all-start.1 = ((bf16[4,640,128]{2,1,0:T(8,128)(2,1)}), bf16[4,640,128]{2,1,0:T(8,128)(2,1)S(1)}, u32[]{:S(2)}, u32[]{:S(2)}) async-start(bf16[4,640,128]{2,1,0:T(8,128)(2,1)} %get-tuple-element.18), calls=%async_computation.1 | async-start | bytes 1310720 | tf_op jit(solution)/shard_map/all_to_all | solution.py:505
  43.4 6.8 %collective-permute-start = (bf16[2320,128]{1,0:T(8,128)(2,1)S(1)}, bf16[2320,128]{1,0:T(8,128)(2,1)S(1)}, u32[]{:S(2)}, u32[]{:S(2)}) collective-permute-start(bf16[2320,128]{1,0:T(8,128)(2,1)S(1)} %get-tuple-element.20.early.mine), channel_id=1, source_target_pairs={{0,1},{1,0},{2,3},{3,2},{4,5},{5,4},{6,7},{7,6},{8,9},{9,8},{10,11... | collective-permute-start | bytes 1781768 | tf_op jit(solution)/shard_map/ppermute | solution.py:506
  52.0 7.0 %collective-permute-start.1 = (bf16[1984,128]{1,0:T(8,128)(2,1)S(1)}, bf16[1984,128]{1,0:T(8,128)(2,1)S(1)}, u32[]{:S(2)}, u32[]{:S(2)}) collective-permute-start(bf16[1984,128]{1,0:T(8,128)(2,1)S(1)} %shard_map.127.late), channel_id=1, source_target_pairs={{0,1},{1,0},{2,3},{3,2},{4,5},{5,4},{6,7},{7,6},{8,9},{9,8},{10,11... | collective-permute-start | bytes 1523720 | tf_op jit(solution)/shard_map/ppermute | solution.py:510

commit v8 on v6

--- a/solution.py
+++ b/solution.py
@@ -13,7 +13,6 @@
 PAIR_HEADS = 10
 ROWS = 5
 PLANE_ROWS = 320
-BLOCK_ROWS = 20
 PEERS = 64
 CHUNK = 6 * ROWS
 BACK = 2 * ROWS
@@ -21,7 +20,7 @@
 EXP_SCALE = float(HEAD_DIM ** (-0.5) * np.log2(np.e))
 
 AXES = ("z", "x", "yl", "yh", "c")
-PLANE = ("z", "yl", "yh")
+PLANE = ("z", "yh", "yl")
 ACTIVE = 4 * PAIR_HEADS
 
 HALF = 4 * PLANE_ROWS
@@ -48,6 +47,10 @@
 
 def head_slot():
     return lax.axis_index("z") * 2 + lax.axis_index("yl")
+
+
+def head_of(rank):
+    return (rank % 8) // 2 * PAIR_HEADS + rank // 8 * 2 + rank % 2
 
 
 def in_hbm(array):
@@ -82,15 +85,15 @@
     for fetch in fetches:
         fetch.start()
     stacked[...] = jnp.zeros_like(stacked)
-    for index in range(6):
-        fetches[index].wait()
-        stacked[pl.ds(index * 8, ROWS)] = held[index]
     source = lax.broadcasted_iota(jnp.int32, (1, 8 * 48), 1)
     message = message_of(source, 48)
     array = (source - message * 48) // 8
     entry = source - message * 48 - array * 8
     target = jnp.where(entry < ROWS, message * CHUNK + array * ROWS + entry, -1)
     order = one_hot(lax.broadcasted_iota(jnp.int32, (8 * CHUNK, 8 * 48), 0) == target)
+    for index in range(6):
+        fetches[index].wait()
+        stacked[pl.ds(index * 8, ROWS)] = held[index]
     for part in range(PEERS // 8):
         place = pl.ds(part * 8 * CHUNK, 8 * CHUNK)
         if part * 8 >= ACTIVE:
@@ -98,7 +101,7 @@
             continue
         pieces = []
         for rank in range(part * 8, part * 8 + 8):
-            head = (rank % 4) * PAIR_HEADS + rank // 4
+            head = head_of(rank)
             pieces.append(stacked[:, head * HEAD_DIM : (head + 1) * HEAD_DIM])
         out[place] = dot_f32(order, jnp.concatenate(pieces, axis=0)).astype(jnp.bfloat16)
     for fetch in fetches[6:]:
@@ -195,8 +198,13 @@
 CUTS = ((0, 512), (512, 1024), (1024, HALF))
 
 
+def floor_of(index, step):
+    return jnp.floor((index + 0.5) * (1.0 / step))
+
+
 def block_of(index):
-    return jnp.floor((index.astype(jnp.float32) + 0.5) * (1.0 / BLOCK_ROWS))
+    message = floor_of(index.astype(jnp.float32), ROWS)
+    return 2.0 * floor_of(message, 8) + message - 2.0 * floor_of(message, 2)
 
 
 def beside_ones(target, rows):
@@ -389,7 +397,7 @@
         rows = dot_f32(order, messages[pl.ds(part * 8 * BACK, 8 * BACK)]).astype(jnp.bfloat16)
         for index in range(8):
             rank = part * 8 + index
-            head = (rank % 4) * PAIR_HEADS + rank // 4
+            head = head_of(rank)
             columns = pl.ds(head * HEAD_DIM, HEAD_DIM)
             first[:, columns] = rows[index * 16 : index * 16 + ROWS]
             second[:, columns] = rows[index * 16 + 8 : index * 16 + 8 + ROWS]

time: 78.7 us -> 78.1 us (level)
  blocking collectives: 63.7 us -> 62.5 us
    all_to_all x1, blocking collectives: 35 us -> 33.5 us  [body(): arrived = lax.all_to_all(pairs, PLANE, 0, 0, tiled=True)]
where the time goes in v8:
time: 78.1 us; the launch traced here: 77.7 us
  blocking collectives  62.5 us (80%)
  Pallas kernels  7.09 us (9%)
  starting transfers between devices  6.71 us (9%)
  between operations  1.32 us (2%)
    all_to_all x1, blocking collectives, body(): arrived = lax.all_to_all(pairs, PLANE, 0, 0, tiled=True)  33.5 us
    all_to_all x1, blocking collectives, body(): returned = lax.all_to_all(pairs, PLANE, 0, 0, tiled=True)  17.6 us
    all_to_all x1, blocking collectives, body(): planes = lax.all_to_all(copies, 'x', 0, 0, tiled=True)  11.5 us
    ppermute x1, starting transfers between devices, body(): theirs = lax.ppermute(mine, 'c', [(0, 1), (1, 0)])  6.71 us
    pallas_call x1, Pallas kernels, second_pass(): pl.pallas_call(second_kernel, out_shape=jax.ShapeDtypeStruct((PEERS * BAC...  2.42 us
    pallas_call x1, Pallas kernels, pack(): pl.pallas_call(pack_kernel, out_shape=(jax.ShapeDtypeStruct((PEERS * CHUN...  1.71 us
    pallas_call x1, Pallas kernels, first_pass(): pl.pallas_call(first_kernel, out_shape=(jax.ShapeDtypeStruct((2 * PLANE_R...  1.63 us
  transfers between devices with their start and end apart: 1, of which 0 were waited for; matrix products, arithmetic and copies ran while one was open for 0% of the time, Pallas kernels for 2%

profile of v8, /device:TPU:1, one launch (start us, length us, event | category | flops | bytes accessed | tf_op | source)
XLA Modules:
  0.0 77.7 jit_solution(1407373360449475018)
XLA Ops:
  0.6 1.7 %shard_map.122 = (bf16[1920,128]{1,0:T(8,128)(2,1)S(1)}, bf16[1040,128]{1,0:T(8,128)(2,1)S(1)}) custom-call(bf16[5,5120]{1,0:T(8,128)(2,1)} %k1.1, bf16[5,5120]{1,0:T(8,128)(2,1)} %v1.1, bf16[5,5120]{1,0:T(8,128)(2,1)} %q1.1, bf16[5,5120]{1,0:T(8,128)(2,1)} %q2.1, bf16[5,5120]{1,0:T(8,128)(2,1)} %k2.1, bf16[5,5120]{1,0:T(8,128)(2,1)} %v2.1, ...), custom_call_target="tpu_custom_call" | custom-call | tf_op jit(solution)/shard_map/pallas_call | solution.py:122
  2.4 33.5 %all_to_all.15 = bf16[64,15,2,128]{3,2,1,0:T(2,128)(2,1)S(1)} all-to-all(bf16[64,15,2,128]{3,2,1,0:T(2,128)(2,1)S(1)} %bitcast.7), channel_id=1, replica_groups=mesh['z'=8,'x'=4,'yl'=2,'yh'=4,'c'=2] {'z','yh','yl'}, dimensions={0} | all-to-all | bytes 983040 | tf_op jit(solution)/shard_map/all_to_all | solution.py:441
  35.8 0.4 shard_map.123
  36.2 11.5 %all_to_all.16.planes = bf16[4,640,128]{2,1,0:T(8,128)(2,1)S(1)} all-to-all(bf16[4,640,128]{2,1,0:T(8,128)(2,1)S(1)} %get-tuple-element.11), channel_id=1, replica_groups=mesh['z'=8,'x'=4,'yl'=2,'yh'=4,'c'=2] {'x'}, dimensions={0} | all-to-all | bytes 1310720 | tf_op jit(solution)/shard_map/all_to_all | solution.py:443
  47.7 0.1 shard_map.124.mine
  47.8 6.7 %collective-permute-start = (bf16[4240,128]{1,0:T(8,128)(2,1)S(1)}, bf16[4240,128]{1,0:T(8,128)(2,1)S(1)}, u32[]{:S(2)}, u32[]{:S(2)}) collective-permute-start(bf16[4240,128]{1,0:T(8,128)(2,1)S(1)} %shard_map.124.mine), channel_id=1, source_target_pairs={{0,1},{1,0},{2,3},{3,2},{4,5},{5,4},{6,7},{7,6},{8,9},{9,8},{10,11... | collective-permute-start | bytes 3256328 | tf_op jit(solution)/shard_map/ppermute | solution.py:445
  55.1 1.6 %shard_map.125 = (f32[640,256]{1,0:T(8,128)S(1)}, f32[640,128]{1,0:T(8,128)S(1)}) custom-call(bf16[640,128]{1,0:T(8,128)(2,1)S(1)} %get-tuple-element.10.queries, bf16[4240,128]{1,0:T(8,128)(2,1)S(1)} %shard_map.124.mine), custom_call_target="tpu_custom_call" | custom-call | flops 524288000 | bytes 1085440 | tf_op jit(solution)/shard_map/pallas_call | solution.py:353
  56.8 0.0 collective-permute-done.theirs
  56.8 2.4 %shard_map.126 = bf16[640,128]{1,0:T(8,128)(2,1)S(1)} custom-call(s32[1]{0:T(128)S(6)} %copy.13.length, bf16[640,128]{1,0:T(8,128)(2,1)S(1)} %get-tuple-element.10.queries, bf16[4240,128]{1,0:T(8,128)(2,1)S(1)} %shard_map.124.mine, bf16[4240,128]{1,0:T(8,128)(2,1)S(1)} %collective-permute-done.theirs, f32[640,256]{1,0:T(8,128)S(1)} %get-tuple-element.14.sums, ...), custom_call_target="tpu_custom_call" | custom-call | tf_op jit(solution)/shard_map/pallas_call | solution.py:374
  59.2 17.6 %all_to_all.17 = bf16[64,5,2,128]{3,2,1,0:T(2,128)(2,1)S(1)} all-to-all(bf16[64,5,2,128]{3,2,1,0:T(2,128)(2,1)S(1)} %bitcast.5), channel_id=1, replica_groups=mesh['z'=8,'x'=4,'yl'=2,'yh'=4,'c'=2] {'z','yh','yl'}, dimensions={0} | all-to-all | bytes 327680 | tf_op jit(solution)/shard_map/all_to_all | solution.py:449
  76.8 0.9 %shard_map.127 = (bf16[5,5120]{1,0:T(8,128)(2,1)}, bf16[5,5120]{1,0:T(8,128)(2,1)}) custom-call(bf16[640,128]{1,0:T(8,128)(2,1)S(1)} %bitcast.6), custom_call_target="tpu_custom_call" | custom-call | tf_op jit(solution)/shard_map/pallas_call | solution.py:408
Async XLA Ops:
  47.8 9.0 %collective-permute-start = (bf16[4240,128]{1,0:T(8,128)(2,1)S(1)}, bf16[4240,128]{1,0:T(8,128)(2,1)S(1)}, u32[]{:S(2)}, u32[]{:S(2)}) collective-permute-start(bf16[4240,128]{1,0:T(8,128)(2,1)S(1)} %shard_map.124.mine), channel_id=1, source_target_pairs={{0,1},{1,0},{2,3},{3,2},{4,5},{5,4},{6,7},{7,6},{8,9},{9,8},{10,11... | collective-permute-start | bytes 3256328 | tf_op jit(solution)/shard_map/ppermute | solution.py:445

commit v9 on v8

--- a/solution.py
+++ b/solution.py
@@ -20,8 +20,7 @@
 EXP_SCALE = float(HEAD_DIM ** (-0.5) * np.log2(np.e))
 
 AXES = ("z", "x", "yl", "yh", "c")
-PLANE = ("z", "yh", "yl")
-ACTIVE = 4 * PAIR_HEADS
+PLANE = ("yh", "z", "yl")
 
 HALF = 4 * PLANE_ROWS
 NEAR_AT = 2 * HALF
@@ -50,7 +49,8 @@
 
 
 def head_of(rank):
-    return (rank % 8) // 2 * PAIR_HEADS + rank // 8 * 2 + rank % 2
+    slot = rank % 16
+    return rank // 16 * PAIR_HEADS + slot if slot < PAIR_HEADS else None
 
 
 def in_hbm(array):
@@ -96,13 +96,13 @@
         stacked[pl.ds(index * 8, ROWS)] = held[index]
     for part in range(PEERS // 8):
         place = pl.ds(part * 8 * CHUNK, 8 * CHUNK)
-        if part * 8 >= ACTIVE:
-            out[place] = jnp.zeros((8 * CHUNK, HEAD_DIM), jnp.bfloat16)
-            continue
         pieces = []
         for rank in range(part * 8, part * 8 + 8):
             head = head_of(rank)
-            pieces.append(stacked[:, head * HEAD_DIM : (head + 1) * HEAD_DIM])
+            if head is None:
+                pieces.append(jnp.zeros((48, HEAD_DIM), jnp.bfloat16))
+            else:
+                pieces.append(stacked[:, head * HEAD_DIM : (head + 1) * HEAD_DIM])
         out[place] = dot_f32(order, jnp.concatenate(pieces, axis=0)).astype(jnp.bfloat16)
     for fetch in fetches[6:]:
         fetch.wait()
@@ -204,7 +204,7 @@
 
 def block_of(index):
     message = floor_of(index.astype(jnp.float32), ROWS)
-    return 2.0 * floor_of(message, 8) + message - 2.0 * floor_of(message, 2)
+    return message - 16.0 * floor_of(message, 16)
 
 
 def beside_ones(target, rows):
@@ -215,7 +215,7 @@
 def same_block(tile):
     row = lax.broadcasted_iota(jnp.int32, (TILE, 1), 0) + (tile * TILE) % PLANE_ROWS
     column = lax.broadcasted_iota(jnp.int32, (1, NEAR), 1)
-    return block_of(row) == block_of(column)
+    return block_of(row) == jnp.where(column < PLANE_ROWS, block_of(column), -1.0)
 
 
 def tile_rows(tile):
@@ -393,11 +393,13 @@
     entry = source - message * BACK
     target = message * 16 + (entry % 2) * 8 + entry // 2
     order = one_hot(lax.broadcasted_iota(jnp.int32, (128, 8 * BACK), 0) == target)
-    for part in range(ACTIVE // 8):
+    for part in range(PEERS // 8):
         rows = dot_f32(order, messages[pl.ds(part * 8 * BACK, 8 * BACK)]).astype(jnp.bfloat16)
         for index in range(8):
             rank = part * 8 + index
             head = head_of(rank)
+            if head is None:
+                continue
             columns = pl.ds(head * HEAD_DIM, HEAD_DIM)
             first[:, columns] = rows[index * 16 : index * 16 + ROWS]
             second[:, columns] = rows[index * 16 + 8 : index * 16 + 8 + ROWS]

time: 78.1 us -> 78.1 us (level)
  starting transfers between devices: 6.71 us -> 5.87 us
  blocking collectives: 62.5 us -> 63.3 us
    all_to_all x1, blocking collectives: 17.6 us -> 18.8 us  [body(): returned = lax.all_to_all(pairs, PLANE, 0, 0, tiled=True)]
    ppermute x1, starting transfers between devices: 6.71 us -> 5.87 us  [body(): theirs = lax.ppermute(mine, 'c', [(0, 1), (1, 0)])]
where the time goes in v9:
time: 78.1 us; the launch traced here: 77.8 us
  blocking collectives  63.3 us (81%)
  Pallas kernels  7.25 us (9%)
  starting transfers between devices  5.87 us (8%)
  between operations  1.32 us (2%)
    all_to_all x1, blocking collectives, body(): arrived = lax.all_to_all(pairs, PLANE, 0, 0, tiled=True)  32.8 us
    all_to_all x1, blocking collectives, body(): returned = lax.all_to_all(pairs, PLANE, 0, 0, tiled=True)  18.8 us
    all_to_all x1, blocking collectives, body(): planes = lax.all_to_all(copies, 'x', 0, 0, tiled=True)  11.7 us
    ppermute x1, starting transfers between devices, body(): theirs = lax.ppermute(mine, 'c', [(0, 1), (1, 0)])  5.87 us
    pallas_call x1, Pallas kernels, second_pass(): pl.pallas_call(second_kernel, out_shape=jax.ShapeDtypeStruct((PEERS * BAC...  2.4 us
    pallas_call x1, Pallas kernels, pack(): pl.pallas_call(pack_kernel, out_shape=(jax.ShapeDtypeStruct((PEERS * CHUN...  1.87 us
    pallas_call x1, Pallas kernels, first_pass(): pl.pallas_call(first_kernel, out_shape=(jax.ShapeDtypeStruct((2 * PLANE_R...  1.62 us
  transfers between devices with their start and end apart: 1, of which 0 were waited for; matrix products, arithmetic and copies ran while one was open for 0% of the time, Pallas kernels for 2%

profile of v9, /device:TPU:1, one launch (start us, length us, event | category | flops | bytes accessed | tf_op | source)
XLA Modules:
  0.0 77.8 jit_solution(6843087121904852123)
XLA Ops:
  0.6 1.9 %shard_map.122 = (bf16[1920,128]{1,0:T(8,128)(2,1)S(1)}, bf16[1040,128]{1,0:T(8,128)(2,1)S(1)}) custom-call(bf16[5,5120]{1,0:T(8,128)(2,1)} %k1.1, bf16[5,5120]{1,0:T(8,128)(2,1)} %v1.1, bf16[5,5120]{1,0:T(8,128)(2,1)} %q1.1, bf16[5,5120]{1,0:T(8,128)(2,1)} %q2.1, bf16[5,5120]{1,0:T(8,128)(2,1)} %k2.1, bf16[5,5120]{1,0:T(8,128)(2,1)} %v2.1, ...), custom_call_target="tpu_custom_call" | custom-call | tf_op jit(solution)/shard_map/pallas_call | solution.py:122
  2.5 32.8 %all_to_all.15 = bf16[64,15,2,128]{3,2,1,0:T(2,128)(2,1)S(1)} all-to-all(bf16[64,15,2,128]{3,2,1,0:T(2,128)(2,1)S(1)} %bitcast.7), channel_id=1, replica_groups=mesh['z'=8,'x'=4,'yl'=2,'yh'=4,'c'=2] {'yh','z','yl'}, dimensions={0} | all-to-all | bytes 983040 | tf_op jit(solution)/shard_map/all_to_all | solution.py:443
  35.3 0.4 shard_map.123
  35.7 11.7 %all_to_all.16.planes = bf16[4,640,128]{2,1,0:T(8,128)(2,1)S(1)} all-to-all(bf16[4,640,128]{2,1,0:T(8,128)(2,1)S(1)} %get-tuple-element.11), channel_id=1, replica_groups=mesh['z'=8,'x'=4,'yl'=2,'yh'=4,'c'=2] {'x'}, dimensions={0} | all-to-all | bytes 1310720 | tf_op jit(solution)/shard_map/all_to_all | solution.py:445
  47.4 0.1 shard_map.124.mine
  47.5 5.9 %collective-permute-start = (bf16[4240,128]{1,0:T(8,128)(2,1)S(1)}, bf16[4240,128]{1,0:T(8,128)(2,1)S(1)}, u32[]{:S(2)}, u32[]{:S(2)}) collective-permute-start(bf16[4240,128]{1,0:T(8,128)(2,1)S(1)} %shard_map.124.mine), channel_id=1, source_target_pairs={{0,1},{1,0},{2,3},{3,2},{4,5},{5,4},{6,7},{7,6},{8,9},{9,8},{10,11... | collective-permute-start | bytes 3256328 | tf_op jit(solution)/shard_map/ppermute | solution.py:447
  54.0 1.6 %shard_map.125 = (f32[640,256]{1,0:T(8,128)S(1)}, f32[640,128]{1,0:T(8,128)S(1)}) custom-call(bf16[640,128]{1,0:T(8,128)(2,1)S(1)} %get-tuple-element.10.queries, bf16[4240,128]{1,0:T(8,128)(2,1)S(1)} %shard_map.124.mine), custom_call_target="tpu_custom_call" | custom-call | flops 524288000 | bytes 1085440 | tf_op jit(solution)/shard_map/pallas_call | solution.py:353
  55.6 0.0 collective-permute-done.theirs
  55.7 2.4 %shard_map.126 = bf16[640,128]{1,0:T(8,128)(2,1)S(1)} custom-call(s32[1]{0:T(128)S(6)} %copy.13.length, bf16[640,128]{1,0:T(8,128)(2,1)S(1)} %get-tuple-element.10.queries, bf16[4240,128]{1,0:T(8,128)(2,1)S(1)} %shard_map.124.mine, bf16[4240,128]{1,0:T(8,128)(2,1)S(1)} %collective-permute-done.theirs, f32[640,256]{1,0:T(8,128)S(1)} %get-tuple-element.14.sums, ...), custom_call_target="tpu_custom_call" | custom-call | tf_op jit(solution)/shard_map/pallas_call | solution.py:374
  58.1 18.8 %all_to_all.17 = bf16[64,5,2,128]{3,2,1,0:T(2,128)(2,1)S(1)} all-to-all(bf16[64,5,2,128]{3,2,1,0:T(2,128)(2,1)S(1)} %bitcast.5), channel_id=1, replica_groups=mesh['z'=8,'x'=4,'yl'=2,'yh'=4,'c'=2] {'yh','z','yl'}, dimensions={0} | all-to-all | bytes 327680 | tf_op jit(solution)/shard_map/all_to_all | solution.py:451
  76.9 0.9 %shard_map.127 = (bf16[5,5120]{1,0:T(8,128)(2,1)}, bf16[5,5120]{1,0:T(8,128)(2,1)}) custom-call(bf16[640,128]{1,0:T(8,128)(2,1)S(1)} %bitcast.6), custom_call_target="tpu_custom_call" | custom-call | tf_op jit(solution)/shard_map/pallas_call | solution.py:410
Async XLA Ops:
  47.5 8.2 %collective-permute-start = (bf16[4240,128]{1,0:T(8,128)(2,1)S(1)}, bf16[4240,128]{1,0:T(8,128)(2,1)S(1)}, u32[]{:S(2)}, u32[]{:S(2)}) collective-permute-start(bf16[4240,128]{1,0:T(8,128)(2,1)S(1)} %shard_map.124.mine), channel_id=1, source_target_pairs={{0,1},{1,0},{2,3},{3,2},{4,5},{5,4},{6,7},{7,6},{8,9},{9,8},{10,11... | collective-permute-start | bytes 3256328 | tf_op jit(solution)/shard_map/ppermute | solution.py:447

commit v10 on v9

--- a/solution.py
+++ b/solution.py
@@ -138,7 +138,7 @@
     )(*[in_hbm(array) for array in arrays])
 
 
-def unpack_kernel(messages, copies, queries, near):
+def unpack_kernel(messages, plane, queries, near):
     source = lax.broadcasted_iota(jnp.int32, (1, 8 * CHUNK), 1)
     message = message_of(source, CHUNK)
     entry = source - message * CHUNK
@@ -151,8 +151,7 @@
             piece = ordered[array * 40 : (array + 1) * 40]
             place = pl.ds((array % 2) * PLANE_ROWS + step * 40, 40)
             if array < 2:
-                for copy in range(4):
-                    copies[copy, place] = piece
+                plane[place] = piece
             elif array < 4:
                 queries[place] = piece
             else:
@@ -164,7 +163,7 @@
     return pl.pallas_call(
         unpack_kernel,
         out_shape=(
-            jax.ShapeDtypeStruct((4, 2 * PLANE_ROWS, HEAD_DIM), jnp.bfloat16),
+            rows,
             rows,
             rows,
         ),
@@ -172,13 +171,12 @@
     )(messages)
 
 
-def join_kernel(planes, near, extra, out):
-    own = lax.axis_index("x")
-    for place in range(4):
-        source = lax.rem(own + place, 4)
+def join_kernel(*refs):
+    planes, (near, extra, out) = refs[:4], refs[4:]
+    for place, plane in enumerate(planes):
         for part in range(2):
-            out[pl.ds(part * HALF + place * PLANE_ROWS, PLANE_ROWS)] = planes[
-                source, pl.ds(part * PLANE_ROWS, PLANE_ROWS)
+            out[pl.ds(part * HALF + place * PLANE_ROWS, PLANE_ROWS)] = plane[
+                pl.ds(part * PLANE_ROWS, PLANE_ROWS)
             ]
     out[pl.ds(NEAR_AT, 2 * PLANE_ROWS)] = near[...]
     out[pl.ds(TEXT_AT, EXTRA)] = extra[...]
@@ -189,7 +187,7 @@
         join_kernel,
         out_shape=jax.ShapeDtypeStruct((SHARED, HEAD_DIM), jnp.bfloat16),
         compiler_params=pltpu.CompilerParams(vmem_limit_bytes=VMEM_LIMIT),
-    )(planes, near, extra)
+    )(*planes, near, extra)
 
 
 TILE = 160
@@ -441,8 +439,11 @@
     )
     pairs = sent.reshape(PEERS, CHUNK // 2, 2, HEAD_DIM)
     arrived = lax.all_to_all(pairs, PLANE, 0, 0, tiled=True)
-    copies, queries, near = unpack(arrived.reshape(PEERS * CHUNK, HEAD_DIM))
-    planes = lax.all_to_all(copies, "x", 0, 0, tiled=True)
+    plane, queries, near = unpack(arrived.reshape(PEERS * CHUNK, HEAD_DIM))
+    planes = [plane] + [
+        lax.ppermute(plane, "x", [((place + step) % 4, place) for place in range(4)])
+        for step in (2, 1, 3)
+    ]
     mine = join(planes, near, extra)
     theirs = lax.ppermute(mine, "c", [(0, 1), (1, 0)])
     sums, tops = first_pass(queries, mine)

time: 78.1 us -> 79.4 us (1.017)
  blocking collectives: 63.3 us -> 50.3 us
  starting transfers between devices: 5.87 us -> 16 us
  waiting for transfers between devices: 0.04 us -> 4.15 us
    all_to_all x1 -> x0, blocking collectives: 11.7 us -> none  [body(): planes = lax.all_to_all(copies, 'x', 0, 0, tiled=True)]
    ppermute x0 -> x3, starting transfers between devices: none -> 9.93 us  [body(): lax.ppermute(plane, 'x', [((place + step) % 4, place) for place in range(...]
    ppermute x0 -> x3, waiting for transfers between devices: none -> 4.11 us  [body(): lax.ppermute(plane, 'x', [((place + step) % 4, place) for place in range(...]
    all_to_all x1, blocking collectives: 18.8 us -> 17.5 us  [body(): returned = lax.all_to_all(pairs, PLANE, 0, 0, tiled=True)]
  transfers between devices with their start and end apart: 1 -> 4, of which waited for: 0 -> 1; matrix products, arithmetic and copies ran while one was open for 0% -> 0% of each run, Pallas kernels for 2% -> 2%
where the time goes in v10:
time: 79.4 us; the launch traced here: 79 us
  blocking collectives  50.3 us (63%)
  starting transfers between devices  16 us (20%)
  Pallas kernels  7.26 us (9%)
  waiting for transfers between devices  4.15 us (5%)
  between operations  1.36 us (2%)
    all_to_all x1, blocking collectives, body(): arrived = lax.all_to_all(pairs, PLANE, 0, 0, tiled=True)  32.8 us
    all_to_all x1, blocking collectives, body(): returned = lax.all_to_all(pairs, PLANE, 0, 0, tiled=True)  17.5 us
    ppermute x3, starting transfers between devices, body(): lax.ppermute(plane, 'x', [((place + step) % 4, place) for place in range(...  9.93 us
    ppermute x1, starting transfers between devices, body(): theirs = lax.ppermute(mine, 'c', [(0, 1), (1, 0)])  6.08 us
    ppermute x3, waiting for transfers between devices, body(): lax.ppermute(plane, 'x', [((place + step) % 4, place) for place in range(...  4.11 us
    pallas_call x1, Pallas kernels, second_pass(): pl.pallas_call(second_kernel, out_shape=jax.ShapeDtypeStruct((PEERS * BAC...  2.4 us
    pallas_call x1, Pallas kernels, pack(): pl.pallas_call(pack_kernel, out_shape=(jax.ShapeDtypeStruct((PEERS * CHUN...  1.87 us
    pallas_call x1, Pallas kernels, first_pass(): pl.pallas_call(first_kernel, out_shape=(jax.ShapeDtypeStruct((2 * PLANE_R...  1.62 us
  transfers between devices with their start and end apart: 4, of which 1 were waited for; matrix products, arithmetic and copies ran while one was open for 0% of the time, Pallas kernels for 2%

profile of v10, /device:TPU:1, one launch (start us, length us, event | category | flops | bytes accessed | tf_op | source)
XLA Modules:
  0.0 79.0 jit_solution(9261048582645203541)
XLA Ops:
  0.6 1.9 %shard_map.122 = (bf16[1920,128]{1,0:T(8,128)(2,1)S(1)}, bf16[1040,128]{1,0:T(8,128)(2,1)S(1)}) custom-call(bf16[5,5120]{1,0:T(8,128)(2,1)} %k1.1, bf16[5,5120]{1,0:T(8,128)(2,1)} %v1.1, bf16[5,5120]{1,0:T(8,128)(2,1)} %q1.1, bf16[5,5120]{1,0:T(8,128)(2,1)} %q2.1, bf16[5,5120]{1,0:T(8,128)(2,1)} %k2.1, bf16[5,5120]{1,0:T(8,128)(2,1)} %v2.1, ...), custom_call_target="tpu_custom_call" | custom-call | tf_op jit(solution)/shard_map/pallas_call | solution.py:122
  2.5 32.8 %all_to_all.10 = bf16[64,15,2,128]{3,2,1,0:T(2,128)(2,1)S(1)} all-to-all(bf16[64,15,2,128]{3,2,1,0:T(2,128)(2,1)S(1)} %bitcast.7), channel_id=1, replica_groups=mesh['z'=8,'x'=4,'yl'=2,'yh'=4,'c'=2] {'yh','z','yl'}, dimensions={0} | all-to-all | bytes 983040 | tf_op jit(solution)/shard_map/all_to_all | solution.py:441
  35.3 0.4 shard_map.123
  35.7 3.1 %collective-permute-start.2 = (bf16[640,128]{1,0:T(8,128)(2,1)S(1)}, bf16[640,128]{1,0:T(8,128)(2,1)S(1)}, u32[]{:S(2)}, u32[]{:S(2)}) collective-permute-start(bf16[640,128]{1,0:T(8,128)(2,1)S(1)} %get-tuple-element.11.refs_0_), channel_id=1, source_target_pairs={{48,0},{0,16},{16,32},{32,48},{49,1},{1,17},{17,33},{33,49},{50,2}... | collective-permute-start | bytes 491528 | tf_op jit(solution)/shard_map/ppermute | solution.py:444
  38.9 3.4 %collective-permute-start.1 = (bf16[640,128]{1,0:T(8,128)(2,1)S(1)}, bf16[640,128]{1,0:T(8,128)(2,1)S(1)}, u32[]{:S(2)}, u32[]{:S(2)}) collective-permute-start(bf16[640,128]{1,0:T(8,128)(2,1)S(1)} %get-tuple-element.11.refs_0_), channel_id=1, source_target_pairs={{16,0},{32,16},{48,32},{0,48},{17,1},{33,17},{49,33},{1,49},{18,2}... | collective-permute-start | bytes 491528 | tf_op jit(solution)/shard_map/ppermute | solution.py:444
  42.2 3.4 %collective-permute-start = (bf16[640,128]{1,0:T(8,128)(2,1)S(1)}, bf16[640,128]{1,0:T(8,128)(2,1)S(1)}, u32[]{:S(2)}, u32[]{:S(2)}) collective-permute-start(bf16[640,128]{1,0:T(8,128)(2,1)S(1)} %get-tuple-element.11.refs_0_), channel_id=1, source_target_pairs={{32,0},{48,16},{0,32},{16,48},{33,1},{49,17},{1,33},{17,49},{34,2}... | collective-permute-start | bytes 491528 | tf_op jit(solution)/shard_map/ppermute | solution.py:444
  45.7 0.0 collective-permute-done.2.refs_3_
  45.7 0.0 collective-permute-done.1.refs_2_
  45.7 4.1 %collective-permute-done.refs_1_ = bf16[640,128]{1,0:T(8,128)(2,1)S(1)} collective-permute-done((bf16[640,128]{1,0:T(8,128)(2,1)S(1)}, bf16[640,128]{1,0:T(8,128)(2,1)S(1)}, u32[]{:S(2)}, u32[]{:S(2)}) %collective-permute-start) | collective-permute-done | bytes 163872 | tf_op jit(solution)/shard_map/ppermute | solution.py:444
  49.8 0.1 shard_map.124.mine
  49.9 6.1 %collective-permute-start.3 = (bf16[4240,128]{1,0:T(8,128)(2,1)S(1)}, bf16[4240,128]{1,0:T(8,128)(2,1)S(1)}, u32[]{:S(2)}, u32[]{:S(2)}) collective-permute-start(bf16[4240,128]{1,0:T(8,128)(2,1)S(1)} %shard_map.124.mine), channel_id=1, source_target_pairs={{0,1},{1,0},{2,3},{3,2},{4,5},{5,4},{6,7},{7,6},{8,9},{9,8},{10,11... | collective-permute-start | bytes 3256328 | tf_op jit(solution)/shard_map/ppermute | solution.py:448
  56.6 1.6 %shard_map.125 = (f32[640,256]{1,0:T(8,128)S(1)}, f32[640,128]{1,0:T(8,128)S(1)}) custom-call(bf16[640,128]{1,0:T(8,128)(2,1)S(1)} %get-tuple-element.10.queries, bf16[4240,128]{1,0:T(8,128)(2,1)S(1)} %shard_map.124.mine), custom_call_target="tpu_custom_call" | custom-call | flops 524288000 | bytes 1085440 | tf_op jit(solution)/shard_map/pallas_call | solution.py:351
  58.2 0.0 collective-permute-done.3.theirs
  58.3 2.4 %shard_map.126 = bf16[640,128]{1,0:T(8,128)(2,1)S(1)} custom-call(s32[1]{0:T(128)S(6)} %copy.13.length, bf16[640,128]{1,0:T(8,128)(2,1)S(1)} %get-tuple-element.10.queries, bf16[4240,128]{1,0:T(8,128)(2,1)S(1)} %shard_map.124.mine, bf16[4240,128]{1,0:T(8,128)(2,1)S(1)} %collective-permute-done.3.theirs, f32[640,256]{1,0:T(8,128)S(1)} %get-tuple-element.14.sums, ...), custom_call_target="tpu_custom_call" | custom-call | tf_op jit(solution)/shard_map/pallas_call | solution.py:372
  60.7 17.5 %all_to_all.11 = bf16[64,5,2,128]{3,2,1,0:T(2,128)(2,1)S(1)} all-to-all(bf16[64,5,2,128]{3,2,1,0:T(2,128)(2,1)S(1)} %bitcast.5), channel_id=1, replica_groups=mesh['z'=8,'x'=4,'yl'=2,'yh'=4,'c'=2] {'yh','z','yl'}, dimensions={0} | all-to-all | bytes 327680 | tf_op jit(solution)/shard_map/all_to_all | solution.py:452
  78.2 0.9 %shard_map.127 = (bf16[5,5120]{1,0:T(8,128)(2,1)}, bf16[5,5120]{1,0:T(8,128)(2,1)}) custom-call(bf16[640,128]{1,0:T(8,128)(2,1)S(1)} %bitcast.6), custom_call_target="tpu_custom_call" | custom-call | tf_op jit(solution)/shard_map/pallas_call | solution.py:408
Async XLA Ops:
  35.7 10.0 %collective-permute-start.2 = (bf16[640,128]{1,0:T(8,128)(2,1)S(1)}, bf16[640,128]{1,0:T(8,128)(2,1)S(1)}, u32[]{:S(2)}, u32[]{:S(2)}) collective-permute-start(bf16[640,128]{1,0:T(8,128)(2,1)S(1)} %get-tuple-element.11.refs_0_), channel_id=1, source_target_pairs={{48,0},{0,16},{16,32},{32,48},{49,1},{1,17},{17,33},{33,49},{50,2}... | collective-permute-start | bytes 491528 | tf_op jit(solution)/shard_map/ppermute | solution.py:444
  38.9 6.8 %collective-permute-start.1 = (bf16[640,128]{1,0:T(8,128)(2,1)S(1)}, bf16[640,128]{1,0:T(8,128)(2,1)S(1)}, u32[]{:S(2)}, u32[]{:S(2)}) collective-permute-start(bf16[640,128]{1,0:T(8,128)(2,1)S(1)} %get-tuple-element.11.refs_0_), channel_id=1, source_target_pairs={{16,0},{32,16},{48,32},{0,48},{17,1},{33,17},{49,33},{1,49},{18,2}... | collective-permute-start | bytes 491528 | tf_op jit(solution)/shard_map/ppermute | solution.py:444
  42.2 7.6 %collective-permute-start = (bf16[640,128]{1,0:T(8,128)(2,1)S(1)}, bf16[640,128]{1,0:T(8,128)(2,1)S(1)}, u32[]{:S(2)}, u32[]{:S(2)}) collective-permute-start(bf16[640,128]{1,0:T(8,128)(2,1)S(1)} %get-tuple-element.11.refs_0_), channel_id=1, source_target_pairs={{32,0},{48,16},{0,32},{16,48},{33,1},{49,17},{1,33},{17,49},{34,2}... | collective-permute-start | bytes 491528 | tf_op jit(solution)/shard_map/ppermute | solution.py:444
  49.9 8.4 %collective-permute-start.3 = (bf16[4240,128]{1,0:T(8,128)(2,1)S(1)}, bf16[4240,128]{1,0:T(8,128)(2,1)S(1)}, u32[]{:S(2)}, u32[]{:S(2)}) collective-permute-start(bf16[4240,128]{1,0:T(8,128)(2,1)S(1)} %shard_map.124.mine), channel_id=1, source_target_pairs={{0,1},{1,0},{2,3},{3,2},{4,5},{5,4},{6,7},{7,6},{8,9},{9,8},{10,11... | collective-permute-start | bytes 3256328 | tf_op jit(solution)/shard_map/ppermute | solution.py:448
